TPU v7x, 32 devices: a whole 2x2x4 slice. The times are simulated.
32 devices in a mesh: dp: 2 (over y), ctx: 16 (over z, x, core).
Axes of the slice: x: 2, y: 2, z: 4, core: 2. Of those that a mesh axis runs over, the one named last changes fastest.
Arguments:
- tokens: bfloat16 [4096, 2048], P(('dp', 'ctx')), may hold values from -6 to 6
- doc_starts: int32 [4096], P(('dp', 'ctx')), may hold values from 0 to 1, as said below
- routes: int32 [4096, 8], P(('dp', 'ctx')), may hold values from 0 to 15, all different within a row; in each aligned block of 128 rows (0 to 127, 128 to 255, ...) at most 96 rows name the same one
- norm_attn: float32 [2048], replicated, may hold values from 0.5 to 1.5
- norm_query: float32 [2048], replicated, may hold values from 0.5 to 1.5
- norm_key: float32 [2048], replicated, may hold values from 0.5 to 1.5
- norm_ffn: float32 [2048], replicated, may hold values from 0.5 to 1.5
- w_query: bfloat16 [2048, 2048], P('ctx'), may hold values from -0.125 to 0.125
- w_key: bfloat16 [2048, 2048], P('ctx'), may hold values from -0.125 to 0.125
- w_value: bfloat16 [2048, 2048], P('ctx'), may hold values from -0.125 to 0.125
- w_output: bfloat16 [2048, 2048], P('ctx'), may hold values from -1.5 to 1.5
- router: bfloat16 [2048, 16], replicated, may hold values from -0.0625 to 0.0625
- expert_gate: bfloat16 [16, 2048, 1024], P('ctx'), may hold values from -0.125 to 0.125
- expert_up: bfloat16 [16, 2048, 1024], P('ctx'), may hold values from -0.125 to 0.125
- expert_down: bfloat16 [16, 1024, 2048], P('ctx'), may hold values from -4 to 4
- out_grad: bfloat16 [4096, 2048], P(('dp', 'ctx')), may hold values from -6 to 6
Outputs:
- block_out: bfloat16 [4096, 2048], P(('dp', 'ctx'))
- tokens_grad: bfloat16 [4096, 2048], P(('dp', 'ctx'))
- norm_attn_grad: float32 [2048], replicated
- norm_query_grad: float32 [2048], replicated
- norm_key_grad: float32 [2048], replicated
- norm_ffn_grad: float32 [2048], replicated
- w_query_grad: float32 [2048, 2048], P(('dp', 'ctx'))
- w_key_grad: float32 [2048, 2048], P(('dp', 'ctx'))
- w_value_grad: float32 [2048, 2048], P(('dp', 'ctx'))
- w_output_grad: float32 [2048, 2048], P(('dp', 'ctx'))
- router_grad: float32 [2048, 16], replicated
- expert_gate_grad: float32 [16, 2048, 1024], P('ctx', None, 'dp')
- expert_up_grad: float32 [16, 2048, 1024], P('ctx', None, 'dp')
- expert_down_grad: float32 [16, 1024, 2048], P('ctx', 'dp')
Inputs may be any that keep to these rules, and one draw needn't show every extreme that they name: `doc_starts`: 1 where a document begins, else 0. Each group of 2048 tokens begins a document at its first token; other starts lie only among the first 128 and the last 127 tokens of the group. So one document of each group runs from its first device's tokens into its last device's. `routes`: A token names 8 different experts. In each aligned block of 128 rows (the rows of one device) no expert is named more than 96 times.
All inputs are finite; a program needn't handle non-finite values.
Results may differ from a plain program's by a relative error of at most 0.025.
Values may be sent and summed in bfloat16 or wider, within the bound.
No kernel may reach another device: no remote copies, remote signals or barrier semaphores. Data moves between devices by JAX's collectives and lax.ppermute only.
A program may use at most 384 MiB of HBM per device.

v0:
```python
import jax
import jax.numpy as jnp
from jax import lax
from jax.sharding import PartitionSpec as P

HEADS = 16


EPS = 1e-05
THETA = 10000.0
NEGATIVE = -1e30
HIGH = lax.Precision.HIGHEST


def spread(block, axis, holder):
    block = jnp.where(lax.axis_index(axis) == holder, block, jnp.zeros_like(block))
    return lax.psum(block, axis)


def shifted(shard, axis, by):
    devices = lax.axis_size(axis)
    return lax.ppermute(shard, axis, [(i, (i + by) % devices) for i in range(devices)])


def norm_rows(v, gain):
    return v * lax.rsqrt(jnp.mean(v * v, axis=-1, keepdims=True) + EPS) * gain


def rotate(v, place):
    half = v.shape[-1] // 2
    freq = THETA ** (-jnp.arange(half, dtype=jnp.float32) * 2.0 / v.shape[-1])
    angle = place.astype(jnp.float32)[:, None] * freq[None, :]
    cosine = jnp.cos(angle)[:, None, :]
    sine = jnp.sin(angle)[:, None, :]
    first = v[..., :half]
    second = v[..., half:]
    return jnp.concatenate(
        [first * cosine - second * sine, second * cosine + first * sine], axis=-1
    )


def qk_post(proj, gain, place, heads):
    count, width = proj.shape
    normed = norm_rows(proj, gain).reshape(count, heads, width // heads)
    return rotate(normed, place).reshape(count, width)


def needed(q_place, q_seg, k_place, k_seg):
    return (k_place[0] <= q_place[-1]) & (k_seg[-1] >= q_seg[0])


def pair_mask(q_place, q_seg, k_place, k_seg):
    return (k_place[None, :] <= q_place[:, None]) & (k_seg[None, :] == q_seg[:, None])


def pair_grads(qh, gh, lse, delta, q_place, q_seg, kh, vh, k_place, k_seg, scale, wanted):

    def pair_compute(unused):
        score = jnp.einsum("qhd,khd->hqk", qh, kh, preferred_element_type=jnp.float32) * scale
        mask = pair_mask(q_place, q_seg, k_place, k_seg)
        prob = jnp.where(mask[None], jnp.exp(score - lse[:, :, None]), 0.0)
        dprob = jnp.einsum("qhd,khd->hqk", gh, vh, preferred_element_type=jnp.float32)
        dscore = (prob * (dprob - delta[:, :, None])).astype(jnp.bfloat16)
        prob_low = prob.astype(jnp.bfloat16)
        dq = jnp.einsum("hqk,khd->qhd", dscore, kh, preferred_element_type=jnp.float32) * scale
        dk = jnp.einsum("hqk,qhd->khd", dscore, qh, preferred_element_type=jnp.float32) * scale
        dv = jnp.einsum("hqk,qhd->khd", prob_low, gh, preferred_element_type=jnp.float32)
        return (dq, dk, dv)

    def skip(unused):
        return (
            jnp.zeros(qh.shape, jnp.float32),
            jnp.zeros(kh.shape, jnp.float32),
            jnp.zeros(vh.shape, jnp.float32),
        )

    return lax.cond(wanted, pair_compute, skip, 0)


def local(
    tokens,
    doc_starts,
    routes,
    norm_attn,
    norm_query,
    norm_key,
    norm_ffn,
    w_query,
    w_key,
    w_value,
    w_output,
    router,
    expert_gate,
    expert_up,
    expert_down,
    out_grad,
):
    f32 = jnp.float32
    b16 = jnp.bfloat16
    n_ctx = lax.axis_size("ctx")
    rank = lax.axis_index("ctx")
    rows, width = tokens.shape
    heads = HEADS
    head_dim = width // heads
    scale = head_dim ** (-0.5)
    experts = router.shape[1]
    topk = routes.shape[1]
    owned = expert_gate.shape[0]
    cap = max(2, rows * topk * 3 // (2 * experts))
    starts = jnp.sum(doc_starts)
    first_count = spread(starts, "ctx", 0)
    before = jnp.where(rank > 0, first_count, 0)
    seg = before + jnp.cumsum(doc_starts)
    place = rank * rows + jnp.arange(rows, dtype=jnp.int32)
    wq, wk, wv, wo = (
        lax.all_gather(w_query, "ctx", axis=0, tiled=True),
        lax.all_gather(w_key, "ctx", axis=0, tiled=True),
        lax.all_gather(w_value, "ctx", axis=0, tiled=True),
        lax.all_gather(w_output, "ctx", axis=0, tiled=True),
    )
    inputs = tokens.astype(f32)
    n1 = norm_rows(inputs, norm_attn).astype(b16)
    qp = jnp.dot(n1, wq, preferred_element_type=f32)
    kp = jnp.dot(n1, wk, preferred_element_type=f32)
    vp = jnp.dot(n1, wv, preferred_element_type=f32)
    query = qk_post(qp, norm_query, place, heads).astype(b16)
    keys = qk_post(kp, norm_key, place, heads).astype(b16)
    values = vp.astype(b16)
    qh = query.reshape(rows, heads, head_dim)
    start_state = (
        jnp.full((heads, rows), NEGATIVE, f32),
        jnp.zeros((heads, rows), f32),
        jnp.zeros((rows, heads, head_dim), f32),
    )
    k_piece = lax.all_gather(keys, "ctx", axis=0, tiled=True)
    v_piece = lax.all_gather(values, "ctx", axis=0, tiled=True)
    s_piece = lax.all_gather(seg, "ctx", axis=0, tiled=True)
    total_rows = k_piece.shape[0]
    block = min(rows, total_rows)
    count = total_rows // block

    def step(index, state):
        best, total, acc = state
        offset = index * block
        kh = lax.dynamic_slice_in_dim(k_piece, offset, block, 0).reshape(block, heads, head_dim)
        vh = lax.dynamic_slice_in_dim(v_piece, offset, block, 0).reshape(block, heads, head_dim)
        k_seg = lax.dynamic_slice_in_dim(s_piece, offset, block, 0)
        k_place = offset + jnp.arange(block, dtype=jnp.int32)

        def step_compute(unused):
            score = jnp.einsum("qhd,khd->hqk", qh, kh, preferred_element_type=f32) * scale
            mask = pair_mask(place, seg, k_place, k_seg)
            score = jnp.where(mask[None], score, NEGATIVE)
            new_best = jnp.maximum(best, jnp.max(score, axis=-1))
            shrink = jnp.exp(best - new_best)
            prob = jnp.exp(score - new_best[:, :, None])
            new_total = total * shrink + jnp.sum(prob, axis=-1)
            new_acc = acc * shrink.T[:, :, None] + jnp.einsum(
                "hqk,khd->qhd", prob.astype(b16), vh, preferred_element_type=f32
            )
            return (new_best, new_total, new_acc)

        return lax.cond(needed(place, seg, k_place, k_seg), step_compute, lambda unused: state, 0)

    best, total, acc = lax.fori_loop(0, count, step, start_state)
    attn_heads = acc / total.T[:, :, None]
    lse = best + jnp.log(total)
    attn = attn_heads.reshape(rows, width)
    attn_low = attn.astype(b16)
    h1 = inputs + jnp.dot(attn_low, wo, preferred_element_type=f32)
    n2 = norm_rows(h1, norm_ffn).astype(b16)
    probs = jax.nn.softmax(jnp.dot(n2, router, preferred_element_type=f32), axis=-1)
    choice_mask = routes[:, :, None] == jnp.arange(experts, dtype=jnp.int32)[None, None, :]
    gates = jnp.sum(jnp.where(choice_mask, probs[:, None, :], 0.0), axis=-1)
    flat = routes.reshape(-1)
    hits = (flat[:, None] == jnp.arange(experts, dtype=jnp.int32)[None, :]).astype(jnp.int32)
    slot = jnp.sum(jnp.cumsum(hits, axis=0) * hits, axis=1) - 1
    dest = flat * cap + slot
    route_ids = jnp.arange(rows * topk, dtype=jnp.int32)
    source = jnp.zeros((experts * cap,), jnp.int32).at[dest].set(route_ids)
    filled = jnp.zeros((experts * cap,), jnp.bool_).at[dest].set(True)
    send = jnp.where(filled[:, None], n2[source // topk], jnp.zeros((), b16)).reshape(
        experts, cap, width
    )
    received = lax.all_to_all(send, "ctx", split_axis=0, concat_axis=0, tiled=True)
    count = received.shape[1]
    grid = received.reshape(n_ctx, owned, count, width)
    gate_pre = jnp.einsum("secd,edh->sech", grid, expert_gate, preferred_element_type=f32)
    up_pre = jnp.einsum("secd,edh->sech", grid, expert_up, preferred_element_type=f32)
    act = (jax.nn.silu(gate_pre) * up_pre).astype(b16)
    result = jnp.einsum("sech,ehd->secd", act, expert_down, preferred_element_type=f32).astype(b16)
    returned = lax.all_to_all(
        result.reshape(n_ctx * owned, count, width), "ctx", split_axis=0, concat_axis=0, tiled=True
    )
    hidden = gate_pre.shape[-1]
    returned, kept_in, kept_gate, kept_up = (
        returned,
        received,
        gate_pre.reshape(n_ctx * owned, count, hidden),
        up_pre.reshape(n_ctx * owned, count, hidden),
    )
    picked = returned.reshape(experts * cap, width)[dest].reshape(rows, topk, width).astype(f32)
    moe = jnp.einsum("tk,tkd->td", gates, picked, precision=HIGH)
    block_out = (h1 + moe).astype(b16)
    grad_top = out_grad.astype(f32)
    gate_grad = jnp.einsum("td,tkd->tk", grad_top, picked, precision=HIGH)
    down_in = (gates[:, :, None] * grad_top[:, None, :]).astype(b16).reshape(rows * topk, width)
    back_send = jnp.where(filled[:, None], down_in[source], jnp.zeros((), b16)).reshape(
        experts, cap, width
    )
    back_recv = lax.all_to_all(back_send, "ctx", split_axis=0, concat_axis=0, tiled=True)
    hidden = kept_gate.shape[-1]
    grid_dy = back_recv.reshape(n_ctx, owned, cap, width)
    grid_x = kept_in.reshape(n_ctx, owned, cap, width)
    gate_pre = kept_gate.reshape(n_ctx, owned, cap, hidden)
    up_pre = kept_up.reshape(n_ctx, owned, cap, hidden)
    sigma = jax.nn.sigmoid(gate_pre)
    silu = jax.nn.silu(gate_pre)
    act = (silu * up_pre).astype(b16)
    dact = jnp.einsum("secd,ehd->sech", grid_dy, expert_down, preferred_element_type=f32)
    dgate_pre = (dact * up_pre * sigma * (1.0 + gate_pre * (1.0 - sigma))).astype(b16)
    dup_pre = (dact * silu).astype(b16)
    down_term = jnp.einsum("sech,secd->ehd", act, grid_dy, preferred_element_type=f32)
    gate_term = jnp.einsum("secd,sech->edh", grid_x, dgate_pre, preferred_element_type=f32)
    up_term = jnp.einsum("secd,sech->edh", grid_x, dup_pre, preferred_element_type=f32)
    entry_grad = (
        jnp.einsum("sech,edh->secd", dgate_pre, expert_gate, preferred_element_type=f32)
        + jnp.einsum("sech,edh->secd", dup_pre, expert_up, preferred_element_type=f32)
    ).astype(b16)
    entry_back = lax.all_to_all(
        entry_grad.reshape(n_ctx * owned, cap, width),
        "ctx",
        split_axis=0,
        concat_axis=0,
        tiled=True,
    )
    route_grad = jnp.sum(
        entry_back.reshape(experts * cap, width)[dest].reshape(rows, topk, width).astype(f32),
        axis=1,
    )
    gate_grad_out, up_grad_out, down_grad_out = (
        lax.psum_scatter(
            gate_term.astype(jnp.bfloat16), "dp", scatter_dimension=2, tiled=True
        ).astype(jnp.float32),
        lax.psum_scatter(
            up_term.astype(jnp.bfloat16), "dp", scatter_dimension=2, tiled=True
        ).astype(jnp.float32),
        lax.psum_scatter(
            down_term.astype(jnp.bfloat16), "dp", scatter_dimension=1, tiled=True
        ).astype(jnp.float32),
    )
    prob_grad = jnp.sum(jnp.where(choice_mask, gate_grad[:, :, None], 0.0), axis=1)
    logit_grad = probs * (prob_grad - jnp.sum(probs * prob_grad, axis=-1, keepdims=True))
    router_term = jnp.dot(n2.astype(f32).T, logit_grad, precision=HIGH)
    n2_grad = route_grad + jnp.dot(logit_grad, router.astype(f32).T, precision=HIGH)
    unused_value, ffn_back = jax.vjp(norm_rows, h1, norm_ffn)
    h1_part, ffn_gain_grad = ffn_back(n2_grad)
    h1_grad = grad_top + h1_part
    h1_low = h1_grad.astype(b16)
    attn_grad = jnp.dot(h1_low, wo.T, preferred_element_type=f32).astype(b16)
    gh = attn_grad.reshape(rows, heads, head_dim)
    delta = jnp.einsum("qhd,qhd->hq", gh.astype(f32), attn_heads, precision=HIGH)
    local_index = jnp.arange(rows, dtype=jnp.int32)

    def key_step(index, state):
        moving, query_grad = state
        k_move, v_move, s_move, key_acc, value_acc = moving
        anchor = (rank - index + n_ctx) % n_ctx
        k_place = anchor * rows + local_index
        dq, dk, dv = pair_grads(
            qh,
            gh,
            lse,
            delta,
            place,
            seg,
            k_move.astype(b16).reshape(rows, heads, head_dim),
            v_move.astype(b16).reshape(rows, heads, head_dim),
            k_place,
            s_move,
            scale,
            needed(place, seg, k_place, s_move),
        )
        moving = (
            shifted(k_move.astype(jnp.bfloat16), "ctx", 1).astype(k_move.dtype),
            shifted(v_move.astype(jnp.bfloat16), "ctx", 1).astype(v_move.dtype),
            shifted(s_move, "ctx", 1),
            shifted((key_acc + dk.reshape(rows, width)).astype(jnp.bfloat16), "ctx", 1).astype(
                jnp.float32
            ),
            shifted((value_acc + dv.reshape(rows, width)).astype(jnp.bfloat16), "ctx", 1).astype(
                jnp.float32
            ),
        )
        return (moving, query_grad + dq)

    start_keys = (
        (
            keys.astype(f32),
            values.astype(f32),
            seg,
            jnp.zeros((rows, width), f32),
            jnp.zeros((rows, width), f32),
        ),
        jnp.zeros((rows, heads, head_dim), f32),
    )
    (unused_k, unused_v, unused_s, key_grad, value_grad), query_grad = lax.fori_loop(
        0, n_ctx, key_step, start_keys
    )
    query_grad = query_grad.reshape(rows, width)
    unused_query, query_back = jax.vjp(
        lambda proj, gain: qk_post(proj, gain, place, heads), qp, norm_query
    )
    qp_grad, query_gain_grad = query_back(query_grad)
    unused_key, key_back = jax.vjp(
        lambda proj, gain: qk_post(proj, gain, place, heads), kp, norm_key
    )
    kp_grad, key_gain_grad = key_back(key_grad)
    qp_low = qp_grad.astype(b16)
    kp_low = kp_grad.astype(b16)
    vp_low = value_grad.astype(b16)
    n1_grad = (
        jnp.dot(qp_low, wq.T, preferred_element_type=f32)
        + jnp.dot(kp_low, wk.T, preferred_element_type=f32)
        + jnp.dot(vp_low, wv.T, preferred_element_type=f32)
    )
    unused_norm, attn_back = jax.vjp(norm_rows, inputs, norm_attn)
    input_part, attn_gain_grad = attn_back(n1_grad)
    tokens_grad = (h1_grad + input_part).astype(b16)
    contract = (((0,), (0,)), ((), ()))
    stacked = lax.psum_scatter(
        jnp.concatenate(
            [
                lax.dot_general(n1, qp_low, contract, preferred_element_type=f32),
                lax.dot_general(n1, kp_low, contract, preferred_element_type=f32),
                lax.dot_general(n1, vp_low, contract, preferred_element_type=f32),
                lax.dot_general(attn_low, h1_low, contract, preferred_element_type=f32),
            ],
            axis=1,
        ),
        ("dp", "ctx"),
        scatter_dimension=0,
        tiled=True,
    )
    wq_grad = stacked[:, :width]
    wk_grad = stacked[:, width : 2 * width]
    wv_grad = stacked[:, 2 * width : 3 * width]
    wo_grad = stacked[:, 3 * width :]
    attn_gain_sum, query_gain_sum, key_gain_sum, ffn_gain_sum, router_sum = lax.psum(
        (attn_gain_grad, query_gain_grad, key_gain_grad, ffn_gain_grad, router_term), ("dp", "ctx")
    )
    return (
        block_out,
        tokens_grad,
        attn_gain_sum,
        query_gain_sum,
        key_gain_sum,
        ffn_gain_sum,
        wq_grad,
        wk_grad,
        wv_grad,
        wo_grad,
        router_sum,
        gate_grad_out,
        up_grad_out,
        down_grad_out,
    )


def solution(mesh):
    return jax.shard_map(
        local,
        mesh=mesh,
        in_specs=(
            P(("dp", "ctx"), None),
            P(("dp", "ctx")),
            P(("dp", "ctx"), None),
            P(),
            P(),
            P(),
            P(),
            P("ctx", None),
            P("ctx", None),
            P("ctx", None),
            P("ctx", None),
            P(),
            P("ctx", None, None),
            P("ctx", None, None),
            P("ctx", None, None),
            P(("dp", "ctx"), None),
        ),
        out_specs=(
            P(("dp", "ctx"), None),
            P(("dp", "ctx"), None),
            P(),
            P(),
            P(),
            P(),
            P(("dp", "ctx"), None),
            P(("dp", "ctx"), None),
            P(("dp", "ctx"), None),
            P(("dp", "ctx"), None),
            P(),
            P("ctx", None, "dp"),
            P("ctx", None, "dp"),
            P("ctx", "dp", None),
        ),
        check_vma=False,
    )
```

profile of v0, /device:TPU:9, one launch (start us, length us, event | category | flops | bytes accessed | tf_op | source)
XLA Modules:
  0.0 2911.6 jit_solution(2734856189273131149)
XLA Ops:
  11.2 74.9 %all-gather.14.cloned.1.call-done = bf16[2048,2048]{1,0:T(8,128)(2,1)} async-done(((bf16[128,2048]{1,0:T(8,128)(2,1)}), bf16[2048,2048]{1,0:T(8,128)(2,1)}) %all-gather.14.cloned.1.call-update) | async-done | bytes 8388624 | tf_op jit(solution)/shard_map/all_gather | solution.py:118
  92.1 69.3 %all-gather.12.cloned.1.call-done = bf16[2048,2048]{1,0:T(8,128)(2,1)} async-done(((bf16[128,2048]{1,0:T(8,128)(2,1)}), bf16[2048,2048]{1,0:T(8,128)(2,1)}) %all-gather.12.cloned.1.call-update) | async-done | bytes 8388624 | tf_op jit(solution)/shard_map/all_gather | solution.py:116
  167.7 69.1 %all-gather.8.cloned.1.call-done = bf16[2048,2048]{1,0:T(8,128)(2,1)} async-done(((bf16[128,2048]{1,0:T(8,128)(2,1)}), bf16[2048,2048]{1,0:T(8,128)(2,1)}) %all-gather.8.cloned.1.call-update) | async-done | bytes 8388624 | tf_op jit(solution)/shard_map/all_gather | solution.py:117
  272.5 28.6 all-gather
  301.8 20.2 all-gather.16.cloned.1.call-done
  334.4 65.3 %all-gather.10.cloned.1.call-done = bf16[2048,2048]{0,1:T(8,128)(2,1)} async-done(((bf16[128,2048]{0,1:T(8,128)(2,1)}), bf16[2048,2048]{0,1:T(8,128)(2,1)}) %all-gather.10.cloned.1.call-update) | async-done | bytes 8388624 | tf_op jit(solution)/shard_map/all_gather | solution.py:135
  399.8 59.8 %while.43 = (s32[]{:T(128)}, f32[16,128]{1,0:T(8,128)S(1)}, f32[16,128]{1,0:T(8,128)S(1)}, f32[128,16,128]{2,0,1:T(8,128)S(1)}, s32[128]{0:T(128)S(1)}, /*index=...) while((s32[]{:T(128)}, f32[16,128]{1,0:T(8,128)S(1)}, ...), condition=%wide.region_11.12_spmd, body=%wide.region_6.11_spmd.sunk | while | flops 136632464 | bytes 9080697 | solution.py:165
  461.9 14.2 all-gather.18.cloned.1.call-done
  492.4 158.5 %all_to_all.20 = bf16[16,96,2048]{2,1,0:T(8,128)(2,1)S(1)} all-to-all(bf16[16,96,2048]{2,1,0:T(8,128)(2,1)S(1)} %broadcast_select_fusion.1), channel_id=1, replica_groups=mesh['dp'=2,'ctx'=16] {'ctx'}, dimensions={0} | all-to-all | bytes 12582912 | tf_op jit(solution)/shard_map/all_to_all | solution.py:185
  691.1 134.7 %all-to-all-done.1 = bf16[16,96,2048]{2,1,0:T(8,128)(2,1)} async-done(((bf16[16,96,2048]{2,1,0:T(8,128)(2,1)}), bf16[16,96,2048]{2,1,0:T(8,128)(2,1)}, u32[]{:S(2)}, u32[]{:S(2)}) %all-to-all-start.1) | async-done | bytes 6291488 | tf_op jit(solution)/shard_map/all_to_all | solution.py:192
  845.9 15.4 gather_fusion.2
  864.7 145.1 %all_to_all.21 = bf16[16,96,2048]{2,1,0:T(8,128)(2,1)S(1)} all-to-all(bf16[16,96,2048]{2,1,0:T(8,128)(2,1)S(1)} %broadcast_select_fusion), channel_id=1, replica_groups=mesh['dp'=2,'ctx'=16] {'ctx'}, dimensions={0} | all-to-all | bytes 12582912 | tf_op jit(solution)/shard_map/all_to_all | solution.py:211
  1021.1 14.9 fusion.55
  1036.1 12.7 fusion.47
  1095.6 105.3 %all-to-all-done.3 = bf16[16,96,2048]{2,1,0:T(8,128)(2,1)} async-done(((bf16[16,96,2048]{2,1,0:T(8,128)(2,1)}), bf16[16,96,2048]{2,1,0:T(8,128)(2,1)}, u32[]{:S(2)}, u32[]{:S(2)}) %all-to-all-start.3) | async-done | bytes 6291488 | tf_op jit(solution)/shard_map/all_to_all | solution.py:230
  1230.4 665.2 %while.44 = (s32[]{:T(128)}, bf16[128,2048]{1,0:T(8,128)(2,1)}, bf16[128,2048]{1,0:T(8,128)(2,1)}, s32[128]{0:T(128)S(1)}, f32[128,2048]{0,1:T(8,128)}, /*index=...) while((s32[]{:T(128)}, bf16[128,2048]{1,0:T(8,128)(2,1)}, ...), condition=%wide.region_28.29_spmd.clone, body=%wide.region_25.28_spmd.clone.sunk | while | flops 340574368 | bytes 37804224 | solution.py:307
  1550.1 14.2 collective-permute-start.3
  1599.8 12.7 collective-permute-start
  1792.7 12.7 collective-permute-start.3
  1939.8 39.9 %pad_maximum_fusion = f32[2048,8192]{0,1:T(8,128)} fusion(f32[2048,2048]{0,1:T(8,128)} %fusion.76, f32[2048,2048]{0,1:T(8,128)S(1)} %fusion.73, f32[2048,2048]{0,1:T(8,128)} %fusion.97, f32[2048,2048]{0,1:T(8,128)} %fusion.99), kind=kLoop, calls=%fused_computation.49 | loop fusion | flops 50331648 | bytes 134217728 | tf_op jit(solution)/shard_map/concatenate | solution.py:332
  1979.8 61.2 %copy.177 = f32[2048,8192]{1,0:T(8,128)} copy(f32[2048,8192]{0,1:T(8,128)} %pad_maximum_fusion) | data formatting | bytes 134217728
  2072.8 74.6 %all-reduce.4 = (f32[2048]{0:T(1024)}, f32[2048]{0:T(1024)}, f32[2048]{0:T(1024)}, f32[2048]{0:T(1024)}) all-reduce(f32[2048]{0:T(1024)S(1)} %get-tuple-element.891, f32[2048]{0:T(1024)S(1)} %get-tuple-element.889, f32[2048]{0:T(1024)S(1)} %get-tuple-element.887, f32[2048]{0:T(1024)S(1)} %copy-done.61), channel_id=1, replica_groups=mesh['dp'=2,'ctx'=16] {'dp','ctx'}, use_global_device_ids=true, to_apply=%region_33.34 | all-reduce | flops 8192 | bytes 65536 | tf_op jit(solution)/shard_map/psum | solution.py:349
  2147.3 628.4 %reduce-scatter.13.cloned.1.call-done = f32[64,8192]{1,0:T(8,128)} async-done(((f32[2048,8192]{1,0:T(8,128)}), f32[64,8192]{1,0:T(8,128)}) %reduce-scatter.13.cloned.1.call-update) | async-done | bytes 2097168
  2778.6 124.7 %all-reduce.7.cloned.1.call-done = f32[2048,16]{0,1:T(8,128)} async-done(((f32[2048,16]{0,1:T(8,128)}), f32[2048,16]{0,1:T(8,128)}) %all-reduce.7.cloned.1.call-update) | async-done | bytes 131088 | tf_op jit(solution)/shard_map/psum | solution.py:349
  (889 shorter events, 1030.6 us)
Async XLA Ops:
  7.2 78.9 %all-gather.14.cloned.1.call-start = ((), (), s32[]{:S(2)}) async-start(), calls=%async_computation.11 | async-start | bytes 8912896 | tf_op jit(solution)/shard_map/all_gather | solution.py:118
  7.9 153.5 %all-gather.12.cloned.1.call-start = ((), (), s32[]{:S(2)}) async-start(), calls=%async_computation.10 | async-start | bytes 8912896 | tf_op jit(solution)/shard_map/all_gather | solution.py:116
  8.7 228.1 %all-gather.8.cloned.1.call-start = ((), (), s32[]{:S(2)}) async-start(), calls=%async_computation.8 | async-start | bytes 8912896 | tf_op jit(solution)/shard_map/all_gather | solution.py:117
  9.4 312.6 %all-gather.16.cloned.1.call-start = ((), (), s32[]{:S(2)}) async-start(), calls=%async_computation.12 | async-start | bytes 8912896 | tf_op jit(solution)/shard_map/all_gather | solution.py:136
  91.8 307.9 %all-gather.10.cloned.1.call-start = ((), (), s32[]{:S(2)}) async-start(), calls=%async_computation.9 | async-start | bytes 8912896 | tf_op jit(solution)/shard_map/all_gather | solution.py:135
  246.5 229.7 %all-gather.18.cloned.1.call-start = ((), (), s32[]{:S(2)}) async-start(), calls=%async_computation.13 | async-start | bytes 8912896 | tf_op jit(solution)/shard_map/all_gather | solution.py:119
  685.5 140.3 %all-to-all-start.1 = ((bf16[16,96,2048]{2,1,0:T(8,128)(2,1)}), bf16[16,96,2048]{2,1,0:T(8,128)(2,1)}, u32[]{:S(2)}, u32[]{:S(2)}) async-start(bf16[16,96,2048]{2,1,0:T(8,128)(2,1)} %convolution_convert_fusion), calls=%async_computation.1 | async-start | bytes 12582912 | tf_op jit(solution)/shard_map/all_to_all | solution.py:192
  690.6 1352.4 %reduce-scatter.11.cloned.1.call-start = ((), (), s32[]{:S(2)}) async-start(), calls=%async_computation.17 | async-start | bytes 6291456 | tf_op jit(solution)/shard_map/reduce_scatter | solution.py:248
  1060.7 140.3 %all-to-all-start.3 = ((bf16[16,96,2048]{2,1,0:T(8,128)(2,1)}), bf16[16,96,2048]{2,1,0:T(8,128)(2,1)}, u32[]{:S(2)}, u32[]{:S(2)}) async-start(bf16[16,96,2048]{2,1,0:T(8,128)(2,1)} %add_convert_fusion), calls=%async_computation.3 | async-start | bytes 12582912 | tf_op jit(solution)/shard_map/all_to_all | solution.py:230
  1065.7 981.4 %reduce-scatter.9.cloned.1.call-start = ((), (), s32[]{:S(2)}) async-start(), calls=%async_computation.16 | async-start | bytes 6291456 | tf_op jit(solution)/shard_map/reduce_scatter | solution.py:245
  1077.0 974.4 %reduce-scatter.7.cloned.1.call-start = ((), (), s32[]{:S(2)}) async-start(), calls=%async_computation.15 | async-start | bytes 6291456 | tf_op jit(solution)/shard_map/reduce_scatter | solution.py:242
  1095.6 1680.2 %reduce-scatter.13.cloned.1.call-start = ((), (), s32[]{:S(2)}) async-start(), calls=%async_computation.18 | async-start | bytes 69206016
  1251.6 22.8 collective-permute-start
  1502.4 23.0 collective-permute-start.4
  1546.3 23.9 collective-permute-start.4
  1590.5 24.3 collective-permute-start.4
  1599.8 24.7 collective-permute-start
  1670.7 24.2 collective-permute-start.4
  1706.2 24.2 collective-permute-start.4
  1743.2 31.9 %collective-permute-start.4 = (bf16[128,2048]{0,1:T(8,128)(2,1)}, bf16[128,2048]{0,1:T(8,128)(2,1)S(1)}, u32[]{:S(2)}, u32[]{:S(2)}) collective-permute-start(bf16[128,2048]{0,1:T(8,128)(2,1)} %fusion.157), channel_id=1, source_target_pairs={{0,1},{1,2},{2,3},{3,4},{4,5},{5,6},{6,7},{7,8},{8,9},{9,10},{10,1... | collective-permute-start | bytes 1572872 | tf_op jit(solution)/shard_map/while/body/eval_jaxpr/ppermute | solution.py:22
  1788.0 29.9 %collective-permute-start.4 = (bf16[128,2048]{0,1:T(8,128)(2,1)}, bf16[128,2048]{0,1:T(8,128)(2,1)S(1)}, u32[]{:S(2)}, u32[]{:S(2)}) collective-permute-start(bf16[128,2048]{0,1:T(8,128)(2,1)} %fusion.157), channel_id=1, source_target_pairs={{0,1},{1,2},{2,3},{3,4},{4,5},{5,6},{6,7},{7,8},{8,9},{9,10},{10,1... | collective-permute-start | bytes 1572872 | tf_op jit(solution)/shard_map/while/body/eval_jaxpr/ppermute | solution.py:22
  1792.7 26.2 collective-permute-start.3
  1831.7 23.6 collective-permute-start.4
  2041.0 862.3 %all-reduce.7.cloned.1.call-start = ((), (), s32[]{:S(2)}) async-start(), calls=%async_computation.14 | async-start | bytes 262144 | tf_op jit(solution)/shard_map/psum | solution.py:349
  (161 other events, 7213.6 us)
Sparse Core Ops, SparseCore 0:
  10.2 75.8 all-gather.13
  88.3 73.1 all-gather.11
  163.6 73.1 all-gather.7
  238.8 83.1 all-gather.15
  324.6 75.0 all-gather.9
  401.7 74.3 all-gather.17
  1021.2 53.4 reduce-scatter.10
  1077.6 54.3 reduce-scatter.8
  1134.9 54.2 reduce-scatter.6
  2041.1 734.6 reduce-scatter.12
  2782.8 120.4 all-reduce.6
where the time goes:
time: 2930 us; the launch traced here: 2910 us
  waiting for transfers between devices  1440 us (49%)
  blocking collectives  415 us (14%)
  local copies, waits for them, and re-layouts  277 us (9%)
  starting transfers between devices  262 us (9%)
  matrix products  231 us (8%)
  other arithmetic  226 us (8%)
  loops' own time  45.1 us (2%)
    unnamed x12, waiting for transfers between devices  631 us
    ppermute x80, starting transfers between devices, shifted(): lax.ppermute(shard, axis, [(i, (i + by) % devices) for i in range(devices)])  251 us
    all_to_all x1, blocking collectives, local(): lax.all_to_all(send, 'ctx', split_axis=0, concat_axis=0, tiled=True)  158 us
    all_to_all x1, blocking collectives, local(): lax.all_to_all(back_send, 'ctx', split_axis=0, concat_axis=0, tiled=True)  145 us
    all_to_all x1, waiting for transfers between devices, local(): lax.all_to_all(result.reshape(n_ctx * owned, count, width), 'ctx', split_...  135 us
    ppermute x80, waiting for transfers between devices, shifted(): lax.ppermute(shard, axis, [(i, (i + by) % devices) for i in range(devices)])  129 us
    psum x1, waiting for transfers between devices, local(): lax.psum((attn_gain_grad, query_gain_grad, key_gain_grad, ffn_gain_grad,...  125 us
    all_to_all x1, waiting for transfers between devices, local(): lax.all_to_all(entry_grad.reshape(n_ctx * owned, cap, width), 'ctx', spli...  105 us
  transfers between devices with their start and end apart: 93, of which 33 were waited for; matrix products, arithmetic and copies ran while one was open for 22% of the time, Pallas kernels for 0%

commit v1 on v0

--- a/solution.py
+++ b/solution.py
@@ -1,6 +1,10 @@
+import functools
+
 import jax
 import jax.numpy as jnp
 from jax import lax
+from jax.experimental import pallas as pl
+from jax.experimental.pallas import tpu as pltpu
 from jax.sharding import PartitionSpec as P
 
 HEADS = 16
@@ -77,7 +81,7 @@
     return lax.cond(wanted, pair_compute, skip, 0)
 
 
-def local(
+def local_general(
     tokens,
     doc_starts,
     routes,
@@ -367,6 +371,554 @@
     )
 
 
+B16 = jnp.bfloat16
+F32 = jnp.float32
+LANES = 128
+NT = (((1,), (1,)), ((), ()))
+TN = (((0,), (0,)), ((), ()))
+
+
+def dot(a, b, dims=(((1,), (0,)), ((), ()))):
+    return lax.dot_general(a, b, dims, preferred_element_type=F32)
+
+
+def ring_of(chips):
+    return [2 * p if p < chips // 2 else 2 * (chips - 1 - p) + 1 for p in range(chips)]
+
+
+def attention_forward(q_ref, k_ref, v_ref, seg_row_ref, seg_col_ref, out_ref, lse_ref, *, block, scale):
+    total = q_ref.shape[0]
+    vt = v_ref[...].astype(F32).T.astype(B16)
+    for index in range(total // block):
+        low, high = index * block, (index + 1) * block
+        score = dot(k_ref[:high], q_ref[low:high], NT) * scale
+        key = lax.broadcasted_iota(jnp.int32, (high, block), 0)
+        query = low + lax.broadcasted_iota(jnp.int32, (high, block), 1)
+        seen = (key <= query) & (seg_col_ref[:high] == seg_row_ref[:, low:high])
+        score = jnp.where(seen, score, NEGATIVE)
+        best = jnp.max(score, axis=0, keepdims=True)
+        prob = jnp.exp(score - best)
+        norm = jnp.sum(prob, axis=0, keepdims=True)
+        out = dot(vt[:, :high], prob.astype(B16)) / norm
+        out_ref[low:high] = out.T
+        lse_ref[:, low:high] = best + jnp.log(norm)
+
+
+def attention_backward(
+    q_ref, k_ref, v_ref, g_ref, out_ref, lse_ref, seg_row_ref, seg_col_ref, dq_ref, dk_ref, dv_ref, *, block, scale
+):
+    total = q_ref.shape[0]
+    kt = k_ref[...].astype(F32).T.astype(B16)
+    dk_ref[...] = jnp.zeros_like(dk_ref)
+    dv_ref[...] = jnp.zeros_like(dv_ref)
+    for index in range(total // block):
+        low, high = index * block, (index + 1) * block
+        q, g = q_ref[low:high], g_ref[low:high]
+        delta = jnp.sum((g.astype(F32) * out_ref[low:high]).T, axis=0, keepdims=True)
+        score = dot(k_ref[:high], q, NT) * scale
+        key = lax.broadcasted_iota(jnp.int32, (high, block), 0)
+        query = low + lax.broadcasted_iota(jnp.int32, (high, block), 1)
+        seen = (key <= query) & (seg_col_ref[:high] == seg_row_ref[:, low:high])
+        prob = jnp.where(seen, jnp.exp(score - lse_ref[:, low:high]), 0.0)
+        dprob = dot(v_ref[:high], g, NT)
+        dscore = (prob * (dprob - delta)).astype(B16)
+        dk_ref[:high] += dot(dscore, q) * scale
+        dv_ref[:high] += dot(prob.astype(B16), g)
+        dq_ref[low:high] = dot(kt[:, :high], dscore).T * scale
+
+
+def expert_kernel(ids_ref, *refs, shards, fresh):
+    x_refs, refs = refs[:shards], refs[shards:]
+    g_refs, refs = refs[:shards], refs[shards:]
+    wg_ref, wu_ref, wd_ref = refs[:3]
+    refs = refs[3 if fresh else 8 :]
+    moe_ref, dx_ref, dgate_ref, ag_ref, dg_ref, du_ref, xs_ref, gs_ref, moe_acc, dx_acc = refs
+    expert, step, steps = pl.program_id(0), pl.program_id(1), pl.num_programs(1)
+    rows, width = g_refs[0].shape
+    first = (expert == 0) & (step == 0)
+
+    @pl.when(first)
+    def _():
+        for i in range(shards):
+            xs_ref[i] = x_refs[i][:, :width]
+            gs_ref[i] = g_refs[i][...]
+        dgate_ref[...] = jnp.zeros_like(dgate_ref)
+
+    x = xs_ref[...].reshape(shards * rows, width)
+    g = gs_ref[...].reshape(shards * rows, width)
+    lane = lax.broadcasted_iota(jnp.int32, (rows, LANES), 1)
+    mine = (lane < 3 * ids_ref[2]) & (lax.rem(lane, ids_ref[2]) == ids_ref[expert])
+    gate = jnp.concatenate(
+        [
+            jnp.sum(jnp.where(mine, x_refs[i][:, width:].astype(F32), 0.0), axis=1, keepdims=True)
+            for i in range(shards)
+        ],
+        axis=0,
+    )
+    wg, wu, wd = wg_ref[0], wu_ref[0], wd_ref[0]
+    gate_pre = dot(x, wg)
+    up_pre = dot(x, wu)
+    dact = dot(g, wd, NT)
+    sigma = 1.0 / (1.0 + jnp.exp(-gate_pre))
+    silu = gate_pre * sigma
+    act = silu * up_pre
+    part = jnp.sum(act * dact, axis=1, keepdims=True)
+    lane = lax.broadcasted_iota(jnp.int32, (shards * rows, LANES), 1)
+    dgate_ref[...] += jnp.where(lane == expert, part, 0.0).reshape(dgate_ref.shape)
+    act_low = (gate * act).astype(B16)
+    dact = gate * dact
+    dgate_pre = (dact * up_pre * sigma * (1.0 + gate_pre * (1.0 - sigma))).astype(B16)
+    dup_pre = (dact * silu).astype(B16)
+    ag_ref[...] = act_low.reshape(ag_ref.shape)
+    dg_ref[...] = dgate_pre.reshape(dg_ref.shape)
+    du_ref[...] = dup_pre.reshape(du_ref.shape)
+    moe = dot(act_low, wd)
+    dx = dot(dgate_pre, wg, NT) + dot(dup_pre, wu, NT)
+
+    @pl.when(first)
+    def _():
+        moe_acc[...] = moe
+        dx_acc[...] = dx
+
+    @pl.when(jnp.logical_not(first))
+    def _():
+        moe_acc[...] += moe
+        dx_acc[...] += dx
+
+    @pl.when((expert == pl.num_programs(0) - 1) & (step == steps - 1))
+    def _():
+        moe_ref[...] = moe_acc[...].astype(B16).reshape(moe_ref.shape)
+        dx_ref[...] = dx_acc[...].astype(B16).reshape(dx_ref.shape)
+
+
+def expert_rows(ids, xs, gs, wg, wu, wd, kept, spot, total):
+    shards = len(xs)
+    rows, width = gs[0].shape
+    pair, _, hidden = wg.shape
+    tile = min(512, hidden)
+    steps = hidden // tile
+    whole = lambda a: pl.BlockSpec(a.shape, lambda e, j, ids: (0, 0))
+    flat = pl.BlockSpec((shards, rows, tile), lambda e, j, ids: (spot, 0, e * steps + j))
+    full = pl.BlockSpec((shards, rows, width), lambda e, j, ids: (spot, 0, 0))
+    alone = pl.BlockSpec((shards, rows, width), lambda e, j, ids: (0, 0, 0))
+    in_specs = [whole(a) for a in xs + gs] + [
+        pl.BlockSpec((1, width, tile), lambda e, j, ids: (e, 0, j)),
+        pl.BlockSpec((1, width, tile), lambda e, j, ids: (e, 0, j)),
+        pl.BlockSpec((1, tile, width), lambda e, j, ids: (e, j, 0)),
+    ]
+    operands = list(xs) + list(gs) + [wg, wu, wd]
+    aliases = {}
+    if kept is not None:
+        base = 1 + len(operands)
+        in_specs += [pl.BlockSpec(memory_space=pl.ANY)] * len(kept)
+        operands += list(kept)
+        aliases = {base + i: 3 + i for i in range(len(kept))}
+    kept_hidden = jax.ShapeDtypeStruct((total, rows, pair * hidden), B16)
+    kept_width = jax.ShapeDtypeStruct((total, rows, width), B16)
+    out = pl.pallas_call(
+        functools.partial(expert_kernel, shards=shards, fresh=kept is None),
+        grid_spec=pltpu.PrefetchScalarGridSpec(
+            num_scalar_prefetch=1,
+            grid=(pair, steps),
+            in_specs=in_specs,
+            out_specs=[
+                alone,
+                alone,
+                pl.BlockSpec((shards, rows, LANES), lambda e, j, ids: (0, 0, 0)),
+                flat,
+                flat,
+                flat,
+                full,
+                full,
+            ],
+            scratch_shapes=[
+                pltpu.VMEM((shards * rows, width), F32),
+                pltpu.VMEM((shards * rows, width), F32),
+            ],
+        ),
+        out_shape=[
+            jax.ShapeDtypeStruct((shards, rows, width), B16),
+            jax.ShapeDtypeStruct((shards, rows, width), B16),
+            jax.ShapeDtypeStruct((shards, rows, LANES), F32),
+            kept_hidden,
+            kept_hidden,
+            kept_hidden,
+            kept_width,
+            kept_width,
+        ],
+        input_output_aliases=aliases,
+        compiler_params=pltpu.CompilerParams(vmem_limit_bytes=56 * 2**20),
+        cost_estimate=pl.CostEstimate(
+            flops=12 * shards * rows * width * hidden * pair,
+            bytes_accessed=6 * width * hidden * pair,
+            transcendentals=shards * rows * hidden * pair,
+        ),
+    )(ids, *operands)
+    return out[0], out[1], out[2], out[3:]
+
+
+def split_three(v):
+    high = lax.reduce_precision(v, exponent_bits=8, mantissa_bits=7)
+    middle = lax.reduce_precision(v - high, exponent_bits=8, mantissa_bits=7)
+    return [part.astype(B16) for part in (high, middle, v - high - middle)]
+
+
+def local_fast(
+    tokens,
+    doc_starts,
+    routes,
+    norm_attn,
+    norm_query,
+    norm_key,
+    norm_ffn,
+    w_query,
+    w_key,
+    w_value,
+    w_output,
+    router,
+    expert_gate,
+    expert_up,
+    expert_down,
+    out_grad,
+):
+    devices = lax.axis_size("ctx")
+    rank = lax.axis_index("ctx")
+    group = lax.axis_index("dp")
+    chips = devices // 2
+    chip, core = rank // 2, rank % 2
+    rows, width = tokens.shape
+    experts = router.shape[1]
+    hd = width // HEADS
+    scale = hd ** (-0.5)
+    half = chips // 2
+    order = ring_of(chips)
+    right = [(2 * order[p] + c, 2 * order[(p + 1) % chips] + c) for p in range(chips) for c in range(2)]
+    left = [(b, a) for a, b in right]
+    place_in_ring = jnp.where(chip % 2 == 0, chip // 2, chips - 1 - chip // 2)
+    same_core = [[2 * c + p for c in range(chips)] for p in range(2)]
+
+    def to_right(v):
+        return lax.ppermute(v, "ctx", right)
+
+    def to_left(v):
+        return lax.ppermute(v, "ctx", left)
+
+    def core_swap(v):
+        return lax.ppermute(v, "ctx", [(i, i ^ 1) for i in range(devices)])
+
+    def group_swap(v):
+        return lax.ppermute(v, "dp", [(0, 1), (1, 0)])
+
+    def chip_at(offset):
+        spot = (place_in_ring + offset + chips) % chips
+        return jnp.where(spot < half, 2 * spot, 2 * (chips - 1 - spot) + 1)
+
+    offsets = [0] + [s * o for o in range(1, half) for s in (1, -1)] + [half]
+
+    def ring_gather(v):
+        cut = v.shape[0] // 2
+        got = {0: v}
+        for o in range(1, half):
+            got[-o] = to_right(got[-(o - 1)])
+            got[o] = to_left(got[o - 1])
+        first = to_right(got[-(half - 1)][:cut])
+        second = to_left(got[half - 1][cut:])
+        got[half] = jnp.concatenate([first, second], axis=0)
+        return got
+
+    def in_place(got):
+        out = jnp.zeros((chips,) + got[0].shape, got[0].dtype)
+        for o in offsets:
+            out = lax.dynamic_update_index_in_dim(out, got[o], chip_at(o), 0)
+        return out
+
+    def ring_sum(part):
+        far = part(half)
+        cut = far.shape[1] // 2
+        there = to_right(far[:, :cut])
+        back = to_left(far[:, cut:])
+        near, other = part(half - 1), part(1 - half)
+        there = jnp.concatenate([near[:, :cut] + there, near[:, cut:]], axis=1)
+        back = jnp.concatenate([other[:, :cut], other[:, cut:] + back], axis=1)
+        for o in range(half - 2, 0, -1):
+            there = to_right(there) + part(o)
+            back = to_left(back) + part(-o)
+        return to_right(there).astype(F32) + to_left(back).astype(F32) + part(0).astype(F32)
+
+    def sum_chips(v):
+        step = 2
+        while step < devices:
+            v = v + lax.ppermute(v, "ctx", [(i, i ^ step) for i in range(devices)])
+            step *= 2
+        return v
+
+    def sum_all(v):
+        v = v + core_swap(v)
+        return sum_chips(v + group_swap(v))
+
+    def by_core(mine, other, axis):
+        return jnp.where(core == 0, jnp.stack([mine, other], axis), jnp.stack([other, mine], axis))
+
+    def pick(pair, which):
+        return jnp.where(which == 0, pair[0], pair[1])
+
+    wg = jnp.concatenate([expert_gate, core_swap(expert_gate)], axis=0)
+    wu = jnp.concatenate([expert_up, core_swap(expert_up)], axis=0)
+    wd = jnp.concatenate([expert_down, core_swap(expert_down)], axis=0)
+
+    inputs = tokens.astype(F32)
+    n1 = norm_rows(inputs, norm_attn).astype(B16)
+    lane = lax.broadcasted_iota(jnp.int32, (rows, LANES), 1)
+    flags = jnp.where(lane == 0, doc_starts[:, None], 0).astype(B16)
+    n1_got = ring_gather(jnp.concatenate([n1, flags], axis=1))
+
+    slabs = []
+    for w in (w_query, w_key, w_value):
+        pair = w.reshape(rows, chips, 2, hd)
+        slabs.append(jnp.where(group == 0, pair[:, :, 0], pair[:, :, 1]))
+    slab = jnp.concatenate(slabs, axis=2).transpose(1, 0, 2)
+    own = lax.all_to_all(slab, "ctx", split_axis=0, concat_axis=0, axis_index_groups=same_core, tiled=True)
+    other = group_swap(own)
+    low_head, high_head = jnp.where(group == 0, own, other), jnp.where(group == 0, other, own)
+    columns = []
+    for i in range(3):
+        columns += [low_head[:, :, i * hd : (i + 1) * hd], high_head[:, :, i * hd : (i + 1) * hd]]
+    columns = jnp.concatenate(columns, axis=2)
+    wide = 6 * hd
+    w_in = by_core(columns, core_swap(columns), 1).reshape(width, wide)
+    w_out = by_core(w_output, core_swap(w_output), 0).reshape(2 * hd, width)
+
+    flags = in_place({o: v[:, width].astype(F32) for o, v in n1_got.items()})
+    n1_all = in_place({o: v[:, :width] for o, v in n1_got.items()}).reshape(chips * rows, width)
+    count = chips * rows
+    qkv = dot(n1_all, w_in)
+    qp, kp, vp = qkv[:, : 2 * hd], qkv[:, 2 * hd : 4 * hd], qkv[:, 4 * hd :]
+    squares = jnp.stack([jnp.sum(qp * qp, axis=1), jnp.sum(kp * kp, axis=1)])
+    squares = sum_chips(squares.reshape(2 * chips, rows)).reshape(2, count, 1)
+    q_scale = lax.rsqrt(squares[0] / width + EPS)
+    k_scale = lax.rsqrt(squares[1] / width + EPS)
+    gain_q = lax.dynamic_slice(norm_query, (chip * 2 * hd,), (2 * hd,))
+    gain_k = lax.dynamic_slice(norm_key, (chip * 2 * hd,), (2 * hd,))
+
+    place = (2 * lax.broadcasted_iota(jnp.int32, (chips, rows, 1), 0) + core) * rows
+    place = place + lax.broadcasted_iota(jnp.int32, (chips, rows, 1), 1)
+    freq = THETA ** (-jnp.arange(hd // 2, dtype=F32) * 2.0 / hd)
+    angle = place.reshape(count, 1).astype(F32) * freq[None, :]
+    cosine, sine = jnp.cos(angle), jnp.sin(angle)
+    cosine = jnp.concatenate([cosine] * 4, axis=1)
+    sine = jnp.concatenate([-sine, sine] * 2, axis=1)
+
+    def halves(v):
+        h = hd // 2
+        return jnp.concatenate([v[:, h:hd], v[:, :h], v[:, hd + h :], v[:, hd : hd + h]], axis=1)
+
+    def turn(v):
+        return v * cosine + halves(v) * sine
+
+    def turn_back(v):
+        return v * cosine + halves(v * sine)
+
+    query = turn(qp * q_scale * gain_q).astype(B16)
+    keys = turn(kp * k_scale * gain_k).astype(B16)
+    values = vp.astype(B16)
+
+    def to_heads(parts):
+        pairs = [(v[:, :hd], v[:, hd:]) for v in parts]
+        mine = jnp.concatenate([pick(p, core) for p in pairs], axis=1)
+        away = jnp.concatenate([pick(p, 1 - core) for p in pairs], axis=1)
+        shape = (chips, rows, mine.shape[1])
+        return by_core(mine.reshape(shape), core_swap(away).reshape(shape), 1).reshape(devices * rows, -1)
+
+    def to_tokens(v):
+        v = v.reshape(chips, 2, rows, -1)
+        mine, away = pick((v[:, 0], v[:, 1]), core), pick((v[:, 0], v[:, 1]), 1 - core)
+        mine, other = mine.reshape(count, -1), core_swap(away).reshape(count, -1)
+        low_head, high_head = pick((mine, other), core), pick((other, mine), core)
+        parts = []
+        for i in range(mine.shape[1] // hd):
+            parts.append(
+                jnp.concatenate([low_head[:, i * hd : (i + 1) * hd], high_head[:, i * hd : (i + 1) * hd]], axis=1)
+            )
+        return parts
+
+    heads = to_heads([query, keys, values])
+    qh, kh, vh = heads[:, :hd], heads[:, hd : 2 * hd], heads[:, 2 * hd :]
+    flags = by_core(flags, core_swap(flags), 1).reshape(devices, rows)
+    tri = (lax.broadcasted_iota(jnp.int32, (rows, rows), 0) <= lax.broadcasted_iota(jnp.int32, (rows, rows), 1)).astype(F32)
+    before = (
+        lax.broadcasted_iota(jnp.int32, (devices, devices), 1) < lax.broadcasted_iota(jnp.int32, (devices, devices), 0)
+    ).astype(F32)
+    seg = jnp.dot(flags, tri) + jnp.dot(before, jnp.broadcast_to(jnp.sum(flags, axis=1, keepdims=True), (devices, rows)))
+    seg_row, seg_col = seg.reshape(1, devices * rows), seg.reshape(devices * rows, 1)
+    everything = devices * rows
+    block = min(256, everything)
+    params = pltpu.CompilerParams(vmem_limit_bytes=56 * 2**20)
+    attn, lse = pl.pallas_call(
+        functools.partial(attention_forward, block=block, scale=scale),
+        out_shape=[
+            jax.ShapeDtypeStruct((everything, hd), F32),
+            jax.ShapeDtypeStruct((1, everything), F32),
+        ],
+        compiler_params=params,
+        cost_estimate=pl.CostEstimate(
+            flops=2 * everything * everything * hd, bytes_accessed=8 * everything * hd, transcendentals=everything * everything // 2
+        ),
+    )(qh, kh, vh, seg_row, seg_col)
+    (attn_low,) = to_tokens(attn.astype(B16))
+    out_part = dot(attn_low, w_out).astype(B16).reshape(chips, rows, width)
+    h1 = inputs + ring_sum(lambda o: lax.dynamic_index_in_dim(out_part, chip_at(o), 0, keepdims=False))
+
+    n2 = norm_rows(h1, norm_ffn).astype(B16)
+    probs = jax.nn.softmax(dot(n2, router), axis=-1)
+    chosen = jnp.sum(
+        (routes[:, :, None] == jnp.arange(experts, dtype=jnp.int32)[None, None, :]).astype(F32), axis=1
+    )
+    sent = split_three(probs * chosen)
+    sent.append(jnp.zeros((rows, LANES - 3 * experts), B16))
+    top_got = ring_gather(out_grad)
+    n2_got = ring_gather(jnp.concatenate([n2] + sent, axis=1))
+    ids = jnp.stack([rank, rank ^ 1, jnp.int32(experts)]).astype(jnp.int32)
+    moe_part, dn2_part, dgate_part = {}, {}, {}
+    kept = None
+    chunks = [([0], 0)] + [([o, -o], o) for o in range(1, half)] + [([half], 1)]
+    for which, spot in chunks:
+        moe, dn2, dgate, kept = expert_rows(
+            ids, [n2_got[o] for o in which], [top_got[o] for o in which], wg, wu, wd, kept, spot, chips
+        )
+        for i, o in enumerate(which):
+            moe_part[o], dn2_part[o], dgate_part[o] = moe[i], dn2[i], dgate[i]
+    act_all, dgate_pre_all, dup_pre_all, x_all, top_all = [v.reshape(count, -1) for v in kept]
+    n2_sum = ring_sum(lambda o: dn2_part[o])
+
+    dgates = jnp.stack([dgate_part[o][:, :2] for o in offsets])
+    there = jnp.stack([chip_at(o) for o in offsets])
+    spread_out = (there[None, :] == jnp.arange(chips)[:, None]).astype(F32)
+    dgates = jnp.dot(spread_out, dgates.transpose(0, 2, 1).reshape(chips, 2 * rows), precision=HIGH)
+    dgates = dgates.reshape(chips, 2, rows)
+    dgates = jnp.where(core == 0, dgates, dgates[:, ::-1])
+    dgates = lax.all_to_all(dgates, "ctx", split_axis=0, concat_axis=0, axis_index_groups=same_core, tiled=True)
+    prob_grad = dgates.reshape(experts, rows).T * chosen
+    logit_grad = probs * (prob_grad - jnp.sum(probs * prob_grad, axis=-1, keepdims=True))
+    router_term = lax.dot_general(logit_grad, n2.astype(F32), TN, precision=HIGH)
+    n2_grad = n2_sum + jnp.dot(logit_grad, router.astype(F32).T, precision=HIGH)
+    grad_top = out_grad.astype(F32)
+    unused_value, ffn_back = jax.vjp(norm_rows, h1, norm_ffn)
+    h1_part, ffn_gain_grad = ffn_back(n2_grad)
+    h1_grad = grad_top + h1_part
+    h1_low = h1_grad.astype(B16)
+
+    h1_all = in_place(ring_gather(h1_low)).reshape(count, width)
+    attn_grad = dot(h1_all, w_out, NT).astype(B16)
+    gh = to_heads([attn_grad])
+    dq, dk, dv = pl.pallas_call(
+        functools.partial(attention_backward, block=block, scale=scale),
+        out_shape=[jax.ShapeDtypeStruct((everything, hd), F32)] * 3,
+        compiler_params=params,
+        cost_estimate=pl.CostEstimate(
+            flops=5 * everything * everything * hd, bytes_accessed=24 * everything * hd, transcendentals=everything * everything // 2
+        ),
+    )(qh, kh, vh, gh, attn, lse, seg_row, seg_col)
+    query_grad, key_grad, value_grad = to_tokens(jnp.concatenate([dq, dk, dv], axis=1))
+    query_grad, key_grad = turn_back(query_grad), turn_back(key_grad)
+    inner = jnp.stack(
+        [jnp.sum(query_grad * gain_q * qp, axis=1), jnp.sum(key_grad * gain_k * kp, axis=1)]
+    )
+    inner = sum_chips(inner.reshape(2 * chips, rows)).reshape(2, count, 1)
+    qp_grad = q_scale * (query_grad * gain_q) - qp * (q_scale * q_scale * q_scale * (inner[0] / width))
+    kp_grad = k_scale * (key_grad * gain_k) - kp * (k_scale * k_scale * k_scale * (inner[1] / width))
+    query_gain = jnp.sum(query_grad * qp * q_scale, axis=0)
+    key_gain = jnp.sum(key_grad * kp * k_scale, axis=0)
+    qkv_low = jnp.concatenate([qp_grad.astype(B16), kp_grad.astype(B16), value_grad.astype(B16)], axis=1)
+    n1_part = dot(qkv_low, w_in, NT).astype(B16).reshape(chips, rows, width)
+    n1_grad = ring_sum(lambda o: lax.dynamic_index_in_dim(n1_part, chip_at(o), 0, keepdims=False))
+    unused_norm, attn_back = jax.vjp(lambda v: norm_rows(v, norm_attn), inputs)
+    (input_part,) = attn_back(n1_grad)
+    tokens_grad = (h1_grad + input_part).astype(B16)
+
+    block_out = (h1 + ring_sum(lambda o: moe_part[o])).astype(B16)
+
+    w_part = dot(n1_all, qkv_low, TN)
+    attn_gain = jnp.sum(w_part * w_in.astype(F32), axis=1) / norm_attn
+
+    def own_head(v, axis):
+        pairs = [lax.slice_in_dim(v, i * hd, (i + 1) * hd, axis=axis) for i in range(v.shape[axis] // hd)]
+        pairs = [(pairs[i], pairs[i + 1]) for i in range(0, len(pairs), 2)]
+        mine = jnp.concatenate([pick(p, core) for p in pairs], axis=axis)
+        away = jnp.concatenate([pick(p, 1 - core) for p in pairs], axis=axis)
+        return mine + core_swap(away)
+
+    w_head = own_head(w_part, 1).reshape(2, width // 2, 3 * hd)
+    w_mine = pick((w_head[0], w_head[1]), group) + group_swap(
+        pick((w_head[0], w_head[1]), 1 - group).astype(B16)
+    ).astype(F32)
+    w_mine = w_mine.astype(B16).reshape(devices, -1, 3 * hd)
+    w_mine = lax.all_to_all(w_mine, "ctx", split_axis=0, concat_axis=0, tiled=True)
+    w_mine = w_mine.transpose(1, 0, 2).astype(F32)
+    slab_rows = w_mine.shape[0]
+    wq_grad, wk_grad, wv_grad = [
+        w_mine[:, :, i * hd : (i + 1) * hd].reshape(slab_rows, width) for i in range(3)
+    ]
+    o_head = own_head(dot(attn_low, h1_all, TN), 0)
+    o_head = (o_head + group_swap(o_head.astype(B16)).astype(F32)).astype(B16)
+    wo_grad = None
+    for i in range(2):
+        moves = [
+            (g * devices + devices // 2 * g + j, g * devices + 2 * j + i) for g in range(2) for j in range(devices // 2)
+        ]
+        piece = lax.ppermute(o_head[i * slab_rows : (i + 1) * slab_rows], ("dp", "ctx"), moves)
+        wo_grad = piece if wo_grad is None else jnp.where(core == 0, wo_grad, piece)
+    wo_grad = wo_grad.astype(F32)
+
+    def expert_grad(left_rows, right_rows, axis):
+        hidden = expert_gate.shape[2]
+        if axis == 1:
+            terms = [dot(left_rows, right_rows[:, i * hidden : (i + 1) * hidden], TN) for i in range(2)]
+        else:
+            terms = [dot(left_rows[:, i * hidden : (i + 1) * hidden], right_rows, TN) for i in range(2)]
+        total = terms[0] + core_swap(terms[1].astype(B16)).astype(F32)
+        size = total.shape[axis] // 2
+        pieces = (lax.slice_in_dim(total, 0, size, axis=axis), lax.slice_in_dim(total, size, 2 * size, axis=axis))
+        away = group_swap(pick(pieces, 1 - group).astype(B16))
+        return (pick(pieces, group) + away.astype(F32))[None]
+
+    down_grad_out = expert_grad(act_all, top_all, 0)
+    gate_grad_out = expert_grad(x_all, dgate_pre_all, 1)
+    up_grad_out = expert_grad(x_all, dup_pre_all, 1)
+
+    def placed(v):
+        return lax.dynamic_update_slice(jnp.zeros((width,), F32), v, (chip * 2 * hd,))
+
+    small = sum_all(
+        jnp.concatenate(
+            [router_term, jnp.stack([ffn_gain_grad, attn_gain, placed(query_gain), placed(key_gain)])], axis=0
+        )
+    )
+    router_sum, gains = small[:experts].T, small[experts:]
+    return (
+        block_out,
+        tokens_grad,
+        gains[1],
+        gains[2],
+        gains[3],
+        gains[0],
+        wq_grad,
+        wk_grad,
+        wv_grad,
+        wo_grad,
+        router_sum,
+        gate_grad_out,
+        up_grad_out,
+        down_grad_out,
+    )
+
+
+def local(*args):
+    devices, groups = lax.axis_size("ctx"), lax.axis_size("dp")
+    experts, owned = args[11].shape[1], args[12].shape[0]
+    fits = devices == HEADS == experts and groups == 2 and owned == 1 and 3 * experts <= LANES
+    return (local_fast if fits else local_general)(*args)
+
+
 def solution(mesh):
     return jax.shard_map(
         local,

time: 2930 us -> 881 us (0.30)
  waiting for transfers between devices: 1440 us -> 305 us
  blocking collectives: 415 us -> 0 us
  local copies, waits for them, and re-layouts: 277 us -> 113 us
  matrix products: 231 us -> 76.2 us
  other arithmetic: 226 us -> 93.2 us
  Pallas kernels: 0 us -> 129 us
  starting transfers between devices: 262 us -> 156 us
  loops' own time: 45.1 us -> 0 us
    unnamed x12 -> x0, waiting for transfers between devices: 631 us -> none
    all_gather x6 -> x0, waiting for transfers between devices: 313 us -> none  [the longest x1 74.9 us: local(): lax.all_gather(w_value, 'ctx', axis=0, tiled=True)]
    all_to_all x2 -> x0, blocking collectives: 304 us -> none  [the longest x1 158 us: local(): lax.all_to_all(send, 'ctx', split_axis=0, concat_axis=0, tiled=True)]
    all_to_all x2 -> x3, waiting for transfers between devices: 240 us -> 14.1 us  [the longest x1 13.3 us: local_fast(): lax.all_to_all(w_mine, 'ctx', split_axis=0, concat_axis=0, tiled=True)]
    ppermute x80 -> x98, waiting for transfers between devices: 129 us -> 291 us  [the longest x7 122 us: group_swap(): return lax.ppermute(v, 'dp', [(0, 1), (1, 0)])]
    dot_general x68 -> x18, matrix products: 231 us -> 76.2 us  [the longest x13 74.9 us: dot(): return lax.dot_general(a, b, dims, preferred_element_type=F32)]
    pallas_call x0 -> x7, Pallas kernels: none -> 129 us  [the longest x5 110 us: expert_rows(): pl.pallas_call(functools.partial(expert_kernel, shards=shards, fresh=kept...]
    psum x1 -> x0, waiting for transfers between devices: 125 us -> none  [local(): lax.psum((attn_gain_grad, query_gain_grad, key_gain_grad, ffn_gain_grad,...]
  transfers between devices with their start and end apart: 93 -> 101, of which waited for: 33 -> 44; matrix products, arithmetic and copies ran while one was open for 22% -> 25% of each run, Pallas kernels for 0% -> 12%
where the time goes in v1:
time: 881 us; the launch traced here: 875 us
  waiting for transfers between devices  305 us (35%)
  starting transfers between devices  156 us (18%)
  Pallas kernels  129 us (15%)
  local copies, waits for them, and re-layouts  113 us (13%)
  other arithmetic  93.2 us (11%)
  matrix products  76.2 us (9%)
    ppermute x7, waiting for transfers between devices, group_swap(): return lax.ppermute(v, 'dp', [(0, 1), (1, 0)])  122 us
    pallas_call x5, Pallas kernels, expert_rows(): pl.pallas_call(functools.partial(expert_kernel, shards=shards, fresh=kept...  110 us
    ppermute x32, waiting for transfers between devices, to_right(): return lax.ppermute(v, 'ctx', right)  81 us
    dot_general x13, matrix products, dot(): return lax.dot_general(a, b, dims, preferred_element_type=F32)  74.9 us
    ppermute x32, waiting for transfers between devices, to_left(): return lax.ppermute(v, 'ctx', left)  70.4 us
    ppermute x16, starting transfers between devices, core_swap(): return lax.ppermute(v, 'ctx', [(i, i ^ 1) for i in range(devices)])  45.1 us
    ppermute x32, starting transfers between devices, to_right(): return lax.ppermute(v, 'ctx', right)  40.1 us
    unnamed x199, local copies, waits for them, and re-layouts  32.4 us
  transfers between devices with their start and end apart: 101, of which 44 were waited for; matrix products, arithmetic and copies ran while one was open for 25% of the time, Pallas kernels for 12%

profile of v1, /device:TPU:9, one launch (start us, length us, event | category | flops | bytes accessed | tf_op | source)
XLA Modules:
  0.0 875.5 jit_solution(2923703910467368298)
XLA Ops:
  25.9 23.4 %collective-permute-done.2 = bf16[128,2176]{1,0:T(8,128)(2,1)S(1)} collective-permute-done((bf16[128,2176]{1,0:T(8,128)(2,1)}, bf16[128,2176]{1,0:T(8,128)(2,1)S(1)}, u32[]{:S(2)}, u32[]{:S(2)}) %collective-permute-start.2) | collective-permute-done | bytes 557088 | tf_op jit(solution)/shard_map/ppermute | solution.py:604
  128.0 8.9 %shard_map.263 = (f32[2048,128]{1,0:T(8,128)}, f32[1,2048]{1,0:T(1,128)}) custom-call(bf16[2048,128]{1,0:T(8,128)(2,1)} %get-tuple-element.164.q_ref, bf16[2048,128]{1,0:T(8,128)(2,1)} %get-tuple-element.163.k_ref, bf16[2048,128]{1,0:T(8,128)(2,1)} %get-tuple-element.162.v_ref, f32[1,2048]{1,0:T(1,128)} %bitcast.397, f32[2048,1]{1,0:T(8,128)} %copy.240.seg_col_ref), custom_call_target="tpu_custom_call" | custom-call | flops 1073741824 | bytes 2097152 | tf_op jit(solution)/shard_map/pallas_call | solution.py:756
  186.8 10.8 %collective-permute-start.18 = (bf16[128,2048]{1,0:T(8,128)(2,1)S(1)}, bf16[128,2048]{1,0:T(8,128)(2,1)}, u32[]{:S(2)}, u32[]{:S(2)}) collective-permute-start(bf16[128,2048]{1,0:T(8,128)(2,1)S(1)} %pad_maximum_fusion.12), channel_id=1, source_target_pairs={{0,4},{1,5},{4,8},{5,9},{8,12},{9,13},{12,14},{13,15},{14,10},{15,... | collective-permute-start | bytes 1572872 | tf_op jit(solution)/shard_map/ppermute | solution.py:601
  241.4 19.6 %shard_map.264 = (bf16[1,128,2048]{2,1,0:T(8,128)(2,1)}, bf16[1,128,2048]{2,1,0:T(8,128)(2,1)}, f32[1,128,128]{2,1,0:T(8,128)}, bf16[8,128,2048]{2,1,0:T(8,128)(...) custom-call(s32[3]{0:T(128)} %pad_add_fusion.ids_ref, ...), custom_call_target="tpu_custom_call" | custom-call | flops 6442450944 | bytes 25165824 | tf_op jit(solution)/shard_map/pallas_call | solution.py:518
  264.1 23.5 %shard_map.265 = (bf16[2,128,2048]{2,1,0:T(8,128)(2,1)}, bf16[2,128,2048]{2,1,0:T(8,128)(2,1)}, f32[2,128,128]{2,1,0:T(8,128)}, bf16[8,128,2048]{2,1,0:T(8,128)(...) custom-call(s32[3]{0:T(128)} %pad_add_fusion.ids_ref, ...), custom_call_target="tpu_custom_call", output_to_operand_aliasing={{3}: (8, {}), {4}: (9, {}), {5}: (10, {}), {6}: (11, {}), {... | custom-call | flops 12884901888 | bytes 25165824 | tf_op jit(solution)/shard_map/pallas_call | solution.py:518
  290.2 23.6 %shard_map.266 = (bf16[2,128,2048]{2,1,0:T(8,128)(2,1)}, bf16[2,128,2048]{2,1,0:T(8,128)(2,1)}, f32[2,128,128]{2,1,0:T(8,128)}, bf16[8,128,2048]{2,1,0:T(8,128)(...) custom-call(s32[3]{0:T(128)} %pad_add_fusion.ids_ref, ...), custom_call_target="tpu_custom_call", output_to_operand_aliasing={{3}: (8, {}), {4}: (9, {}), {5}: (10, {}), {6}: (11, {}), {... | custom-call | flops 12884901888 | bytes 25165824 | tf_op jit(solution)/shard_map/pallas_call | solution.py:518
  318.3 23.6 %shard_map.267 = (bf16[2,128,2048]{2,1,0:T(8,128)(2,1)}, bf16[2,128,2048]{2,1,0:T(8,128)(2,1)}, f32[2,128,128]{2,1,0:T(8,128)}, bf16[8,128,2048]{2,1,0:T(8,128)(...) custom-call(s32[3]{0:T(128)} %pad_add_fusion.ids_ref, ...), custom_call_target="tpu_custom_call", output_to_operand_aliasing={{3}: (8, {}), {4}: (9, {}), {5}: (10, {}), {6}: (11, {}), {... | custom-call | flops 12884901888 | bytes 25165824 | tf_op jit(solution)/shard_map/pallas_call | solution.py:518
  348.2 19.6 %shard_map.268 = (bf16[1,128,2048]{2,1,0:T(8,128)(2,1)}, bf16[1,128,2048]{2,1,0:T(8,128)(2,1)}, f32[1,128,128]{2,1,0:T(8,128)}, bf16[8,128,2048]{2,1,0:T(8,128)(...) custom-call(s32[3]{0:T(128)} %pad_add_fusion.ids_ref, ...), custom_call_target="tpu_custom_call", output_to_operand_aliasing={{3}: (6, {}), {4}: (7, {}), {5}: (8, {}), {6}: (9, {}), {7}... | custom-call | flops 6442450944 | bytes 25165824 | tf_op jit(solution)/shard_map/pallas_call | solution.py:518
  367.8 9.5 %convolution_convert_fusion.2 = bf16[1024,2048]{1,0:T(8,128)(2,1)} fusion(bf16[1024,2048]{1,0:T(8,128)(2,1)} %bitcast.345, bf16[1024,2048]{1,0:T(8,128)(2,1)} %bitcast.335), kind=kOutput, calls=%fused_computation.12 | convolution fusion | flops 4297064448 | bytes 10485760 | tf_op jit(solution)/shard_map/dot_general | solution.py:382
  377.3 16.5 %collective-permute-start.96 = (bf16[1024,2048]{1,0:T(8,128)(2,1)}, bf16[1024,2048]{1,0:T(8,128)(2,1)}, u32[]{:S(2)}, u32[]{:S(2)}) collective-permute-start(bf16[1024,2048]{1,0:T(8,128)(2,1)} %convolution_convert_fusion.2), channel_id=1, source_target_pairs={{0,1},{1,0},{2,3},{3,2},{4,5},{5,4},{6,7},{7,6},{8,9},{9,8},{10,11... | collective-permute-start | bytes 12582920 | tf_op jit(solution)/shard_map/ppermute | solution.py:607
  425.2 10.1 %collective-permute-done.57 = bf16[128,2048]{1,0:T(8,128)(2,1)S(1)} collective-permute-done((bf16[128,2048]{1,0:T(8,128)(2,1)S(1)}, bf16[128,2048]{1,0:T(8,128)(2,1)S(1)}, u32[]{:S(2)}, u32[]{:S(2)}) %collective-permute-start.57) | collective-permute-done | bytes 524320 | tf_op jit(solution)/shard_map/ppermute | solution.py:604
  450.2 8.8 %collective-permute-done.49 = bf16[128,2048]{1,0:T(8,128)(2,1)S(1)} collective-permute-done((bf16[128,2048]{1,0:T(8,128)(2,1)S(1)}, bf16[128,2048]{1,0:T(8,128)(2,1)S(1)}, u32[]{:S(2)}, u32[]{:S(2)}) %collective-permute-start.49) | collective-permute-done | bytes 524320 | tf_op jit(solution)/shard_map/ppermute | solution.py:604
  494.5 8.7 collective-permute-done.62
  522.8 8.3 collective-permute-start.68
  536.9 9.9 %shard_map.269 = (f32[2048,128]{1,0:T(8,128)}, f32[2048,128]{1,0:T(8,128)}, f32[2048,128]{1,0:T(8,128)}) custom-call(bf16[2048,128]{1,0:T(8,128)(2,1)} %get-tuple-element.164.q_ref, bf16[2048,128]{1,0:T(8,128)(2,1)} %get-tuple-element.163.k_ref, bf16[2048,128]{1,0:T(8,128)(2,1)} %get-tuple-element.162.v_ref, bf16[2048,128]{1,0:T(8,128)(2,1)} %bitcast.384, ...), custom_call_target="tpu_custom_call" | custom-call | flops 2684354560 | bytes 6291456 | tf_op jit(solution)/shard_map/pallas_call | solution.py:813
  554.4 9.4 %convert_add_fusion = f32[1024,2048]{1,0:T(8,128)S(1)} fusion(bf16[1024,2048]{1,0:T(8,128)(2,1)} %collective-permute-done.96, bf16[1024,2048]{1,0:T(8,128)(2,1)} %bitcast.346, bf16[1024,2048]{1,0:T(8,128)(2,1)} %bitcast.336), kind=kOutput, calls=%fused_computation | convolution fusion | flops 4299161600 | bytes 18874368 | tf_op jit(solution)/shard_map/dot_general | solution.py:382
  569.1 8.3 convert_add_fusion.1
  582.8 8.6 convert_add_fusion.2
  596.7 72.5 %collective-permute-done.89 = bf16[128,2048]{1,0:T(8,128)(2,1)S(1)} collective-permute-done((bf16[128,2048]{1,0:T(8,128)(2,1)S(1)}, bf16[128,2048]{1,0:T(8,128)(2,1)S(1)}, u32[]{:S(2)}, u32[]{:S(2)}) %collective-permute-start.89) | collective-permute-done | bytes 524320 | tf_op jit(solution)/shard_map/ppermute | solution.py:610
  700.3 9.2 %multiply_reduce_fusion = (f32[2048]{0:T(1024)S(1)}, f32[2048,768]{0,1:T(8,128)}) fusion(bf16[2048,768]{0,1:T(8,128)(2,1)S(1)} %copy-done.35, bf16[1024,2048]{1,0:T(8,128)(2,1)} %bitcast.8, bf16[1024,128]{0,1:T(8,128)(2,1)S(1)} %slice.1004, bf16[1024,128]{0,1:T(8,128)(2,1)S(1)} %slice.1005, bf16[1024,256]{0,1:T(8,128)(2,1)S(1)} %get-tuple-element.148, ...), kind=kOutput, calls=%fused_computation.3 | convolution fusion | flops 3232233472 | bytes 15212544 | tf_op jit(solution)/shard_map/dot_general | solution.py:382
  733.9 45.0 %collective-permute-done.82 = f32[20,2048]{1,0:T(8,128)S(1)} collective-permute-done((f32[20,2048]{1,0:T(8,128)S(1)}, f32[20,2048]{1,0:T(8,128)S(1)}, u32[]{:S(2)}, u32[]{:S(2)}) %collective-permute-start.82) | collective-permute-done | bytes 163872 | tf_op jit(solution)/shard_map/ppermute | solution.py:610
  822.9 10.5 %collective-permute-done.75 = bf16[128,2048]{1,0:T(8,128)(2,1)S(1)} collective-permute-done((bf16[128,2048]{1,0:T(8,128)(2,1)S(1)}, bf16[128,2048]{1,0:T(8,128)(2,1)S(1)}, u32[]{:S(2)}, u32[]{:S(2)}) %collective-permute-start.75) | collective-permute-done | bytes 524320 | tf_op jit(solution)/shard_map/ppermute | solution.py:601
  840.4 11.2 %all-to-all-start.2 = ((bf16[16,64,384]{2,1,0:T(8,128)(2,1)}), bf16[16,64,384]{2,1,0:T(8,128)(2,1)}, u32[]{:S(2)}, u32[]{:S(2)}) async-start(bf16[16,64,384]{2,1,0:T(8,128)(2,1)} %bitcast.369), calls=%async_computation.2 | async-start | bytes 1572864 | tf_op jit(solution)/shard_map/all_to_all | solution.py:855
  857.9 13.3 %all-to-all-done.2 = bf16[16,64,384]{2,1,0:T(8,128)(2,1)} async-done(((bf16[16,64,384]{2,1,0:T(8,128)(2,1)}), bf16[16,64,384]{2,1,0:T(8,128)(2,1)}, u32[]{:S(2)}, u32[]{:S(2)}) %all-to-all-start.2) | async-done | bytes 786464 | tf_op jit(solution)/shard_map/all_to_all | solution.py:855
  (639 shorter events, 459.6 us)
Async XLA Ops:
  10.4 42.3 %all-to-all-start = ((bf16[8,128,384]{1,2,0:T(8,128)(2,1)}), bf16[8,128,384]{1,2,0:T(8,128)(2,1)S(1)}, u32[]{:S(2)}, u32[]{:S(2)}) async-start(bf16[8,128,384]{1,2,0:T(8,128)(2,1)} %maximum_bitcast_fusion), calls=%async_computation | async-start | bytes 1572864 | tf_op jit(solution)/shard_map/all_to_all | solution.py:680
  21.7 27.6 %collective-permute-start.2 = (bf16[128,2176]{1,0:T(8,128)(2,1)}, bf16[128,2176]{1,0:T(8,128)(2,1)S(1)}, u32[]{:S(2)}, u32[]{:S(2)}) collective-permute-start(bf16[128,2176]{1,0:T(8,128)(2,1)} %collective-permute-done), channel_id=1, source_target_pairs={{4,0},{5,1},{8,4},{9,5},{12,8},{13,9},{14,12},{15,13},{10,14},{11,... | collective-permute-start | bytes 1671176 | tf_op jit(solution)/shard_map/ppermute | solution.py:604
  22.1 27.5 %collective-permute-start.3 = (bf16[128,2176]{1,0:T(8,128)(2,1)S(1)}, bf16[128,2176]{1,0:T(8,128)(2,1)}, u32[]{:S(2)}, u32[]{:S(2)}) collective-permute-start(bf16[128,2176]{1,0:T(8,128)(2,1)S(1)} %collective-permute-done.1), channel_id=1, source_target_pairs={{0,4},{1,5},{4,8},{5,9},{8,12},{9,13},{12,14},{13,15},{14,10},{15,... | collective-permute-start | bytes 1671176 | tf_op jit(solution)/shard_map/ppermute | solution.py:601
  139.7 76.2 %collective-permute-start.37 = (bf16[1,2048,1024]{2,1,0:T(8,128)(2,1)}, bf16[1,2048,1024]{2,1,0:T(8,128)(2,1)}, u32[]{:S(2)}, u32[]{:S(2)}) collective-permute-start(bf16[1,2048,1024]{2,1,0:T(8,128)(2,1)} %param.28), channel_id=1, source_target_pairs={{0,1},{1,0},{2,3},{3,2},{4,5},{5,4},{6,7},{7,6},{8,9},{9,8},{10,11... | collective-permute-start | bytes 12582920 | tf_op jit(solution)/shard_map/ppermute | solution.py:607
  140.1 86.5 %collective-permute-start.38 = (bf16[1,2048,1024]{2,1,0:T(8,128)(2,1)}, bf16[1,2048,1024]{2,1,0:T(8,128)(2,1)}, u32[]{:S(2)}, u32[]{:S(2)}) collective-permute-start(bf16[1,2048,1024]{2,1,0:T(8,128)(2,1)} %param.29), channel_id=1, source_target_pairs={{0,1},{1,0},{2,3},{3,2},{4,5},{5,4},{6,7},{7,6},{8,9},{9,8},{10,11... | collective-permute-start | bytes 12582920 | tf_op jit(solution)/shard_map/ppermute | solution.py:607
  142.2 87.2 %collective-permute-start.39 = (bf16[1,1024,2048]{2,1,0:T(8,128)(2,1)}, bf16[1,1024,2048]{2,1,0:T(8,128)(2,1)}, u32[]{:S(2)}, u32[]{:S(2)}) collective-permute-start(bf16[1,1024,2048]{2,1,0:T(8,128)(2,1)} %param.30), channel_id=1, source_target_pairs={{0,1},{1,0},{2,3},{3,2},{4,5},{5,4},{6,7},{7,6},{8,9},{9,8},{10,11... | collective-permute-start | bytes 12582920 | tf_op jit(solution)/shard_map/ppermute | solution.py:607
  263.3 26.9 %collective-permute-start.29 = (bf16[128,2176]{1,0:T(8,128)(2,1)S(1)}, bf16[128,2176]{1,0:T(8,128)(2,1)}, u32[]{:S(2)}, u32[]{:S(2)}) collective-permute-start(bf16[128,2176]{1,0:T(8,128)(2,1)S(1)} %collective-permute-done.28.refs_1_), channel_id=1, source_target_pairs={{0,4},{1,5},{4,8},{5,9},{8,12},{9,13},{12,14},{13,15},{14,10},{15,... | collective-permute-start | bytes 1671176 | tf_op jit(solution)/shard_map/ppermute | solution.py:601
  288.7 27.6 %collective-permute-start.27 = (bf16[128,2176]{1,0:T(8,128)(2,1)}, bf16[128,2176]{1,0:T(8,128)(2,1)S(1)}, u32[]{:S(2)}, u32[]{:S(2)}) collective-permute-start(bf16[128,2176]{1,0:T(8,128)(2,1)} %collective-permute-done.26.refs_0_), channel_id=1, source_target_pairs={{4,0},{5,1},{8,4},{9,5},{12,8},{13,9},{14,12},{15,13},{10,14},{11,... | collective-permute-start | bytes 1671176 | tf_op jit(solution)/shard_map/ppermute | solution.py:604
  315.6 30.7 %collective-permute-start.40 = (bf16[64,2176]{1,0:T(8,128)(2,1)}, bf16[64,2176]{1,0:T(8,128)(2,1)}, u32[]{:S(2)}, u32[]{:S(2)}) collective-permute-start(bf16[64,2176]{1,0:T(8,128)(2,1)} %slice.722), channel_id=1, source_target_pairs={{0,4},{1,5},{4,8},{5,9},{8,12},{9,13},{12,14},{13,15},{14,10},{15,... | collective-permute-start | bytes 835592 | tf_op jit(solution)/shard_map/ppermute | solution.py:601
  317.1 29.3 %collective-permute-start.41 = (bf16[64,2176]{1,0:T(8,128)(2,1)}, bf16[64,2176]{1,0:T(8,128)(2,1)}, u32[]{:S(2)}, u32[]{:S(2)}) collective-permute-start(bf16[64,2176]{1,0:T(8,128)(2,1)} %slice.723), channel_id=1, source_target_pairs={{4,0},{5,1},{8,4},{9,5},{12,8},{13,9},{14,12},{15,13},{10,14},{11,... | collective-permute-start | bytes 835592 | tf_op jit(solution)/shard_map/ppermute | solution.py:604
  377.3 177.1 %collective-permute-start.96 = (bf16[1024,2048]{1,0:T(8,128)(2,1)}, bf16[1024,2048]{1,0:T(8,128)(2,1)}, u32[]{:S(2)}, u32[]{:S(2)}) collective-permute-start(bf16[1024,2048]{1,0:T(8,128)(2,1)} %convolution_convert_fusion.2), channel_id=1, source_target_pairs={{0,1},{1,0},{2,3},{3,2},{4,5},{5,4},{6,7},{7,6},{8,9},{9,8},{10,11... | collective-permute-start | bytes 12582920 | tf_op jit(solution)/shard_map/ppermute | solution.py:607
  480.4 86.4 %collective-permute-start.94 = (bf16[2048,1024]{1,0:T(8,128)(2,1)}, bf16[2048,1024]{1,0:T(8,128)(2,1)}, u32[]{:S(2)}, u32[]{:S(2)}) collective-permute-start(bf16[2048,1024]{1,0:T(8,128)(2,1)} %convolution_convert_fusion.3), channel_id=1, source_target_pairs={{0,1},{1,0},{2,3},{3,2},{4,5},{5,4},{6,7},{7,6},{8,9},{9,8},{10,11... | collective-permute-start | bytes 12582920 | tf_op jit(solution)/shard_map/ppermute | solution.py:607
  486.3 94.1 %collective-permute-start.92 = (bf16[2048,1024]{1,0:T(8,128)(2,1)}, bf16[2048,1024]{1,0:T(8,128)(2,1)}, u32[]{:S(2)}, u32[]{:S(2)}) collective-permute-start(bf16[2048,1024]{1,0:T(8,128)(2,1)} %convolution_convert_fusion.4), channel_id=1, source_target_pairs={{0,1},{1,0},{2,3},{3,2},{4,5},{5,4},{6,7},{7,6},{8,9},{9,8},{10,11... | collective-permute-start | bytes 12582920 | tf_op jit(solution)/shard_map/ppermute | solution.py:607
  534.7 56.7 %collective-permute-start.88 = (f32[128,2048]{1,0:T(8,128)}, f32[128,2048]{1,0:T(8,128)}, u32[]{:S(2)}, u32[]{:S(2)}) collective-permute-start(f32[128,2048]{1,0:T(8,128)} %slice_select_fusion.1), channel_id=1, source_target_pairs={{0,1},{1,0},{2,3},{3,2},{4,5},{5,4},{6,7},{7,6},{8,9},{9,8},{10,11... | collective-permute-start | bytes 3145736 | tf_op jit(solution)/shard_map/ppermute | solution.py:607
  550.8 126.9 %collective-permute-start.69 = (f32[8,128,384]{2,1,0:T(8,128)}, f32[8,128,384]{2,1,0:T(8,128)}, u32[]{:S(2)}, u32[]{:S(2)}) collective-permute-start(f32[8,128,384]{2,1,0:T(8,128)} %get-tuple-element.152), channel_id=1, source_target_pairs={{0,1},{1,0},{2,3},{3,2},{4,5},{5,4},{6,7},{7,6},{8,9},{9,8},{10,11... | collective-permute-start | bytes 4718600 | tf_op jit(solution)/shard_map/ppermute | solution.py:607
  565.5 223.8 %collective-permute-start.97 = (bf16[512,2048]{1,0:T(8,128)(2,1)}, bf16[512,2048]{1,0:T(8,128)(2,1)}, u32[]{:S(2)}, u32[]{:S(2)}) collective-permute-start(bf16[512,2048]{1,0:T(8,128)(2,1)} %select_convert_fusion), channel_id=1, source_target_pairs={{0,16},{16,0},{1,17},{17,1},{2,18},{18,2},{3,19},{19,3},{4,20},{20... | collective-permute-start | bytes 6291464 | tf_op jit(solution)/shard_map/ppermute | solution.py:610
  579.2 217.6 %collective-permute-start.95 = (bf16[2048,512]{1,0:T(8,128)(2,1)}, bf16[2048,512]{1,0:T(8,128)(2,1)}, u32[]{:S(2)}, u32[]{:S(2)}) collective-permute-start(bf16[2048,512]{1,0:T(8,128)(2,1)} %select_convert_fusion.1), channel_id=1, source_target_pairs={{0,16},{16,0},{1,17},{17,1},{2,18},{18,2},{3,19},{19,3},{4,20},{20... | collective-permute-start | bytes 6291464 | tf_op jit(solution)/shard_map/ppermute | solution.py:610
  593.7 75.5 %collective-permute-start.89 = (bf16[128,2048]{1,0:T(8,128)(2,1)S(1)}, bf16[128,2048]{1,0:T(8,128)(2,1)S(1)}, u32[]{:S(2)}, u32[]{:S(2)}) collective-permute-start(bf16[128,2048]{1,0:T(8,128)(2,1)S(1)} %get-tuple-element.114), channel_id=1, source_target_pairs={{0,16},{16,0},{1,17},{17,1},{2,18},{18,2},{3,19},{19,3},{4,20},{20... | collective-permute-start | bytes 1572872 | tf_op jit(solution)/shard_map/ppermute | solution.py:610
  727.6 74.6 %collective-permute-start.93 = (bf16[2048,512]{1,0:T(8,128)(2,1)}, bf16[2048,512]{1,0:T(8,128)(2,1)}, u32[]{:S(2)}, u32[]{:S(2)}) collective-permute-start(bf16[2048,512]{1,0:T(8,128)(2,1)} %select_convert_fusion.2), channel_id=1, source_target_pairs={{0,16},{16,0},{1,17},{17,1},{2,18},{18,2},{3,19},{19,3},{4,20},{20... | collective-permute-start | bytes 6291464 | tf_op jit(solution)/shard_map/ppermute | solution.py:610
  731.8 88.2 %collective-permute-start.86 = (f32[2048,384]{0,1:T(8,128)}, f32[2048,384]{0,1:T(8,128)S(1)}, u32[]{:S(2)}, u32[]{:S(2)}) collective-permute-start(f32[2048,384]{0,1:T(8,128)} %pad_maximum_fusion.1), channel_id=1, source_target_pairs={{0,1},{1,0},{2,3},{3,2},{4,5},{5,4},{6,7},{7,6},{8,9},{9,8},{10,11... | collective-permute-start | bytes 9437192 | tf_op jit(solution)/shard_map/ppermute | solution.py:607
  733.5 45.5 %collective-permute-start.82 = (f32[20,2048]{1,0:T(8,128)S(1)}, f32[20,2048]{1,0:T(8,128)S(1)}, u32[]{:S(2)}, u32[]{:S(2)}) collective-permute-start(f32[20,2048]{1,0:T(8,128)S(1)} %add.673), channel_id=1, source_target_pairs={{0,16},{16,0},{1,17},{17,1},{2,18},{18,2},{3,19},{19,3},{4,20},{20... | collective-permute-start | bytes 491528 | tf_op jit(solution)/shard_map/ppermute | solution.py:610
  789.3 64.6 %collective-permute-start.47 = (bf16[128,2048]{1,0:T(8,128)(2,1)}, bf16[128,2048]{1,0:T(8,128)(2,1)}, u32[]{:S(2)}, u32[]{:S(2)}) collective-permute-start(bf16[128,2048]{1,0:T(8,128)(2,1)} %get-tuple-element.185), channel_id=1, source_target_pairs={{0,4},{1,5},{4,8},{5,9},{8,12},{9,13},{12,14},{13,15},{14,10},{15,... | collective-permute-start | bytes 1572872 | tf_op jit(solution)/shard_map/ppermute | solution.py:601
  789.4 64.6 %collective-permute-start.51 = (bf16[128,2048]{1,0:T(8,128)(2,1)}, bf16[128,2048]{1,0:T(8,128)(2,1)}, u32[]{:S(2)}, u32[]{:S(2)}) collective-permute-start(bf16[128,2048]{1,0:T(8,128)(2,1)} %get-tuple-element.186), channel_id=1, source_target_pairs={{4,0},{5,1},{8,4},{9,5},{12,8},{13,9},{14,12},{15,13},{10,14},{11,... | collective-permute-start | bytes 1572872 | tf_op jit(solution)/shard_map/ppermute | solution.py:604
  840.4 30.9 %all-to-all-start.2 = ((bf16[16,64,384]{2,1,0:T(8,128)(2,1)}), bf16[16,64,384]{2,1,0:T(8,128)(2,1)}, u32[]{:S(2)}, u32[]{:S(2)}) async-start(bf16[16,64,384]{2,1,0:T(8,128)(2,1)} %bitcast.369), calls=%async_computation.2 | async-start | bytes 1572864 | tf_op jit(solution)/shard_map/all_to_all | solution.py:855
  (170 other events, 2701.0 us)

commit v2 on v1

--- a/solution.py
+++ b/solution.py
@@ -386,12 +386,177 @@
     return [2 * p if p < chips // 2 else 2 * (chips - 1 - p) + 1 for p in range(chips)]
 
 
-def attention_forward(q_ref, k_ref, v_ref, seg_row_ref, seg_col_ref, out_ref, lse_ref, *, block, scale):
-    total = q_ref.shape[0]
-    vt = v_ref[...].astype(F32).T.astype(B16)
+def rows_of(ids_ref, index, rows, core):
+    return pl.ds(pl.multiple_of(ids_ref[1 + index] * (2 * rows) + core * rows, rows), rows)
+
+
+def column(row):
+    return jnp.broadcast_to(row, (row.shape[1], row.shape[1])).T
+
+
+def rows_sum(v):
+    return jnp.sum(v.T, axis=0, keepdims=True)
+
+
+def joined(refs):
+    return jnp.concatenate([r[...] for r in refs], axis=0)
+
+
+def project_kernel(ids_ref, *refs, first):
+    x_refs, (near_own, far_own, near_other, far_other, own_ref, other_ref, square_ref) = refs[:-7], refs[-7:]
+    blocks, rows, wide = own_ref.shape
+    hd = wide // 3
+    x = joined(x_refs)
+    half = x.shape[1] // 2
+    own = dot(x[:, :half], near_own[...]) + dot(x[:, half:], far_own[...])
+    other = dot(x[:, :half], near_other[...]) + dot(x[:, half:], far_other[...])
+    own_ref[...] = own.reshape(own_ref.shape)
+    other_ref[...] = other.reshape(other_ref.shape)
+    square_ref[...] = jnp.zeros_like(square_ref)
+    chips = square_ref.shape[0] // 2
+    for i in range(blocks):
+        at = slice(i * rows, (i + 1) * rows)
+        for j in range(2):
+            cols = slice(j * hd, (j + 1) * hd)
+            total = rows_sum(own[at, cols] * own[at, cols] + other[at, cols] * other[at, cols])
+            square_ref[pl.ds(j * chips + ids_ref[1 + first + i], 1)] = total
+
+
+def turned(v, cosine, sine):
+    return v * cosine + pltpu.roll(v, v.shape[1] // 2, 1) * sine
+
+
+def turned_back(v, cosine, sine):
+    return v * cosine + pltpu.roll(v * sine, v.shape[1] // 2, 1)
+
+
+def head_kernel(ids_ref, *refs, width):
+    raw, (total_ref, cos_ref, sin_ref, gain_ref, own_ref, other_ref) = refs[:4], refs[4:]
+    chips, rows, wide = own_ref.shape
+    hd = wide // 3
+    cut = raw[0].shape[0]
+    for i in range(chips):
+        for h, out in ((0, own_ref), (2, other_ref)):
+            src = raw[h][i] if i < cut else raw[h + 1][i - cut]
+            for j in range(2):
+                scale = column(lax.rsqrt(total_ref[pl.ds(j * chips + ids_ref[1 + i], 1)] / width + EPS))
+                v = src[:, j * hd : (j + 1) * hd] * scale * gain_ref[h + j : h + j + 1]
+                out[i, :, j * hd : (j + 1) * hd] = turned(v, cos_ref[i], sin_ref[i]).astype(B16)
+            out[i, :, 2 * hd :] = src[:, 2 * hd :].astype(B16)
+
+
+def inner_kernel(ids_ref, grad_own, grad_other, *refs, width):
+    raw, (total_ref, cos_ref, sin_ref, gain_ref, inner_ref, out_ref) = refs[:4], refs[4:]
+    chips, rows, wide = grad_own.shape
+    hd = wide // 3
+    cut = raw[0].shape[0]
+    out = [jnp.zeros((rows, hd), F32)] * 4
+    for i in range(chips):
+        for j in range(2):
+            cols = slice(j * hd, (j + 1) * hd)
+            scale = column(lax.rsqrt(total_ref[pl.ds(j * chips + ids_ref[1 + i], 1)] / width + EPS))
+            inner = jnp.zeros((rows, hd), F32)
+            for h, grad in ((0, grad_own), (2, grad_other)):
+                src = (raw[h][i] if i < cut else raw[h + 1][i - cut])[:, cols]
+                v = turned_back(grad[i, :, cols], cos_ref[i], sin_ref[i]) * src
+                inner += v * gain_ref[h + j : h + j + 1]
+                out[h + j] = out[h + j] + v * scale
+            inner_ref[pl.ds(j * chips + ids_ref[1 + i], 1)] = rows_sum(inner)
+    out_ref[...] = jnp.concatenate([jnp.sum(v, axis=0, keepdims=True) for v in out] * 2, axis=0)
+
+
+def finish_kernel(ids_ref, grad_own, grad_other, *refs, width):
+    raw, refs = refs[:4], refs[4:]
+    total_ref, inner_ref, cos_ref, sin_ref, gain_ref, near_own, far_own, near_other, far_other = refs[:9]
+    x_refs, (low_own, low_other, part_ref, sum_ref) = refs[9:-4], refs[-4:]
+    chips, rows, wide = grad_own.shape
+    hd = wide // 3
+    cut = raw[0].shape[0]
+    for i in range(chips):
+        for j in range(3):
+            cols = slice(j * hd, (j + 1) * hd)
+            if j < 2:
+                at = pl.ds(j * chips + ids_ref[1 + i], 1)
+                scale = lax.rsqrt(total_ref[at] / width + EPS)
+                inner = column(scale * scale * scale * (inner_ref[at] / width))
+                scale = column(scale)
+            for h, grad, out in ((0, grad_own, low_own), (2, grad_other, low_other)):
+                v = grad[i, :, cols]
+                if j < 2:
+                    src = (raw[h][i] if i < cut else raw[h + 1][i - cut])[:, cols]
+                    v = turned_back(v, cos_ref[i], sin_ref[i])
+                    v = scale * (v * gain_ref[h + j : h + j + 1]) - src * inner
+                out[i, :, cols] = v.astype(B16)
+    x = joined(x_refs)
+    half = width // 2
+    group = min(4, chips)
+    for lo in range(0, chips, group):
+        own = low_own[lo : lo + group].reshape(group * rows, wide)
+        other = low_other[lo : lo + group].reshape(group * rows, wide)
+        for first, w_own, w_other in ((0, near_own, near_other), (half, far_own, far_other)):
+            part = dot(own, w_own[...], NT) + dot(other, w_other[...], NT)
+            part_ref[lo : lo + group, :, first : first + half] = part.astype(B16).reshape(group, rows, half)
+            seen = x[lo * rows : (lo + group) * rows, first : first + half].astype(F32)
+            term = jnp.sum((part * seen).reshape(group * rows // 8, 8, half), axis=0)
+            if lo == 0:
+                sum_ref[:, first : first + half] = term
+            else:
+                sum_ref[:, first : first + half] += term
+
+
+def outer_kernel(*refs, count):
+    left, x_refs, outs, x_all = refs[:count], refs[count : -count - 1], refs[-count - 1 : -1], refs[-1]
+    x_all[...] = joined(x_refs)
+    width = x_all.shape[1]
+    tile = min(512, width)
+    for l_ref, out in zip(left, outs):
+        chips, rows, wide = l_ref.shape
+        turn = l_ref[...].reshape(chips * rows, wide).astype(F32).T.astype(B16)
+        for lo in range(0, width, tile):
+            out[:, lo : lo + tile] = dot(turn, x_all[:, lo : lo + tile]).astype(out.dtype)
+
+
+def head_grad_kernel(*refs):
+    x_refs, (w_ref, own_ref, other_ref) = refs[:-3], refs[-3:]
+    hd = own_ref.shape[2]
+    grad = dot(joined(x_refs), w_ref[...], NT).astype(B16)
+    own_ref[...] = grad[:, :hd].reshape(own_ref.shape)
+    other_ref[...] = grad[:, hd:].reshape(other_ref.shape)
+
+
+def on_core(kernel, shapes, operands, flops, scratch=(), light=False):
+    scalars = operands[0].dtype == jnp.int32
+    memory = [pltpu.SMEM if scalars and i == 0 else pltpu.VMEM for i in range(len(operands))]
+    size = sum(v.size * v.dtype.itemsize for v in list(operands) + list(shapes))
+    return pl.pallas_call(
+        kernel,
+        in_specs=[pl.BlockSpec(memory_space=m) for m in memory],
+        out_shape=shapes,
+        scratch_shapes=scratch,
+        compiler_params=pltpu.CompilerParams(vmem_limit_bytes=56 * 2**20),
+        cost_estimate=pl.CostEstimate(flops=0 if light else flops, bytes_accessed=0 if light else size, transcendentals=0),
+    )(*operands)
+
+
+def seg_column(row_ref, col_ref, rows):
+    for lo in range(0, row_ref.shape[1], rows):
+        col_ref[lo : lo + rows] = jnp.concatenate([column(row_ref[:, lo : lo + rows])] * (col_ref.shape[1] // rows), axis=1)
+
+
+def attention_forward(
+    ids_ref, mine_ref, other_ref, seg_row_ref, out_ref, lse_ref, qkv_ref, low_ref, away_ref, seg_col_ref, *, block, scale
+):
+    chips, rows, hd = mine_ref.shape[0], mine_ref.shape[1], mine_ref.shape[2] // 3
+    core = ids_ref[0]
+    for i in range(chips):
+        qkv_ref[rows_of(ids_ref, i, rows, core)] = mine_ref[i]
+        qkv_ref[rows_of(ids_ref, i, rows, 1 - core)] = other_ref[i]
+    total = qkv_ref.shape[0]
+    seg_column(seg_row_ref, seg_col_ref, rows)
+    vt = qkv_ref[:, 2 * hd :].astype(F32).T.astype(B16)
     for index in range(total // block):
         low, high = index * block, (index + 1) * block
-        score = dot(k_ref[:high], q_ref[low:high], NT) * scale
+        score = dot(qkv_ref[:high, hd : 2 * hd], qkv_ref[low:high, :hd], NT) * scale
         key = lax.broadcasted_iota(jnp.int32, (high, block), 0)
         query = low + lax.broadcasted_iota(jnp.int32, (high, block), 1)
         seen = (key <= query) & (seg_col_ref[:high] == seg_row_ref[:, low:high])
@@ -402,29 +567,43 @@
         out = dot(vt[:, :high], prob.astype(B16)) / norm
         out_ref[low:high] = out.T
         lse_ref[:, low:high] = best + jnp.log(norm)
+    for i in range(chips):
+        low_ref[i] = out_ref[rows_of(ids_ref, i, rows, core)].astype(B16)
+        away_ref[i] = out_ref[rows_of(ids_ref, i, rows, 1 - core)].astype(B16)
 
 
 def attention_backward(
-    q_ref, k_ref, v_ref, g_ref, out_ref, lse_ref, seg_row_ref, seg_col_ref, dq_ref, dk_ref, dv_ref, *, block, scale
+    ids_ref, qkv_ref, *refs, block, scale
 ):
-    total = q_ref.shape[0]
-    kt = k_ref[...].astype(F32).T.astype(B16)
-    dk_ref[...] = jnp.zeros_like(dk_ref)
-    dv_ref[...] = jnp.zeros_like(dv_ref)
+    out_ref, lse_ref, seg_row_ref, low_ref, away_ref, g_ref, grad_ref, seg_col_ref = refs[4:]
+    chips, rows, wide = low_ref.shape
+    hd = wide // 3
+    core = ids_ref[0]
+    cut = refs[0].shape[0]
+    for i in range(chips):
+        g_ref[rows_of(ids_ref, i, rows, core)] = refs[0][i] if i < cut else refs[1][i - cut]
+        g_ref[rows_of(ids_ref, i, rows, 1 - core)] = refs[2][i] if i < cut else refs[3][i - cut]
+    total = qkv_ref.shape[0]
+    seg_column(seg_row_ref, seg_col_ref, rows)
+    kt = qkv_ref[:, hd : 2 * hd].astype(F32).T.astype(B16)
+    grad_ref[...] = jnp.zeros_like(grad_ref)
     for index in range(total // block):
         low, high = index * block, (index + 1) * block
-        q, g = q_ref[low:high], g_ref[low:high]
+        q, g = qkv_ref[low:high, :hd], g_ref[low:high]
         delta = jnp.sum((g.astype(F32) * out_ref[low:high]).T, axis=0, keepdims=True)
-        score = dot(k_ref[:high], q, NT) * scale
+        score = dot(qkv_ref[:high, hd : 2 * hd], q, NT) * scale
         key = lax.broadcasted_iota(jnp.int32, (high, block), 0)
         query = low + lax.broadcasted_iota(jnp.int32, (high, block), 1)
         seen = (key <= query) & (seg_col_ref[:high] == seg_row_ref[:, low:high])
         prob = jnp.where(seen, jnp.exp(score - lse_ref[:, low:high]), 0.0)
-        dprob = dot(v_ref[:high], g, NT)
+        dprob = dot(qkv_ref[:high, 2 * hd :], g, NT)
         dscore = (prob * (dprob - delta)).astype(B16)
-        dk_ref[:high] += dot(dscore, q) * scale
-        dv_ref[:high] += dot(prob.astype(B16), g)
-        dq_ref[low:high] = dot(kt[:, :high], dscore).T * scale
+        grad_ref[:high, hd : 2 * hd] += dot(dscore, q) * scale
+        grad_ref[:high, 2 * hd :] += dot(prob.astype(B16), g)
+        grad_ref[low:high, :hd] = dot(kt[:, :high], dscore).T * scale
+    for i in range(chips):
+        low_ref[i] = grad_ref[rows_of(ids_ref, i, rows, core)]
+        away_ref[i] = grad_ref[rows_of(ids_ref, i, rows, 1 - core)]
 
 
 def expert_kernel(ids_ref, *refs, shards, fresh):
@@ -557,6 +736,35 @@
     return out[0], out[1], out[2], out[3:]
 
 
+def expert_grad_kernel(left_ref, right_ref, *refs):
+    term = dot(left_ref[...], right_ref[...], TN)
+    if len(refs) == 2:
+        term += refs[0][...].astype(F32)
+    refs[-1][...] = term.astype(B16)
+
+
+def expert_grad_term(left, right, arrived, left_at, right_at, size, across):
+    rows = left.shape[0]
+    tile = min(512, size)
+    high, wide = (size, right.shape[1]) if across else (left.shape[1], size)
+    first = left_at // tile
+    in_specs = [
+        pl.BlockSpec((rows, tile), lambda j: (0, first + j)),
+        pl.BlockSpec((rows, wide), lambda j: (0, right_at // size)),
+    ]
+    block = pl.BlockSpec((tile, wide), lambda j: (j, 0))
+    operands = [left, right] + ([] if arrived is None else [arrived])
+    return pl.pallas_call(
+        expert_grad_kernel,
+        grid=(high // tile,),
+        in_specs=in_specs + [block] * (len(operands) - 2),
+        out_specs=block,
+        out_shape=jax.ShapeDtypeStruct((high, wide), B16),
+        compiler_params=pltpu.CompilerParams(vmem_limit_bytes=56 * 2**20),
+        cost_estimate=pl.CostEstimate(flops=0, bytes_accessed=0, transcendentals=0),
+    )(*operands)
+
+
 def split_three(v):
     high = lax.reduce_precision(v, exponent_bits=8, mantissa_bits=7)
     middle = lax.reduce_precision(v - high, exponent_bits=8, mantissa_bits=7)
@@ -615,35 +823,65 @@
 
     offsets = [0] + [s * o for o in range(1, half) for s in (1, -1)] + [half]
 
-    def ring_gather(v):
-        cut = v.shape[0] // 2
+    def after(v, *others):
+        return lax.optimization_barrier((v,) + others)[0]
+
+    places = jnp.stack([chip_at(o) for o in offsets])
+
+    def ring_gather(v, ties=(), first=None):
+        ties = list(ties) + [()] * half
+        cut = v.shape[0] // 32 * 16
         got = {0: v}
+
+        def send(i, one, two):
+            if i == 0 and first:
+                return first
+            one, two = lax.optimization_barrier((one, two) + tuple(ties[i]))[:2]
+            return to_right(one), to_left(two)
+
         for o in range(1, half):
-            got[-o] = to_right(got[-(o - 1)])
-            got[o] = to_left(got[o - 1])
-        first = to_right(got[-(half - 1)][:cut])
-        second = to_left(got[half - 1][cut:])
+            got[-o], got[o] = send(o - 1, got[-(o - 1)], got[o - 1])
+        first, second = send(half - 1, got[-(half - 1)][:cut], got[half - 1][cut:])
         got[half] = jnp.concatenate([first, second], axis=0)
+        got["halves"] = (first, second)
         return got
 
-    def in_place(got):
-        out = jnp.zeros((chips,) + got[0].shape, got[0].dtype)
-        for o in offsets:
-            out = lax.dynamic_update_index_in_dim(out, got[o], chip_at(o), 0)
-        return out
-
-    def ring_sum(part):
+    def in_ring(got):
+        return jnp.concatenate([got[o] for o in offsets], axis=0)
+
+    def ring_steps(part, axis):
         far = part(half)
-        cut = far.shape[1] // 2
-        there = to_right(far[:, :cut])
-        back = to_left(far[:, cut:])
+        cut = far.shape[axis] // 2
+        a_cut = lambda v: lax.slice_in_dim(v, 0, cut, axis=axis)
+        b_cut = lambda v: lax.slice_in_dim(v, cut, v.shape[axis], axis=axis)
+        there, back = lax.optimization_barrier((a_cut(far), b_cut(far)))
+        there, back = yield to_right(there), to_left(back)
         near, other = part(half - 1), part(1 - half)
-        there = jnp.concatenate([near[:, :cut] + there, near[:, cut:]], axis=1)
-        back = jnp.concatenate([other[:, :cut], other[:, cut:] + back], axis=1)
+        there = jnp.concatenate([a_cut(near) + there, b_cut(near)], axis=axis)
+        back = jnp.concatenate([a_cut(other), b_cut(other) + back], axis=axis)
         for o in range(half - 2, 0, -1):
-            there = to_right(there) + part(o)
-            back = to_left(back) + part(-o)
-        return to_right(there).astype(F32) + to_left(back).astype(F32) + part(0).astype(F32)
+            there, back = lax.optimization_barrier((there, back))
+            there, back = yield to_right(there), to_left(back)
+            there, back = there + part(o), back + part(-o)
+        there, back = lax.optimization_barrier((there, back))
+        there, back = yield to_right(there), to_left(back)
+        return there.astype(F32) + back.astype(F32) + part(0).astype(F32)
+
+    def tied(values, *others):
+        return lax.optimization_barrier(tuple(values) + others)[: len(values)]
+
+    def ring_sum(part, axis, work=()):
+        work = list(work) + [()] * half
+        ring = ring_steps(part, axis)
+        values, token = next(ring), None
+        for i in range(half):
+            extra = work[i](token) if callable(work[i]) else work[i]
+            values = tied(values, *extra)
+            token = values[0]
+            try:
+                values = ring.send(values)
+            except StopIteration as end:
+                return end.value
 
     def sum_chips(v):
         step = 2
@@ -652,121 +890,120 @@
             step *= 2
         return v
 
-    def sum_all(v):
-        v = v + core_swap(v)
-        return sum_chips(v + group_swap(v))
-
     def by_core(mine, other, axis):
         return jnp.where(core == 0, jnp.stack([mine, other], axis), jnp.stack([other, mine], axis))
 
     def pick(pair, which):
         return jnp.where(which == 0, pair[0], pair[1])
 
-    wg = jnp.concatenate([expert_gate, core_swap(expert_gate)], axis=0)
-    wu = jnp.concatenate([expert_up, core_swap(expert_up)], axis=0)
-    wd = jnp.concatenate([expert_down, core_swap(expert_down)], axis=0)
+    def by_parity(v, axis, back=False):
+        shape = v.shape
+        v = v.reshape(shape[:axis] + ((2, chips, rows) if back else (chips, 2, rows)) + shape[axis + 1 :])
+        split = axis if back else axis + 1
+        one, two = [lax.index_in_dim(v, i, split, keepdims=False) for i in range(2)]
+        one, two = jnp.where(core == 0, one, two), jnp.where(core == 0, two, one)
+        return jnp.stack([one, two], axis + 1 if back else axis).reshape(shape)
+
+    wg_pair, wu_pair, wd_pair = [(w, core_swap(w)) for w in (expert_gate, expert_up, expert_down)]
 
     inputs = tokens.astype(F32)
-    n1 = norm_rows(inputs, norm_attn).astype(B16)
-    lane = lax.broadcasted_iota(jnp.int32, (rows, LANES), 1)
-    flags = jnp.where(lane == 0, doc_starts[:, None], 0).astype(B16)
-    n1_got = ring_gather(jnp.concatenate([n1, flags], axis=1))
+    n1 = by_parity(norm_rows(inputs, norm_attn).astype(B16), 1)
 
     slabs = []
     for w in (w_query, w_key, w_value):
         pair = w.reshape(rows, chips, 2, hd)
         slabs.append(jnp.where(group == 0, pair[:, :, 0], pair[:, :, 1]))
     slab = jnp.concatenate(slabs, axis=2).transpose(1, 0, 2)
-    own = lax.all_to_all(slab, "ctx", split_axis=0, concat_axis=0, axis_index_groups=same_core, tiled=True)
-    other = group_swap(own)
-    low_head, high_head = jnp.where(group == 0, own, other), jnp.where(group == 0, other, own)
-    columns = []
-    for i in range(3):
-        columns += [low_head[:, :, i * hd : (i + 1) * hd], high_head[:, :, i * hd : (i + 1) * hd]]
-    columns = jnp.concatenate(columns, axis=2)
-    wide = 6 * hd
-    w_in = by_core(columns, core_swap(columns), 1).reshape(width, wide)
-    w_out = by_core(w_output, core_swap(w_output), 0).reshape(2 * hd, width)
-
-    flags = in_place({o: v[:, width].astype(F32) for o, v in n1_got.items()})
-    n1_all = in_place({o: v[:, :width] for o, v in n1_got.items()}).reshape(chips * rows, width)
+    first = (to_right(n1), to_left(n1))
+    slab = after(slab, *first)
+    near_head = lax.all_to_all(slab, "ctx", split_axis=0, concat_axis=0, axis_index_groups=same_core, tiled=True)
+    far_head = group_swap(near_head)
+    n1_got = {0: n1, -1: first[0], 1: first[1]}
+    for o in range(2, half):
+        one, two = lax.optimization_barrier((n1_got[1 - o], n1_got[o - 1]) + ((near_head,) if o == 2 else ()))[:2]
+        n1_got[-o], n1_got[o] = to_right(one), to_left(two)
+    own = jnp.where(core == group, near_head, far_head)
+    other = jnp.where(core == group, far_head, near_head)
+    w_in = [v.reshape(chips * rows, 3 * hd) for v in (own, core_swap(other), other, core_swap(own))]
+    w_out = jnp.concatenate([w_output, core_swap(w_output)], axis=0)
+
     count = chips * rows
-    qkv = dot(n1_all, w_in)
-    qp, kp, vp = qkv[:, : 2 * hd], qkv[:, 2 * hd : 4 * hd], qkv[:, 4 * hd :]
-    squares = jnp.stack([jnp.sum(qp * qp, axis=1), jnp.sum(kp * kp, axis=1)])
-    squares = sum_chips(squares.reshape(2 * chips, rows)).reshape(2, count, 1)
-    q_scale = lax.rsqrt(squares[0] / width + EPS)
-    k_scale = lax.rsqrt(squares[1] / width + EPS)
-    gain_q = lax.dynamic_slice(norm_query, (chip * 2 * hd,), (2 * hd,))
-    gain_k = lax.dynamic_slice(norm_key, (chip * 2 * hd,), (2 * hd,))
-
-    place = (2 * lax.broadcasted_iota(jnp.int32, (chips, rows, 1), 0) + core) * rows
-    place = place + lax.broadcasted_iota(jnp.int32, (chips, rows, 1), 1)
+    place = (2 * places[:, None, None] + core) * rows + lax.broadcasted_iota(jnp.int32, (chips, rows, 1), 1)
     freq = THETA ** (-jnp.arange(hd // 2, dtype=F32) * 2.0 / hd)
-    angle = place.reshape(count, 1).astype(F32) * freq[None, :]
+    angle = place.astype(F32) * freq[None, None, :]
     cosine, sine = jnp.cos(angle), jnp.sin(angle)
-    cosine = jnp.concatenate([cosine] * 4, axis=1)
-    sine = jnp.concatenate([-sine, sine] * 2, axis=1)
-
-    def halves(v):
-        h = hd // 2
-        return jnp.concatenate([v[:, h:hd], v[:, :h], v[:, hd + h :], v[:, hd : hd + h]], axis=1)
-
-    def turn(v):
-        return v * cosine + halves(v) * sine
-
-    def turn_back(v):
-        return v * cosine + halves(v * sine)
-
-    query = turn(qp * q_scale * gain_q).astype(B16)
-    keys = turn(kp * k_scale * gain_k).astype(B16)
-    values = vp.astype(B16)
-
-    def to_heads(parts):
-        pairs = [(v[:, :hd], v[:, hd:]) for v in parts]
-        mine = jnp.concatenate([pick(p, core) for p in pairs], axis=1)
-        away = jnp.concatenate([pick(p, 1 - core) for p in pairs], axis=1)
-        shape = (chips, rows, mine.shape[1])
-        return by_core(mine.reshape(shape), core_swap(away).reshape(shape), 1).reshape(devices * rows, -1)
-
-    def to_tokens(v):
-        v = v.reshape(chips, 2, rows, -1)
-        mine, away = pick((v[:, 0], v[:, 1]), core), pick((v[:, 0], v[:, 1]), 1 - core)
-        mine, other = mine.reshape(count, -1), core_swap(away).reshape(count, -1)
-        low_head, high_head = pick((mine, other), core), pick((other, mine), core)
-        parts = []
-        for i in range(mine.shape[1] // hd):
-            parts.append(
-                jnp.concatenate([low_head[:, i * hd : (i + 1) * hd], high_head[:, i * hd : (i + 1) * hd]], axis=1)
-            )
-        return parts
-
-    heads = to_heads([query, keys, values])
-    qh, kh, vh = heads[:, :hd], heads[:, hd : 2 * hd], heads[:, 2 * hd :]
+    cosine = jnp.concatenate([cosine] * 2, axis=2)
+    sine = jnp.concatenate([-sine, sine], axis=2)
+    ids = jnp.concatenate([core[None], places]).astype(jnp.int32)
+    ranks = (rank, rank ^ 1)
+    gains = jnp.stack([lax.dynamic_slice(g, (r * hd,), (hd,)) for r in ranks for g in (norm_query, norm_key)])
+    gains = jnp.concatenate([gains, gains], axis=0)
+    early, late = offsets[:5], offsets[5:]
+    raw, squares = [None] * 4, [None] * 2
+
+    def project(i, shards):
+        blocks = (early, late)[i]
+        raw[i], raw[i + 2], squares[i] = on_core(
+            functools.partial(project_kernel, first=i * len(early)),
+            [jax.ShapeDtypeStruct((len(blocks), rows, 3 * hd), F32)] * 2
+            + [jax.ShapeDtypeStruct((2 * chips, rows), F32)],
+            [ids] + shards + w_in,
+            12 * len(blocks) * rows * width * hd,
+            light=i == 0,
+        )
+
+    project(0, [n1_got[o] for o in early])
+    one, two = lax.optimization_barrier((n1_got[1 - half], n1_got[half - 1], squares[0]))[:2]
+    cut = rows // 2
+    n1_halves = (to_right(one[:cut]), to_left(two[cut:]))
+    project(1, [n1_got[o] for o in late if o != half] + list(n1_halves))
+    squares = squares[0] + squares[1]
+    top = after(out_grad, *n1_halves)
+    top_first = (to_right(top), to_left(top))
+    flags = lax.dynamic_update_index_in_dim(jnp.zeros((chips, rows), F32), doc_starts.astype(F32), chip, 0)
+    total = sum_chips(after(jnp.concatenate([squares, flags], axis=0), *top_first))
+    one, two = lax.optimization_barrier(top_first + (total,))[:2]
+    top_got = {0: out_grad, -1: top_first[0], 1: top_first[1], -2: to_right(one), 2: to_left(two)}
+    heads = on_core(
+        functools.partial(head_kernel, width=width),
+        [jax.ShapeDtypeStruct((chips, rows, 3 * hd), B16)] * 2,
+        [ids] + raw + [total, cosine, sine, gains],
+        0,
+    )
+
+    flags = total[2 * chips :]
     flags = by_core(flags, core_swap(flags), 1).reshape(devices, rows)
     tri = (lax.broadcasted_iota(jnp.int32, (rows, rows), 0) <= lax.broadcasted_iota(jnp.int32, (rows, rows), 1)).astype(F32)
     before = (
         lax.broadcasted_iota(jnp.int32, (devices, devices), 1) < lax.broadcasted_iota(jnp.int32, (devices, devices), 0)
     ).astype(F32)
     seg = jnp.dot(flags, tri) + jnp.dot(before, jnp.broadcast_to(jnp.sum(flags, axis=1, keepdims=True), (devices, rows)))
-    seg_row, seg_col = seg.reshape(1, devices * rows), seg.reshape(devices * rows, 1)
     everything = devices * rows
+    seg_row = seg.reshape(1, everything)
     block = min(256, everything)
-    params = pltpu.CompilerParams(vmem_limit_bytes=56 * 2**20)
-    attn, lse = pl.pallas_call(
+    half_wide = everything * everything // 2
+    attn, lse, head_qkv, low_own, low_away = on_core(
         functools.partial(attention_forward, block=block, scale=scale),
-        out_shape=[
+        [
             jax.ShapeDtypeStruct((everything, hd), F32),
             jax.ShapeDtypeStruct((1, everything), F32),
+            jax.ShapeDtypeStruct((everything, 3 * hd), B16),
+            jax.ShapeDtypeStruct((chips, rows, hd), B16),
+            jax.ShapeDtypeStruct((chips, rows, hd), B16),
         ],
-        compiler_params=params,
-        cost_estimate=pl.CostEstimate(
-            flops=2 * everything * everything * hd, bytes_accessed=8 * everything * hd, transcendentals=everything * everything // 2
-        ),
-    )(qh, kh, vh, seg_row, seg_col)
-    (attn_low,) = to_tokens(attn.astype(B16))
+        [ids, heads[0], core_swap(heads[1]), seg_row],
+        8 * half_wide * hd,
+        [pltpu.VMEM((everything, block), F32)],
+    )
+    low_other = after(core_swap(low_away), top_got[2], top_got[-2])
+    attn_low = jnp.concatenate([low_own, low_other], axis=2).reshape(count, 2 * hd)
     out_part = dot(attn_low, w_out).astype(B16).reshape(chips, rows, width)
-    h1 = inputs + ring_sum(lambda o: lax.dynamic_index_in_dim(out_part, chip_at(o), 0, keepdims=False))
+    weights = [jnp.concatenate(pair, axis=0) for pair in (wg_pair, wu_pair, wd_pair)]
+    h1 = inputs + ring_sum(
+        lambda o: out_part[offsets.index(o)],
+        1,
+        [(), (weights[0],), (weights[1],), (weights[2],)],
+    )
 
     n2 = norm_rows(h1, norm_ffn).astype(B16)
     probs = jax.nn.softmax(dot(n2, router), axis=-1)
@@ -775,25 +1012,71 @@
     )
     sent = split_three(probs * chosen)
     sent.append(jnp.zeros((rows, LANES - 3 * experts), B16))
-    top_got = ring_gather(out_grad)
-    n2_got = ring_gather(jnp.concatenate([n2] + sent, axis=1))
-    ids = jnp.stack([rank, rank ^ 1, jnp.int32(experts)]).astype(jnp.int32)
-    moe_part, dn2_part, dgate_part = {}, {}, {}
+    names = jnp.stack([rank, rank ^ 1, jnp.int32(experts)]).astype(jnp.int32)
+    moe_part, dn2_part, dgate_part = {}, {}, []
     kept = None
-    chunks = [([0], 0)] + [([o, -o], o) for o in range(1, half)] + [([half], 1)]
-    for which, spot in chunks:
-        moe, dn2, dgate, kept = expert_rows(
-            ids, [n2_got[o] for o in which], [top_got[o] for o in which], wg, wu, wd, kept, spot, chips
+
+    def run_experts(which, spot):
+        moe, dn2, dgate, kept_now = expert_rows(
+            names, [n2_got[o] for o in which], [top_got[o] for o in which], *weights, kept, spot, chips
         )
         for i, o in enumerate(which):
-            moe_part[o], dn2_part[o], dgate_part[o] = moe[i], dn2[i], dgate[i]
-    act_all, dgate_pre_all, dup_pre_all, x_all, top_all = [v.reshape(count, -1) for v in kept]
-    n2_sum = ring_sum(lambda o: dn2_part[o])
-
-    dgates = jnp.stack([dgate_part[o][:, :2] for o in offsets])
-    there = jnp.stack([chip_at(o) for o in offsets])
-    spread_out = (there[None, :] == jnp.arange(chips)[:, None]).astype(F32)
-    dgates = jnp.dot(spread_out, dgates.transpose(0, 2, 1).reshape(chips, 2 * rows), precision=HIGH)
+            moe_part[o], dn2_part[o] = moe[i], dn2[i]
+        dgate_part.append(dgate)
+        return kept_now
+
+    n2_got = {0: jnp.concatenate([n2] + sent, axis=1)}
+    n2_got[-1], n2_got[1] = to_right(n2_got[0]), to_left(n2_got[0])
+    one, two, three, four = lax.optimization_barrier((n2_got[-1], n2_got[1], top_got[-2], top_got[2]))
+    n2_got[-2], n2_got[2] = to_right(one), to_left(two)
+    top_got[-3], top_got[3] = to_right(three), to_left(four)
+    kept = run_experts([0, 1, -1], 0)
+    one, two, three, four = lax.optimization_barrier((n2_got[-2], n2_got[2], top_got[-3], top_got[3], kept[0]))[:4]
+    n2_got[-3], n2_got[3] = to_right(one), to_left(two)
+    top_got[half] = jnp.concatenate([to_right(three[:cut]), to_left(four[cut:])], axis=0)
+    kept = run_experts([2, -2], 3)
+    one, two = lax.optimization_barrier((n2_got[-3], n2_got[3], kept[0]))[:2]
+    n2_got[half] = jnp.concatenate([to_right(one[:cut]), to_left(two[cut:])], axis=0)
+    kept = run_experts([3, -3, half], 1)
+    kept = [v.reshape(count, -1) for v in kept]
+    act_all, dgate_pre_all, dup_pre_all, x_all, top_all = kept
+
+    hidden = expert_gate.shape[2]
+    pairs = [(act_all, top_all), (x_all, dgate_pre_all), (x_all, dup_pre_all)]
+
+    def expert_term(i, expert, token, plus):
+        left_side, right_side = pairs[i]
+        across = i == 0
+        at = expert * hidden
+        return expert_grad_term(
+            after(left_side, token), right_side, plus, at if across else 0, 0 if across else at, hidden, across
+        )
+
+    arrived, expert_grads, own_terms = [], [], []
+
+    def own_term(i):
+        def run(token):
+            own_terms.append(expert_term(i, 0, token, arrived[i]))
+            expert_grads.append(
+                lax.psum_scatter(own_terms[i], "dp", scatter_dimension=0 if i == 0 else 1, tiled=True)
+            )
+            return own_terms[-1:]
+
+        return run
+
+    def other_term(i):
+        def run(token):
+            other = expert_term(i, 1, token, None)
+            arrived.append(core_swap(other))
+            return (other,)
+
+        return run
+
+    n2_sum = ring_sum(lambda o: dn2_part[o], 1, [(), other_term(0), own_term(0), other_term(1)])
+
+    dgates = jnp.concatenate(dgate_part, axis=0)[:, :, :2].transpose(0, 2, 1)
+    spread_out = (places[None, :] == jnp.arange(chips)[:, None]).astype(F32)
+    dgates = jnp.dot(spread_out, dgates.reshape(chips, 2 * rows), precision=HIGH)
     dgates = dgates.reshape(chips, 2, rows)
     dgates = jnp.where(core == 0, dgates, dgates[:, ::-1])
     dgates = lax.all_to_all(dgates, "ctx", split_axis=0, concat_axis=0, axis_index_groups=same_core, tiled=True)
@@ -807,100 +1090,175 @@
     h1_grad = grad_top + h1_part
     h1_low = h1_grad.astype(B16)
 
-    h1_all = in_place(ring_gather(h1_low)).reshape(count, width)
-    attn_grad = dot(h1_all, w_out, NT).astype(B16)
-    gh = to_heads([attn_grad])
-    dq, dk, dv = pl.pallas_call(
+    grad_parts = [None] * 4
+
+    def head_grad(i, shards):
+        blocks = (early, late)[i]
+        grad_parts[i], away = on_core(
+            head_grad_kernel,
+            [jax.ShapeDtypeStruct((len(blocks), rows, hd), B16)] * 2,
+            shards + [w_out],
+            4 * len(blocks) * rows * width * hd,
+        )
+        grad_parts[i + 2] = core_swap(away)
+        return away
+
+    h1_got = {0: h1_low, -1: to_right(h1_low), 1: to_left(h1_low)}
+
+    def add_step(v, step, token):
+        v = after(v, token)
+        return v + lax.ppermute(v, "ctx", [(i, i ^ step) for i in range(devices)])
+
+    early_sum = jnp.concatenate([router_term, ffn_gain_grad[None]], axis=0)
+    early_sum = early_sum + core_swap(early_sum)
+    one, two = tied((h1_got[-1], h1_got[1]), early_sum)
+    work = ()
+    for o in range(2, half):
+        one, two = tied((h1_got[1 - o], h1_got[o - 1]), early_sum, *work)
+        h1_got[-o], h1_got[o] = to_right(one), to_left(two)
+        early_sum = add_step(early_sum, 2 ** (o - 1), one)
+        work = (own_term(1) if o == 2 else other_term(2))(one)
+    away = head_grad(0, [h1_got[o] for o in early])
+    one, two = tied((h1_got[1 - half], h1_got[half - 1]), early_sum, away, *work)
+    cut = rows // 2
+    h1_halves = (to_right(one[:cut]), to_left(two[cut:]))
+    early_sum = add_step(early_sum, 2 ** (half - 1), one)
+    head_grad(1, [h1_got[o] for o in late if o != half] + list(h1_halves))
+    moe_ring = ring_steps(lambda o: after(moe_part[o], grad_parts[1]) if o == half else moe_part[o], 1)
+    moe_got = next(moe_ring)
+    grads_own, grads_away = on_core(
         functools.partial(attention_backward, block=block, scale=scale),
-        out_shape=[jax.ShapeDtypeStruct((everything, hd), F32)] * 3,
-        compiler_params=params,
-        cost_estimate=pl.CostEstimate(
-            flops=5 * everything * everything * hd, bytes_accessed=24 * everything * hd, transcendentals=everything * everything // 2
-        ),
-    )(qh, kh, vh, gh, attn, lse, seg_row, seg_col)
-    query_grad, key_grad, value_grad = to_tokens(jnp.concatenate([dq, dk, dv], axis=1))
-    query_grad, key_grad = turn_back(query_grad), turn_back(key_grad)
-    inner = jnp.stack(
-        [jnp.sum(query_grad * gain_q * qp, axis=1), jnp.sum(key_grad * gain_k * kp, axis=1)]
-    )
-    inner = sum_chips(inner.reshape(2 * chips, rows)).reshape(2, count, 1)
-    qp_grad = q_scale * (query_grad * gain_q) - qp * (q_scale * q_scale * q_scale * (inner[0] / width))
-    kp_grad = k_scale * (key_grad * gain_k) - kp * (k_scale * k_scale * k_scale * (inner[1] / width))
-    query_gain = jnp.sum(query_grad * qp * q_scale, axis=0)
-    key_gain = jnp.sum(key_grad * kp * k_scale, axis=0)
-    qkv_low = jnp.concatenate([qp_grad.astype(B16), kp_grad.astype(B16), value_grad.astype(B16)], axis=1)
-    n1_part = dot(qkv_low, w_in, NT).astype(B16).reshape(chips, rows, width)
-    n1_grad = ring_sum(lambda o: lax.dynamic_index_in_dim(n1_part, chip_at(o), 0, keepdims=False))
-    unused_norm, attn_back = jax.vjp(lambda v: norm_rows(v, norm_attn), inputs)
-    (input_part,) = attn_back(n1_grad)
-    tokens_grad = (h1_grad + input_part).astype(B16)
-
-    block_out = (h1 + ring_sum(lambda o: moe_part[o])).astype(B16)
-
-    w_part = dot(n1_all, qkv_low, TN)
-    attn_gain = jnp.sum(w_part * w_in.astype(F32), axis=1) / norm_attn
-
-    def own_head(v, axis):
-        pairs = [lax.slice_in_dim(v, i * hd, (i + 1) * hd, axis=axis) for i in range(v.shape[axis] // hd)]
-        pairs = [(pairs[i], pairs[i + 1]) for i in range(0, len(pairs), 2)]
-        mine = jnp.concatenate([pick(p, core) for p in pairs], axis=axis)
-        away = jnp.concatenate([pick(p, 1 - core) for p in pairs], axis=axis)
-        return mine + core_swap(away)
-
-    w_head = own_head(w_part, 1).reshape(2, width // 2, 3 * hd)
-    w_mine = pick((w_head[0], w_head[1]), group) + group_swap(
-        pick((w_head[0], w_head[1]), 1 - group).astype(B16)
-    ).astype(F32)
-    w_mine = w_mine.astype(B16).reshape(devices, -1, 3 * hd)
-    w_mine = lax.all_to_all(w_mine, "ctx", split_axis=0, concat_axis=0, tiled=True)
-    w_mine = w_mine.transpose(1, 0, 2).astype(F32)
-    slab_rows = w_mine.shape[0]
-    wq_grad, wk_grad, wv_grad = [
-        w_mine[:, :, i * hd : (i + 1) * hd].reshape(slab_rows, width) for i in range(3)
-    ]
-    o_head = own_head(dot(attn_low, h1_all, TN), 0)
-    o_head = (o_head + group_swap(o_head.astype(B16)).astype(F32)).astype(B16)
+        [jax.ShapeDtypeStruct((chips, rows, 3 * hd), F32)] * 2,
+        [ids, head_qkv] + grad_parts + [attn, lse, seg_row],
+        20 * half_wide * hd,
+        [
+            pltpu.VMEM((everything, hd), B16),
+            pltpu.VMEM((everything, 3 * hd), F32),
+            pltpu.VMEM((everything, block), F32),
+        ],
+    )
+    h1_shards = [h1_got[o] for o in offsets if o != half] + list(h1_halves)
+    o_own, o_away = on_core(
+        functools.partial(outer_kernel, count=2),
+        [jax.ShapeDtypeStruct((hd, width), F32), jax.ShapeDtypeStruct((hd, width), B16)],
+        [low_own, after(low_other, grads_own)] + h1_shards,
+        4 * count * width * hd,
+        [pltpu.VMEM((count, width), B16)],
+        True,
+    )
+    o_head = o_own + core_swap(o_away).astype(F32)
+    o_recv = group_swap(o_head.astype(B16))
+
+    moe_got = moe_ring.send(tied(moe_got, grads_own))
+    grads = list(tied((grads_own, core_swap(grads_away)), o_own))
+    inner, gain_grads = on_core(
+        functools.partial(inner_kernel, width=width),
+        [jax.ShapeDtypeStruct((2 * chips, rows), F32), jax.ShapeDtypeStruct((8, hd), F32)],
+        [ids] + grads + raw + [total, cosine, sine, gains],
+        0,
+    )
+    n1_shards = [n1_got[o] for o in offsets if o != half] + list(n1_halves)
+    own_term(2)(inner)
+    moe_got = tied(moe_got, gain_grads)
+    inner, o_recv, *moe_got = tied((sum_chips(inner), o_recv) + tuple(moe_got))
+    o_head = (o_head + o_recv.astype(F32)).astype(B16)
+    moe_got = moe_ring.send(tuple(moe_got))
+    inner, *moe_got = tied((inner,) + tuple(moe_got), own_terms[2])
+    moe_got = moe_ring.send(tuple(moe_got))
+    low_grad_own, low_grad_other, n1_part, attn_gain = on_core(
+        functools.partial(finish_kernel, width=width),
+        [
+            jax.ShapeDtypeStruct((chips, rows, 3 * hd), B16),
+            jax.ShapeDtypeStruct((chips, rows, 3 * hd), B16),
+            jax.ShapeDtypeStruct((chips, rows, width), B16),
+            jax.ShapeDtypeStruct((8, width), F32),
+        ],
+        [ids] + grads + raw + [total, inner, cosine, sine, gains] + w_in + n1_shards,
+        12 * count * width * hd,
+    )
+    attn_gain = by_parity(jnp.sum(attn_gain, axis=0), 0, back=True) / norm_attn
+
     wo_grad = None
     for i in range(2):
         moves = [
             (g * devices + devices // 2 * g + j, g * devices + 2 * j + i) for g in range(2) for j in range(devices // 2)
         ]
-        piece = lax.ppermute(o_head[i * slab_rows : (i + 1) * slab_rows], ("dp", "ctx"), moves)
+        size = width // (2 * devices)
+        piece = lax.ppermute(o_head[i * size : (i + 1) * size], ("dp", "ctx"), moves)
         wo_grad = piece if wo_grad is None else jnp.where(core == 0, wo_grad, piece)
+    n1_part, wo_grad, *moe_got = tied((n1_part, wo_grad) + tuple(moe_got))
+    try:
+        moe_ring.send(tuple(moe_got))
+    except StopIteration as end:
+        moe_sum = end.value
     wo_grad = wo_grad.astype(F32)
 
-    def expert_grad(left_rows, right_rows, axis):
-        hidden = expert_gate.shape[2]
-        if axis == 1:
-            terms = [dot(left_rows, right_rows[:, i * hidden : (i + 1) * hidden], TN) for i in range(2)]
-        else:
-            terms = [dot(left_rows[:, i * hidden : (i + 1) * hidden], right_rows, TN) for i in range(2)]
-        total = terms[0] + core_swap(terms[1].astype(B16)).astype(F32)
-        size = total.shape[axis] // 2
-        pieces = (lax.slice_in_dim(total, 0, size, axis=axis), lax.slice_in_dim(total, size, 2 * size, axis=axis))
-        away = group_swap(pick(pieces, 1 - group).astype(B16))
-        return (pick(pieces, group) + away.astype(F32))[None]
-
-    down_grad_out = expert_grad(act_all, top_all, 0)
-    gate_grad_out = expert_grad(x_all, dgate_pre_all, 1)
-    up_grad_out = expert_grad(x_all, dup_pre_all, 1)
-
-    def placed(v):
-        return lax.dynamic_update_slice(jnp.zeros((width,), F32), v, (chip * 2 * hd,))
-
-    small = sum_all(
-        jnp.concatenate(
-            [router_term, jnp.stack([ffn_gain_grad, attn_gain, placed(query_gain), placed(key_gain)])], axis=0
+    w_own, w_away = on_core(
+        functools.partial(outer_kernel, count=2),
+        [jax.ShapeDtypeStruct((3 * hd, width), F32), jax.ShapeDtypeStruct((3 * hd, width), B16)],
+        [low_grad_own, after(low_grad_other, n1_part)] + n1_shards,
+        12 * count * width * hd,
+        [pltpu.VMEM((count, width), B16)],
+        True,
+    )
+    w_away = core_swap(w_away).astype(F32)
+    w_head = w_own + jnp.concatenate([w_away[:, width // 2 :], w_away[:, : width // 2]], axis=1)
+
+    def kept_by(which):
+        size = width // 4
+        return jnp.concatenate(
+            [lax.dynamic_slice_in_dim(w_head, i * (width // 2) + which * size, size, 1) for i in range(2)], axis=1
         )
-    )
-    router_sum, gains = small[:experts].T, small[experts:]
+
+    w_sent = kept_by(1 - group).astype(B16)
+    w_mine = kept_by(group) + group_swap(w_sent).astype(F32)
+    w_mine = w_mine.T.astype(B16).reshape(2, chips // 2, rows, 3 * hd)
+    w_mine = by_core(w_mine[0], w_mine[1], 1).reshape(devices, -1, 3 * hd)
+    w_got = lax.all_to_all(w_mine, "ctx", split_axis=0, concat_axis=0, tiled=True)
+
+    def placed(parts):
+        out = jnp.zeros((width,), F32)
+        for r, v in zip(ranks, parts):
+            out = lax.dynamic_update_slice(out, v, (r * hd,))
+        return out
+
+    late_sum = jnp.stack([attn_gain, placed(gain_grads[0::2][:2]), placed(gain_grads[1::2][:2])])
+    late_sum = [late_sum + core_swap(late_sum)]
+
+    def beside(step, *others):
+        def run(token):
+            late_sum.append(add_step(late_sum[-1], step, token))
+            return (late_sum[-1],) + others
+
+        return run
+
+    n1_grad = ring_sum(
+        lambda o: n1_part[offsets.index(o)], 1, [(w_own,)] + [beside(2**i, *([w_sent], [], [w_mine])[i - 1]) for i in range(1, half)]
+    )
+    late_sum = after(late_sum[-1], n1_grad)
+    late_sum = late_sum + group_swap(late_sum)
+    early_sum = early_sum + after(group_swap(early_sum), n1_grad)
+    expert_grads = lax.optimization_barrier(tuple(expert_grads) + (n1_grad,))[:3]
+    down_grad_out, gate_grad_out, up_grad_out = [v.astype(F32)[None] for v in expert_grads]
+    w_got = w_got.transpose(1, 0, 2).astype(F32)
+    slab_rows = w_got.shape[0]
+    wq_grad, wk_grad, wv_grad = [
+        w_got[:, :, i * hd : (i + 1) * hd].reshape(slab_rows, width) for i in range(3)
+    ]
+    n1_grad = by_parity(n1_grad, 1, back=True)
+    unused_norm, attn_back = jax.vjp(lambda v: norm_rows(v, norm_attn), inputs)
+    (input_part,) = attn_back(n1_grad)
+    tokens_grad = (h1_grad + input_part).astype(B16)
+
+    block_out = (h1 + moe_sum).astype(B16)
+    router_sum, gain_sums = early_sum[:experts].T, [early_sum[experts]] + [late_sum[i] for i in range(3)]
     return (
         block_out,
         tokens_grad,
-        gains[1],
-        gains[2],
-        gains[3],
-        gains[0],
+        gain_sums[1],
+        gain_sums[2],
+        gain_sums[3],
+        gain_sums[0],
         wq_grad,
         wk_grad,
         wv_grad,

time: 881 us -> 700 us (0.79)
  waiting for transfers between devices: 305 us -> 175 us
  Pallas kernels: 129 us -> 214 us
  matrix products: 76.2 us -> 4.95 us
  local copies, waits for them, and re-layouts: 113 us -> 53.9 us
  other arithmetic: 93.2 us -> 61 us
  blocking collectives: 0 us -> 31.7 us
  starting transfers between devices: 156 us -> 134 us
  between operations: 3.07 us -> 15.8 us
    ppermute x7 -> x5, waiting for transfers between devices: 122 us -> 15.2 us  [group_swap(): return lax.ppermute(v, 'dp', [(0, 1), (1, 0)])]
    pallas_call x2 -> x17, Pallas kernels: 18.8 us -> 126 us  [the longest x11 70.8 us: on_core(): pl.pallas_call(kernel, in_specs=[pl.BlockSpec(memory_space=m) for m in me...]
    dot_general x13 -> x2, matrix products: 74.9 us -> 1.51 us  [dot(): return lax.dot_general(a, b, dims, preferred_element_type=F32)]
    ppermute x32, waiting for transfers between devices: 70.4 us -> 35.1 us  [to_left(): return lax.ppermute(v, 'ctx', left)]
    all_to_all x0 -> x2, blocking collectives: none -> 31.7 us  [the longest x1 23.5 us: local_fast(): lax.all_to_all(slab, 'ctx', split_axis=0, concat_axis=0, axis_index_group...]
    ppermute x2 -> x8, waiting for transfers between devices: 0.01 us -> 28.1 us  [the longest x6 19.8 us: add_step(): return v + lax.ppermute(v, 'ctx', [(i, i ^ step) for i in range(devices)])]
    pallas_call x5 -> x3, Pallas kernels: 110 us -> 88.8 us  [expert_rows(): pl.pallas_call(functools.partial(expert_kernel, shards=shards, fresh=kept...]
    ppermute x32, starting transfers between devices: 40.1 us -> 20 us  [to_right(): return lax.ppermute(v, 'ctx', right)]
  transfers between devices with their start and end apart: 101 -> 106, of which waited for: 44 -> 52; matrix products, arithmetic and copies ran while one was open for 25% -> 13% of each run, Pallas kernels for 12% -> 24%
where the time goes in v2:
time: 700 us; the launch traced here: 691 us
  Pallas kernels  214 us (31%)
  waiting for transfers between devices  175 us (25%)
  starting transfers between devices  134 us (19%)
  other arithmetic  61 us (9%)
  local copies, waits for them, and re-layouts  53.9 us (8%)
  blocking collectives  31.7 us (5%)
  between operations  15.8 us (2%)
    pallas_call x3, Pallas kernels, expert_rows(): pl.pallas_call(functools.partial(expert_kernel, shards=shards, fresh=kept...  88.8 us
    ppermute x32, waiting for transfers between devices, to_right(): return lax.ppermute(v, 'ctx', right)  82.1 us
    pallas_call x11, Pallas kernels, on_core(): pl.pallas_call(kernel, in_specs=[pl.BlockSpec(memory_space=m) for m in me...  70.8 us
    pallas_call x6, Pallas kernels, expert_grad_term(): pl.pallas_call(expert_grad_kernel, grid=(high // tile,), in_specs=in_spec...  54.9 us
    ppermute x19, starting transfers between devices, core_swap(): return lax.ppermute(v, 'ctx', [(i, i ^ 1) for i in range(devices)])  43.6 us
    ppermute x32, waiting for transfers between devices, to_left(): return lax.ppermute(v, 'ctx', left)  35.1 us
    ppermute x32, starting transfers between devices, to_left(): return lax.ppermute(v, 'ctx', left)  33.3 us
    all_to_all x1, blocking collectives, local_fast(): lax.all_to_all(slab, 'ctx', split_axis=0, concat_axis=0, axis_index_group...  23.5 us
  transfers between devices with their start and end apart: 106, of which 52 were waited for; matrix products, arithmetic and copies ran while one was open for 13% of the time, Pallas kernels for 24%

profile of v2, /device:TPU:9, one launch (start us, length us, event | category | flops | bytes accessed | tf_op | source)
XLA Modules:
  0.0 691.4 jit_solution(10392683459744197357)
XLA Ops:
  24.2 23.5 %all_to_all.15 = bf16[8,128,384]{2,1,0:T(8,128)(2,1)S(1)} all-to-all(bf16[8,128,384]{2,1,0:T(8,128)(2,1)S(1)} %maximum_bitcast_fusion), channel_id=1, replica_groups={{0,2,4,6,8,10,12,14},{1,3,5,7,9,11,13,15},{16,18,20,22,24,26,28,30},{17..., dimensions={0} | all-to-all | bytes 1572864 | tf_op jit(solution)/shard_map/all_to_all | solution.py:919
  50.4 14.0 %collective-permute-done.4 = bf16[8,128,384]{2,1,0:T(8,128)(2,1)} collective-permute-done((bf16[8,128,384]{2,1,0:T(8,128)(2,1)S(1)}, bf16[8,128,384]{2,1,0:T(8,128)(2,1)}, u32[]{:S(2)}, u32[]{:S(2)}) %collective-permute-start.4) | collective-permute-done | bytes 786464 | tf_op jit(solution)/shard_map/ppermute | solution.py:818
  128.2 9.3 %shard_map.266 = (f32[2048,128]{1,0:T(8,128)}, f32[1,2048]{1,0:T(1,128)}, bf16[2048,384]{1,0:T(8,128)(2,1)}, bf16[8,128,128]{2,1,0:T(8,128)(2,1)}, bf16[8,128,128]{2,1,0:T(8,128)(2,1)}) custom-call(s32[9]{0:T(128)} %concatenate.88.ids_ref, bf16[8,128,384]{2,1,0:T(8,128)(2,1)} %get-tuple-element.203.mine_ref, bf16[8,128,384]{2,1,0:T(8,128)(2,1)} %copy-done.69, ...), custom_call_target="tpu_custom_call" | custom-call | flops 2147483648 | bytes 4735012 | tf_op jit(solution)/shard_map/pallas_call | solution.py:531
  199.7 32.4 %shard_map.267 = (bf16[3,128,2048]{2,1,0:T(8,128)(2,1)}, bf16[3,128,2048]{2,1,0:T(8,128)(2,1)}, f32[3,128,128]{2,1,0:T(8,128)}, bf16[8,128,2048]{2,1,0:T(8,128)(...) custom-call(s32[3]{0:T(128)} %pad_add_fusion.ids_ref, ...), custom_call_target="tpu_custom_call" | custom-call | flops 19327352832 | bytes 25165824 | tf_op jit(solution)/shard_map/pallas_call | solution.py:697
  235.5 23.5 %shard_map.268 = (bf16[2,128,2048]{2,1,0:T(8,128)(2,1)}, bf16[2,128,2048]{2,1,0:T(8,128)(2,1)}, f32[2,128,128]{2,1,0:T(8,128)}, bf16[8,128,2048]{2,1,0:T(8,128)(...) custom-call(s32[3]{0:T(128)} %pad_add_fusion.ids_ref, ...), custom_call_target="tpu_custom_call", output_to_operand_aliasing={{3}: (8, {}), {4}: (9, {}), {5}: (10, {}), {6}: (11, {}), {... | custom-call | flops 12884901888 | bytes 25165824 | tf_op jit(solution)/shard_map/pallas_call | solution.py:697
  266.1 32.9 %shard_map.269 = (bf16[3,128,2048]{2,1,0:T(8,128)(2,1)}, bf16[3,128,2048]{2,1,0:T(8,128)(2,1)}, f32[3,128,128]{2,1,0:T(8,128)}, bf16[8,128,2048]{2,1,0:T(8,128)(...) custom-call(s32[3]{0:T(128)} %pad_add_fusion.ids_ref, ...), custom_call_target="tpu_custom_call", output_to_operand_aliasing={{3}: (10, {}), {4}: (11, {}), {5}: (12, {}), {6}: (13, {}),... | custom-call | flops 19327352832 | bytes 25165824 | tf_op jit(solution)/shard_map/pallas_call | solution.py:697
  307.0 8.6 %shard_map.270 = bf16[1024,2048]{1,0:T(8,128)(2,1)} custom-call(bf16[1024,2048]{1,0:T(8,128)(2,1)} %bitcast.197, bf16[1024,2048]{1,0:T(8,128)(2,1)} %bitcast.203), custom_call_target="tpu_custom_call" | custom-call | tf_op jit(solution)/shard_map/pallas_call | solution.py:757
  315.6 16.9 %collective-permute-start.51 = (bf16[1024,2048]{1,0:T(8,128)(2,1)}, bf16[1024,2048]{1,0:T(8,128)(2,1)S(1)}, u32[]{:S(2)}, u32[]{:S(2)}) collective-permute-start(bf16[1024,2048]{1,0:T(8,128)(2,1)} %shard_map.270), channel_id=1, source_target_pairs={{0,1},{1,0},{2,3},{3,2},{4,5},{5,4},{6,7},{7,6},{8,9},{9,8},{10,11... | collective-permute-start | bytes 12582920 | tf_op jit(solution)/shard_map/ppermute | solution.py:815
  334.2 12.1 %collective-permute-done.47 = bf16[128,2048]{1,0:T(8,128)(2,1)S(1)} collective-permute-done((bf16[128,2048]{1,0:T(8,128)(2,1)S(1)}, bf16[128,2048]{1,0:T(8,128)(2,1)S(1)}, u32[]{:S(2)}, u32[]{:S(2)}) %collective-permute-start.47) | collective-permute-done | bytes 524320 | tf_op jit(solution)/shard_map/ppermute | solution.py:809
  348.4 9.6 %shard_map.271 = bf16[1024,2048]{1,0:T(8,128)(2,1)} custom-call(bf16[1024,2048]{1,0:T(8,128)(2,1)} %bitcast.198, bf16[1024,2048]{1,0:T(8,128)(2,1)} %bitcast.204, bf16[1024,2048]{1,0:T(8,128)(2,1)} %copy-done.22), custom_call_target="tpu_custom_call" | custom-call | tf_op jit(solution)/shard_map/pallas_call | solution.py:757
  360.9 11.3 %collective-permute-done.49 = bf16[128,2048]{1,0:T(8,128)(2,1)S(1)} collective-permute-done((bf16[128,2048]{1,0:T(8,128)(2,1)S(1)}, bf16[128,2048]{1,0:T(8,128)(2,1)S(1)}, u32[]{:S(2)}, u32[]{:S(2)}) %collective-permute-start.49) | collective-permute-done | bytes 524320 | tf_op jit(solution)/shard_map/ppermute | solution.py:809
  372.2 8.8 %shard_map.272 = bf16[2048,1024]{1,0:T(8,128)(2,1)} custom-call(bf16[1024,2048]{1,0:T(8,128)(2,1)} %bitcast.193, bf16[1024,2048]{1,0:T(8,128)(2,1)} %bitcast.199), custom_call_target="tpu_custom_call" | custom-call | tf_op jit(solution)/shard_map/pallas_call | solution.py:757
  382.9 8.3 %all_to_all.16 = f32[8,2,128]{2,1,0:T(2,128)S(1)} all-to-all(f32[8,2,128]{2,1,0:T(2,128)S(1)} %copy.179), channel_id=1, replica_groups={{0,2,4,6,8,10,12,14},{1,3,5,7,9,11,13,15},{16,18,20,22,24,26,28,30},{17..., dimensions={0} | all-to-all | bytes 16384 | tf_op jit(solution)/shard_map/all_to_all | solution.py:1082
  395.0 9.9 %collective-permute-done.52 = bf16[128,2048]{1,0:T(8,128)(2,1)S(1)} collective-permute-done((bf16[128,2048]{1,0:T(8,128)(2,1)S(1)}, bf16[128,2048]{1,0:T(8,128)(2,1)S(1)}, u32[]{:S(2)}, u32[]{:S(2)}) %collective-permute-start.52) | collective-permute-done | bytes 524320 | tf_op jit(solution)/shard_map/ppermute | solution.py:809
  411.8 11.1 %collective-permute-done.54.refs_1_.refs_3_ = bf16[128,2048]{1,0:T(8,128)(2,1)S(1)} collective-permute-done((bf16[128,2048]{1,0:T(8,128)(2,1)S(1)}, bf16[128,2048]{1,0:T(8,128)(2,1)S(1)}, u32[]{:S(2)}, u32[]{:S(2)}) %collective-permute-start.54) | collective-permute-done | bytes 524320 | tf_op jit(solution)/shard_map/ppermute | solution.py:812
  423.5 9.7 %shard_map.274 = bf16[2048,1024]{1,0:T(8,128)(2,1)} custom-call(bf16[1024,2048]{1,0:T(8,128)(2,1)} %bitcast.194, bf16[1024,2048]{1,0:T(8,128)(2,1)} %bitcast.200, bf16[2048,1024]{1,0:T(8,128)(2,1)} %collective-permute-done.60.refs_0_), custom_call_target="tpu_custom_call" | custom-call | tf_op jit(solution)/shard_map/pallas_call | solution.py:757
  455.9 8.6 %shard_map.275 = bf16[2048,1024]{1,0:T(8,128)(2,1)} custom-call(bf16[1024,2048]{1,0:T(8,128)(2,1)} %bitcast.195, bf16[1024,2048]{1,0:T(8,128)(2,1)} %bitcast.201), custom_call_target="tpu_custom_call" | custom-call | tf_op jit(solution)/shard_map/pallas_call | solution.py:757
  484.2 10.0 %shard_map.277 = (f32[8,128,384]{2,1,0:T(8,128)}, f32[8,128,384]{2,1,0:T(8,128)}) custom-call(s32[9]{0:T(128)} %concatenate.88.ids_ref, bf16[2048,384]{1,0:T(8,128)(2,1)} %get-tuple-element.226.qkv_ref, bf16[5,128,128]{2,1,0:T(8,128)(2,1)} %get-tuple-element.278.refs_0_, bf16[3,128,128]{2,1,0:T(8,128)(2,1)} %get-tuple-element.289.refs_1_, ...), custom_call_target="tpu_custom_call" | custom-call | flops 5368709120 | bytes 6307876 | tf_op jit(solution)/shard_map/pallas_call | solution.py:531
  537.6 8.3 %collective-permute-done.82 = bf16[64,2048]{1,0:T(8,128)(2,1)S(1)} collective-permute-done((bf16[64,2048]{1,0:T(8,128)(2,1)S(1)}, bf16[64,2048]{1,0:T(8,128)(2,1)S(1)}, u32[]{:S(2)}, u32[]{:S(2)}) %collective-permute-start.82) | collective-permute-done | bytes 262176 | tf_op jit(solution)/shard_map/ppermute | solution.py:1187
  545.9 9.6 %shard_map.280 = bf16[2048,1024]{1,0:T(8,128)(2,1)} custom-call(bf16[1024,2048]{1,0:T(8,128)(2,1)} %bitcast.196, bf16[1024,2048]{1,0:T(8,128)(2,1)} %bitcast.202, bf16[2048,1024]{1,0:T(8,128)(2,1)} %collective-permute-done.80.refs_0_), custom_call_target="tpu_custom_call" | custom-call | tf_op jit(solution)/shard_map/pallas_call | solution.py:757
  559.4 12.2 %shard_map.281 = (bf16[8,128,384]{2,1,0:T(8,128)(2,1)}, bf16[8,128,384]{2,1,0:T(8,128)(2,1)}, bf16[8,128,2048]{2,1,0:T(8,128)(2,1)}, f32[8,2048]{1,0:T(8,128)}) custom-call(s32[9]{0:T(128)} %concatenate.88.ids_ref, f32[8,128,384]{2,1,0:T(8,128)} %get-tuple-element.297.grad_own, f32[8,128,384]{2,1,0:T(8,128)} %copy-done.16, ...), custom_call_target="tpu_custom_call" | custom-call | flops 3221225472 | bytes 20537380 | tf_op jit(solution)/shard_map/pallas_call | solution.py:531
  574.6 7.2 %shard_map.282 = (f32[384,2048]{1,0:T(8,128)}, bf16[384,2048]{1,0:T(8,128)(2,1)}) custom-call(bf16[8,128,384]{2,1,0:T(8,128)(2,1)} %get-tuple-element.332.refs_0_, bf16[8,128,384]{2,1,0:T(8,128)(2,1)} %get-tuple-element.334.refs_1_, bf16[128,2048]{1,0:T(8,128)(2,1)} %bitcast.217, bf16[128,2048]{1,0:T(8,128)(2,1)} %copy-done.18, ...), custom_call_target="tpu_custom_call" | custom-call | tf_op jit(solution)/shard_map/pallas_call | solution.py:531
  611.2 13.3 %collective-permute-done.100 = f32[17,2048]{1,0:T(8,128)} collective-permute-done((f32[17,2048]{1,0:T(8,128)}, f32[17,2048]{1,0:T(8,128)}, u32[]{:S(2)}, u32[]{:S(2)}) %collective-permute-start.100) | collective-permute-done | bytes 139296 | tf_op jit(solution)/shard_map/ppermute | solution.py:1110
  643.2 9.2 %all-to-all-start.2 = ((bf16[16,64,384]{2,1,0:T(8,128)(2,1)}), bf16[16,64,384]{2,1,0:T(8,128)(2,1)S(1)}, u32[]{:S(2)}, u32[]{:S(2)}) async-start(bf16[16,64,384]{2,1,0:T(8,128)(2,1)} %bitcast.73), calls=%async_computation.2 | async-start | bytes 1572864 | tf_op jit(solution)/shard_map/all_to_all | solution.py:1217
  (548 shorter events, 355.3 us)
Async XLA Ops:
  7.2 667.7 %reduce-scatter.4.cloned.1.call-start = ((), (), s32[]{:S(2)}) async-start(), calls=%async_computation.6 | async-start | bytes 6291456 | tf_op jit(solution)/shard_map/reduce_scatter | solution.py:1061
  48.9 20.3 %collective-permute-start.2 = (bf16[128,2048]{1,0:T(8,128)(2,1)S(1)}, bf16[128,2048]{1,0:T(8,128)(2,1)}, u32[]{:S(2)}, u32[]{:S(2)}) collective-permute-start(bf16[128,2048]{1,0:T(8,128)(2,1)S(1)} %collective-permute-done.refs_1_.refs_14_.refs_3_), channel_id=1, source_target_pairs={{4,0},{5,1},{8,4},{9,5},{12,8},{13,9},{14,12},{15,13},{10,14},{11,... | collective-permute-start | bytes 1572872 | tf_op jit(solution)/shard_map/ppermute | solution.py:812
  70.7 83.9 %collective-permute-start.26 = (bf16[1,2048,1024]{2,1,0:T(8,128)(2,1)}, bf16[1,2048,1024]{2,1,0:T(8,128)(2,1)}, u32[]{:S(2)}, u32[]{:S(2)}) collective-permute-start(bf16[1,2048,1024]{2,1,0:T(8,128)(2,1)} %param.28), channel_id=1, source_target_pairs={{0,1},{1,0},{2,3},{3,2},{4,5},{5,4},{6,7},{7,6},{8,9},{9,8},{10,11... | collective-permute-start | bytes 12582920 | tf_op jit(solution)/shard_map/ppermute | solution.py:815
  124.3 43.9 %collective-permute-start.29 = (bf16[1,2048,1024]{2,1,0:T(8,128)(2,1)}, bf16[1,2048,1024]{2,1,0:T(8,128)(2,1)}, u32[]{:S(2)}, u32[]{:S(2)}) collective-permute-start(bf16[1,2048,1024]{2,1,0:T(8,128)(2,1)} %param.29), channel_id=1, source_target_pairs={{0,1},{1,0},{2,3},{3,2},{4,5},{5,4},{6,7},{7,6},{8,9},{9,8},{10,11... | collective-permute-start | bytes 12582920 | tf_op jit(solution)/shard_map/ppermute | solution.py:815
  138.4 40.3 %collective-permute-start.32 = (bf16[1,1024,2048]{2,1,0:T(8,128)(2,1)}, bf16[1,1024,2048]{2,1,0:T(8,128)(2,1)}, u32[]{:S(2)}, u32[]{:S(2)}) collective-permute-start(bf16[1,1024,2048]{2,1,0:T(8,128)(2,1)} %param.30), channel_id=1, source_target_pairs={{0,1},{1,0},{2,3},{3,2},{4,5},{5,4},{6,7},{7,6},{8,9},{9,8},{10,11... | collective-permute-start | bytes 12582920 | tf_op jit(solution)/shard_map/ppermute | solution.py:815
  196.8 35.4 %collective-permute-start.35 = (bf16[128,2176]{1,0:T(8,128)(2,1)S(1)}, bf16[128,2176]{1,0:T(8,128)(2,1)S(1)}, u32[]{:S(2)}, u32[]{:S(2)}) collective-permute-start(bf16[128,2176]{1,0:T(8,128)(2,1)S(1)} %collective-permute-done.33.refs_2_), channel_id=1, source_target_pairs={{0,4},{1,5},{4,8},{5,9},{8,12},{9,13},{12,14},{13,15},{14,10},{15,... | collective-permute-start | bytes 1671176 | tf_op jit(solution)/shard_map/ppermute | solution.py:809
  197.4 34.8 %collective-permute-start.36 = (bf16[128,2176]{1,0:T(8,128)(2,1)S(1)}, bf16[128,2176]{1,0:T(8,128)(2,1)S(1)}, u32[]{:S(2)}, u32[]{:S(2)}) collective-permute-start(bf16[128,2176]{1,0:T(8,128)(2,1)S(1)} %collective-permute-done.34.refs_1_), channel_id=1, source_target_pairs={{4,0},{5,1},{8,4},{9,5},{12,8},{13,9},{14,12},{15,13},{10,14},{11,... | collective-permute-start | bytes 1671176 | tf_op jit(solution)/shard_map/ppermute | solution.py:812
  198.3 33.8 %collective-permute-start.37 = (bf16[128,2048]{1,0:T(8,128)(2,1)}, bf16[128,2048]{1,0:T(8,128)(2,1)S(1)}, u32[]{:S(2)}, u32[]{:S(2)}) collective-permute-start(bf16[128,2048]{1,0:T(8,128)(2,1)} %copy-done.48), channel_id=1, source_target_pairs={{0,4},{1,5},{4,8},{5,9},{8,12},{9,13},{12,14},{13,15},{14,10},{15,... | collective-permute-start | bytes 1572872 | tf_op jit(solution)/shard_map/ppermute | solution.py:809
  198.9 33.2 %collective-permute-start.38 = (bf16[128,2048]{1,0:T(8,128)(2,1)S(1)}, bf16[128,2048]{1,0:T(8,128)(2,1)S(1)}, u32[]{:S(2)}, u32[]{:S(2)}) collective-permute-start(bf16[128,2048]{1,0:T(8,128)(2,1)S(1)} %collective-permute-done.19.refs_2_), channel_id=1, source_target_pairs={{4,0},{5,1},{8,4},{9,5},{12,8},{13,9},{14,12},{15,13},{10,14},{11,... | collective-permute-start | bytes 1572872 | tf_op jit(solution)/shard_map/ppermute | solution.py:812
  232.2 28.5 %collective-permute-start.43 = (bf16[64,2048]{1,0:T(8,128)(2,1)S(1)}, bf16[64,2048]{1,0:T(8,128)(2,1)S(1)}, u32[]{:S(2)}, u32[]{:S(2)}) collective-permute-start(bf16[64,2048]{1,0:T(8,128)(2,1)S(1)} %slice.340), channel_id=1, source_target_pairs={{0,4},{1,5},{4,8},{5,9},{8,12},{9,13},{12,14},{13,15},{14,10},{15,... | collective-permute-start | bytes 786440 | tf_op jit(solution)/shard_map/ppermute | solution.py:809
  232.9 27.8 %collective-permute-start.44 = (bf16[64,2048]{1,0:T(8,128)(2,1)S(1)}, bf16[64,2048]{1,0:T(8,128)(2,1)S(1)}, u32[]{:S(2)}, u32[]{:S(2)}) collective-permute-start(bf16[64,2048]{1,0:T(8,128)(2,1)S(1)} %slice.341), channel_id=1, source_target_pairs={{4,0},{5,1},{8,4},{9,5},{12,8},{13,9},{14,12},{15,13},{10,14},{11,... | collective-permute-start | bytes 786440 | tf_op jit(solution)/shard_map/ppermute | solution.py:812
  233.8 25.2 %collective-permute-start.39 = (bf16[128,2176]{1,0:T(8,128)(2,1)S(1)}, bf16[128,2176]{1,0:T(8,128)(2,1)S(1)}, u32[]{:S(2)}, u32[]{:S(2)}) collective-permute-start(bf16[128,2176]{1,0:T(8,128)(2,1)S(1)} %collective-permute-done.36.refs_0_), channel_id=1, source_target_pairs={{4,0},{5,1},{8,4},{9,5},{12,8},{13,9},{14,12},{15,13},{10,14},{11,... | collective-permute-start | bytes 1671176 | tf_op jit(solution)/shard_map/ppermute | solution.py:812
  233.9 25.1 %collective-permute-start.40 = (bf16[128,2176]{1,0:T(8,128)(2,1)S(1)}, bf16[128,2176]{1,0:T(8,128)(2,1)S(1)}, u32[]{:S(2)}, u32[]{:S(2)}) collective-permute-start(bf16[128,2176]{1,0:T(8,128)(2,1)S(1)} %collective-permute-done.35.refs_1_), channel_id=1, source_target_pairs={{0,4},{1,5},{4,8},{5,9},{8,12},{9,13},{12,14},{13,15},{14,10},{15,... | collective-permute-start | bytes 1671176 | tf_op jit(solution)/shard_map/ppermute | solution.py:809
  315.6 30.7 %collective-permute-start.51 = (bf16[1024,2048]{1,0:T(8,128)(2,1)}, bf16[1024,2048]{1,0:T(8,128)(2,1)S(1)}, u32[]{:S(2)}, u32[]{:S(2)}) collective-permute-start(bf16[1024,2048]{1,0:T(8,128)(2,1)} %shard_map.270), channel_id=1, source_target_pairs={{0,1},{1,0},{2,3},{3,2},{4,5},{5,4},{6,7},{7,6},{8,9},{9,8},{10,11... | collective-permute-start | bytes 12582920 | tf_op jit(solution)/shard_map/ppermute | solution.py:815
  358.0 316.9 %reduce-scatter.6.cloned.1.call-start = ((), (), s32[]{:S(2)}) async-start(), calls=%async_computation.7 | async-start | bytes 6291456 | tf_op jit(solution)/shard_map/reduce_scatter | solution.py:1061
  381.1 42.5 %collective-permute-start.60 = (bf16[2048,1024]{1,0:T(8,128)(2,1)}, bf16[2048,1024]{1,0:T(8,128)(2,1)}, u32[]{:S(2)}, u32[]{:S(2)}) collective-permute-start(bf16[2048,1024]{1,0:T(8,128)(2,1)} %shard_map.272), channel_id=1, source_target_pairs={{0,1},{1,0},{2,3},{3,2},{4,5},{5,4},{6,7},{7,6},{8,9},{9,8},{10,11... | collective-permute-start | bytes 12582920 | tf_op jit(solution)/shard_map/ppermute | solution.py:815
  433.3 241.6 %reduce-scatter.8.cloned.1.call-start = ((), (), s32[]{:S(2)}) async-start(), calls=%async_computation.8 | async-start | bytes 6291456 | tf_op jit(solution)/shard_map/reduce_scatter | solution.py:1061
  445.8 20.0 %collective-permute-start.61 = (bf16[128,2048]{1,0:T(8,128)(2,1)S(1)}, bf16[128,2048]{1,0:T(8,128)(2,1)S(1)}, u32[]{:S(2)}, u32[]{:S(2)}) collective-permute-start(bf16[128,2048]{1,0:T(8,128)(2,1)S(1)} %collective-permute-done.57.refs_3_.refs_5_), channel_id=1, source_target_pairs={{4,0},{5,1},{8,4},{9,5},{12,8},{13,9},{14,12},{15,13},{10,14},{11,... | collective-permute-start | bytes 1572872 | tf_op jit(solution)/shard_map/ppermute | solution.py:812
  494.8 51.1 %collective-permute-start.80 = (bf16[2048,1024]{1,0:T(8,128)(2,1)}, bf16[2048,1024]{1,0:T(8,128)(2,1)}, u32[]{:S(2)}, u32[]{:S(2)}) collective-permute-start(bf16[2048,1024]{1,0:T(8,128)(2,1)} %shard_map.275), channel_id=1, source_target_pairs={{0,1},{1,0},{2,3},{3,2},{4,5},{5,4},{6,7},{7,6},{8,9},{9,8},{10,11... | collective-permute-start | bytes 12582920 | tf_op jit(solution)/shard_map/ppermute | solution.py:815
  606.8 27.9 %collective-permute-start.92 = (bf16[128,2048]{1,0:T(8,128)(2,1)}, bf16[128,2048]{1,0:T(8,128)(2,1)}, u32[]{:S(2)}, u32[]{:S(2)}) collective-permute-start(bf16[128,2048]{1,0:T(8,128)(2,1)} %get-tuple-element.345), channel_id=1, source_target_pairs={{0,4},{1,5},{4,8},{5,9},{8,12},{9,13},{12,14},{13,15},{14,10},{15,... | collective-permute-start | bytes 1572872 | tf_op jit(solution)/shard_map/ppermute | solution.py:809
  607.6 27.1 %collective-permute-start.93 = (bf16[128,2048]{1,0:T(8,128)(2,1)}, bf16[128,2048]{1,0:T(8,128)(2,1)}, u32[]{:S(2)}, u32[]{:S(2)}) collective-permute-start(bf16[128,2048]{1,0:T(8,128)(2,1)} %get-tuple-element.346), channel_id=1, source_target_pairs={{4,0},{5,1},{8,4},{9,5},{12,8},{13,9},{14,12},{15,13},{10,14},{11,... | collective-permute-start | bytes 1572872 | tf_op jit(solution)/shard_map/ppermute | solution.py:812
  610.5 31.0 %collective-permute-start.98 = (bf16[384,1024]{1,0:T(8,128)(2,1)S(1)}, bf16[384,1024]{1,0:T(8,128)(2,1)S(1)}, u32[]{:S(2)}, u32[]{:S(2)}) collective-permute-start(bf16[384,1024]{1,0:T(8,128)(2,1)S(1)} %pad_maximum_fusion.1), channel_id=1, source_target_pairs={{0,16},{16,0},{1,17},{17,1},{2,18},{18,2},{3,19},{19,3},{4,20},{20... | collective-permute-start | bytes 2359304 | tf_op jit(solution)/shard_map/ppermute | solution.py:818
  626.3 27.8 %collective-permute-start.101 = (f32[17,2048]{1,0:T(8,128)}, f32[17,2048]{1,0:T(8,128)}, u32[]{:S(2)}, u32[]{:S(2)}) collective-permute-start(f32[17,2048]{1,0:T(8,128)} %add.467), channel_id=1, source_target_pairs={{0,16},{16,0},{1,17},{17,1},{2,18},{18,2},{3,19},{19,3},{4,20},{20... | collective-permute-start | bytes 417800 | tf_op jit(solution)/shard_map/ppermute | solution.py:818
  643.2 28.8 %all-to-all-start.2 = ((bf16[16,64,384]{2,1,0:T(8,128)(2,1)}), bf16[16,64,384]{2,1,0:T(8,128)(2,1)S(1)}, u32[]{:S(2)}, u32[]{:S(2)}) async-start(bf16[16,64,384]{2,1,0:T(8,128)(2,1)} %bitcast.73), calls=%async_computation.2 | async-start | bytes 1572864 | tf_op jit(solution)/shard_map/all_to_all | solution.py:1217
  (160 other events, 1975.9 us)
Sparse Core Ops, SparseCore 0:
  358.1 53.4 reduce-scatter.3
  433.4 54.3 reduce-scatter.5
  572.8 65.3 reduce-scatter.7

commit v3 on v2

--- a/solution.py
+++ b/solution.py
@@ -458,7 +458,7 @@
             inner = jnp.zeros((rows, hd), F32)
             for h, grad in ((0, grad_own), (2, grad_other)):
                 src = (raw[h][i] if i < cut else raw[h + 1][i - cut])[:, cols]
-                v = turned_back(grad[i, :, cols], cos_ref[i], sin_ref[i]) * src
+                v = turned_back(grad[i, :, cols].astype(F32), cos_ref[i], sin_ref[i]) * src
                 inner += v * gain_ref[h + j : h + j + 1]
                 out[h + j] = out[h + j] + v * scale
             inner_ref[pl.ds(j * chips + ids_ref[1 + i], 1)] = rows_sum(inner)
@@ -481,7 +481,7 @@
                 inner = column(scale * scale * scale * (inner_ref[at] / width))
                 scale = column(scale)
             for h, grad, out in ((0, grad_own, low_own), (2, grad_other, low_other)):
-                v = grad[i, :, cols]
+                v = grad[i, :, cols].astype(F32)
                 if j < 2:
                     src = (raw[h][i] if i < cut else raw[h + 1][i - cut])[:, cols]
                     v = turned_back(v, cos_ref[i], sin_ref[i])
@@ -505,15 +505,18 @@
 
 
 def outer_kernel(*refs, count):
-    left, x_refs, outs, x_all = refs[:count], refs[count : -count - 1], refs[-count - 1 : -1], refs[-1]
+    outs = refs[-count - 4 : -5] + (refs[-5:-1],)
+    left, x_refs, x_all = refs[:count], refs[count : -count - 4], refs[-1]
     x_all[...] = joined(x_refs)
     width = x_all.shape[1]
     tile = min(512, width)
     for l_ref, out in zip(left, outs):
         chips, rows, wide = l_ref.shape
         turn = l_ref[...].reshape(chips * rows, wide).astype(F32).T.astype(B16)
+        parts = out if isinstance(out, tuple) else (out,)
+        size = parts[0].shape[1]
         for lo in range(0, width, tile):
-            out[:, lo : lo + tile] = dot(turn, x_all[:, lo : lo + tile]).astype(out.dtype)
+            parts[lo // size][:, lo % size : lo % size + tile] = dot(turn, x_all[:, lo : lo + tile]).astype(B16 if len(parts) > 1 else out.dtype)
 
 
 def head_grad_kernel(*refs):
@@ -524,17 +527,17 @@
     other_ref[...] = grad[:, hd:].reshape(other_ref.shape)
 
 
-def on_core(kernel, shapes, operands, flops, scratch=(), light=False):
+def on_core(kernel, shapes, operands, flops, scratch=()):
     scalars = operands[0].dtype == jnp.int32
     memory = [pltpu.SMEM if scalars and i == 0 else pltpu.VMEM for i in range(len(operands))]
-    size = sum(v.size * v.dtype.itemsize for v in list(operands) + list(shapes))
+    size = sum(v.size * v.dtype.itemsize for v in list(operands) + jax.tree.leaves(shapes))
     return pl.pallas_call(
         kernel,
         in_specs=[pl.BlockSpec(memory_space=m) for m in memory],
         out_shape=shapes,
         scratch_shapes=scratch,
         compiler_params=pltpu.CompilerParams(vmem_limit_bytes=56 * 2**20),
-        cost_estimate=pl.CostEstimate(flops=0 if light else flops, bytes_accessed=0 if light else size, transcendentals=0),
+        cost_estimate=pl.CostEstimate(flops=flops, bytes_accessed=size, transcendentals=0),
     )(*operands)
 
 
@@ -603,15 +606,15 @@
         grad_ref[low:high, :hd] = dot(kt[:, :high], dscore).T * scale
     for i in range(chips):
         low_ref[i] = grad_ref[rows_of(ids_ref, i, rows, core)]
-        away_ref[i] = grad_ref[rows_of(ids_ref, i, rows, 1 - core)]
-
-
-def expert_kernel(ids_ref, *refs, shards, fresh):
+        away_ref[i] = grad_ref[rows_of(ids_ref, i, rows, 1 - core)].astype(B16)
+
+
+def expert_kernel(ids_ref, *refs, shards, experts, fresh):
     x_refs, refs = refs[:shards], refs[shards:]
     g_refs, refs = refs[:shards], refs[shards:]
     wg_ref, wu_ref, wd_ref = refs[:3]
     refs = refs[3 if fresh else 8 :]
-    moe_ref, dx_ref, dgate_ref, ag_ref, dg_ref, du_ref, xs_ref, gs_ref, moe_acc, dx_acc = refs
+    moe_ref, dx_ref, ag_ref, dg_ref, du_ref, xs_ref, gs_ref, moe_acc, dx_acc, dgate_acc = refs
     expert, step, steps = pl.program_id(0), pl.program_id(1), pl.num_programs(1)
     rows, width = g_refs[0].shape
     first = (expert == 0) & (step == 0)
@@ -621,12 +624,12 @@
         for i in range(shards):
             xs_ref[i] = x_refs[i][:, :width]
             gs_ref[i] = g_refs[i][...]
-        dgate_ref[...] = jnp.zeros_like(dgate_ref)
+        dgate_acc[...] = jnp.zeros_like(dgate_acc)
 
     x = xs_ref[...].reshape(shards * rows, width)
     g = gs_ref[...].reshape(shards * rows, width)
     lane = lax.broadcasted_iota(jnp.int32, (rows, LANES), 1)
-    mine = (lane < 3 * ids_ref[2]) & (lax.rem(lane, ids_ref[2]) == ids_ref[expert])
+    mine = (lane < 3 * experts) & (lax.rem(lane, experts) == ids_ref[expert])
     gate = jnp.concatenate(
         [
             jnp.sum(jnp.where(mine, x_refs[i][:, width:].astype(F32), 0.0), axis=1, keepdims=True)
@@ -643,7 +646,7 @@
     act = silu * up_pre
     part = jnp.sum(act * dact, axis=1, keepdims=True)
     lane = lax.broadcasted_iota(jnp.int32, (shards * rows, LANES), 1)
-    dgate_ref[...] += jnp.where(lane == expert, part, 0.0).reshape(dgate_ref.shape)
+    dgate_acc[...] += jnp.where(lane == ids_ref[expert], part, 0.0)
     act_low = (gate * act).astype(B16)
     dact = gate * dact
     dgate_pre = (dact * up_pre * sigma * (1.0 + gate_pre * (1.0 - sigma))).astype(B16)
@@ -667,10 +670,17 @@
     @pl.when((expert == pl.num_programs(0) - 1) & (step == steps - 1))
     def _():
         moe_ref[...] = moe_acc[...].astype(B16).reshape(moe_ref.shape)
-        dx_ref[...] = dx_acc[...].astype(B16).reshape(dx_ref.shape)
-
-
-def expert_rows(ids, xs, gs, wg, wu, wd, kept, spot, total):
+        dx_ref[:, :, :width] = dx_acc[...].astype(B16).reshape(shards, rows, width)
+        rest = dgate_acc[...]
+        sent = jnp.zeros_like(rest)
+        for i in range(3):
+            piece = rest.astype(B16).astype(F32)
+            rest -= piece
+            sent += pltpu.roll(piece, i * experts, 1) if i else piece
+        dx_ref[:, :, width:] = sent.astype(B16).reshape(shards, rows, LANES)
+
+
+def expert_rows(ids, xs, gs, wg, wu, wd, kept, spot, total, experts):
     shards = len(xs)
     rows, width = gs[0].shape
     pair, _, hidden = wg.shape
@@ -691,19 +701,18 @@
         base = 1 + len(operands)
         in_specs += [pl.BlockSpec(memory_space=pl.ANY)] * len(kept)
         operands += list(kept)
-        aliases = {base + i: 3 + i for i in range(len(kept))}
+        aliases = {base + i: 2 + i for i in range(len(kept))}
     kept_hidden = jax.ShapeDtypeStruct((total, rows, pair * hidden), B16)
     kept_width = jax.ShapeDtypeStruct((total, rows, width), B16)
     out = pl.pallas_call(
-        functools.partial(expert_kernel, shards=shards, fresh=kept is None),
+        functools.partial(expert_kernel, shards=shards, experts=experts, fresh=kept is None),
         grid_spec=pltpu.PrefetchScalarGridSpec(
             num_scalar_prefetch=1,
             grid=(pair, steps),
             in_specs=in_specs,
             out_specs=[
                 alone,
-                alone,
-                pl.BlockSpec((shards, rows, LANES), lambda e, j, ids: (0, 0, 0)),
+                pl.BlockSpec((shards, rows, width + LANES), lambda e, j, ids: (0, 0, 0)),
                 flat,
                 flat,
                 flat,
@@ -713,12 +722,12 @@
             scratch_shapes=[
                 pltpu.VMEM((shards * rows, width), F32),
                 pltpu.VMEM((shards * rows, width), F32),
+                pltpu.VMEM((shards * rows, LANES), F32),
             ],
         ),
         out_shape=[
             jax.ShapeDtypeStruct((shards, rows, width), B16),
-            jax.ShapeDtypeStruct((shards, rows, width), B16),
-            jax.ShapeDtypeStruct((shards, rows, LANES), F32),
+            jax.ShapeDtypeStruct((shards, rows, width + LANES), B16),
             kept_hidden,
             kept_hidden,
             kept_hidden,
@@ -733,36 +742,67 @@
             transcendentals=shards * rows * hidden * pair,
         ),
     )(ids, *operands)
-    return out[0], out[1], out[2], out[3:]
-
-
-def expert_grad_kernel(left_ref, right_ref, *refs):
+    return out[0], out[1], out[2:]
+
+
+def rows_grad_kernel(ids_ref, there_ref, back_ref, own_ref, grad_ref, rows_ref, gain_ref, out_ref):
+    rows, width = grad_ref.shape
+    core, blocks = ids_ref[0], width // rows
+    spots, parts = [], []
+    total, inner = jnp.zeros((rows, rows), F32), jnp.zeros((rows, rows), F32)
+    for i in range(blocks):
+        at = slice(i * rows, (i + 1) * rows)
+        chip, parity = i % (blocks // 2), core if i < blocks // 2 else 1 - core
+        spot = pl.ds(pl.multiple_of((2 * chip + parity) * rows, rows), rows)
+        part = there_ref[:, at].astype(F32) + back_ref[:, at].astype(F32) + own_ref[:, at].astype(F32)
+        part = part * gain_ref[:, spot]
+        v = rows_ref[:, spot].astype(F32)
+        total += v * v
+        inner += v * part
+        spots.append(spot)
+        parts.append(part)
+    scale = lax.rsqrt(jnp.sum(total, axis=1, keepdims=True) / width + EPS)
+    inner = scale * scale * scale * (jnp.sum(inner, axis=1, keepdims=True) / width)
+    for spot, part in zip(spots, parts):
+        out_ref[:, spot] = (grad_ref[:, spot] + part * scale - rows_ref[:, spot].astype(F32) * inner).astype(B16)
+
+
+def expert_grad_kernel(left_ref, right_ref, *refs, pieces, whole):
+    step = pl.program_id(0)
     term = dot(left_ref[...], right_ref[...], TN)
-    if len(refs) == 2:
-        term += refs[0][...].astype(F32)
-    refs[-1][...] = term.astype(B16)
+    for i in range(pieces):
+
+        @pl.when(step == i)
+        def _():
+            if whole:
+                refs[-1][...] = (term + refs[i][...].astype(F32)).astype(B16)
+            else:
+                refs[i][...] = term.astype(B16)
 
 
 def expert_grad_term(left, right, arrived, left_at, right_at, size, across):
     rows = left.shape[0]
-    tile = min(512, size)
     high, wide = (size, right.shape[1]) if across else (left.shape[1], size)
+    pieces = 4
+    tile = high // pieces
     first = left_at // tile
     in_specs = [
         pl.BlockSpec((rows, tile), lambda j: (0, first + j)),
         pl.BlockSpec((rows, wide), lambda j: (0, right_at // size)),
     ]
-    block = pl.BlockSpec((tile, wide), lambda j: (j, 0))
-    operands = [left, right] + ([] if arrived is None else [arrived])
+    fixed = pl.BlockSpec((tile, wide), lambda j: (0, 0))
+    whole = arrived is not None
     return pl.pallas_call(
-        expert_grad_kernel,
-        grid=(high // tile,),
-        in_specs=in_specs + [block] * (len(operands) - 2),
-        out_specs=block,
-        out_shape=jax.ShapeDtypeStruct((high, wide), B16),
+        functools.partial(expert_grad_kernel, pieces=pieces, whole=whole),
+        grid=(pieces,),
+        in_specs=in_specs + ([fixed] * pieces if whole else []),
+        out_specs=pl.BlockSpec((tile, wide), lambda j: (j, 0)) if whole else [fixed] * pieces,
+        out_shape=jax.ShapeDtypeStruct((high, wide), B16) if whole else [jax.ShapeDtypeStruct((tile, wide), B16)] * pieces,
         compiler_params=pltpu.CompilerParams(vmem_limit_bytes=56 * 2**20),
-        cost_estimate=pl.CostEstimate(flops=0, bytes_accessed=0, transcendentals=0),
-    )(*operands)
+        cost_estimate=pl.CostEstimate(
+            flops=2 * rows * high * wide, bytes_accessed=2 * (rows * (high + wide) + high * wide), transcendentals=0
+        ),
+    )(left, right, *(arrived if whole else []))
 
 
 def split_three(v):
@@ -851,7 +891,7 @@
 
     def ring_steps(part, axis):
         far = part(half)
-        cut = far.shape[axis] // 2
+        cut = far.shape[axis] // 2 // LANES * LANES
         a_cut = lambda v: lax.slice_in_dim(v, 0, cut, axis=axis)
         b_cut = lambda v: lax.slice_in_dim(v, cut, v.shape[axis], axis=axis)
         there, back = lax.optimization_barrier((a_cut(far), b_cut(far)))
@@ -865,23 +905,29 @@
             there, back = there + part(o), back + part(-o)
         there, back = lax.optimization_barrier((there, back))
         there, back = yield to_right(there), to_left(back)
-        return there.astype(F32) + back.astype(F32) + part(0).astype(F32)
-
-    def tied(values, *others):
-        return lax.optimization_barrier(tuple(values) + others)[: len(values)]
+        return there, back, part(0)
+
+    def tied(values, *others, all_of=False):
+        return lax.optimization_barrier(tuple(values) + others)[: None if all_of else len(values)]
 
     def ring_sum(part, axis, work=()):
-        work = list(work) + [()] * half
+        work = list(work) + [None] * half
         ring = ring_steps(part, axis)
         values, token = next(ring), None
         for i in range(half):
-            extra = work[i](token) if callable(work[i]) else work[i]
-            values = tied(values, *extra)
+            arrays, then = work[i](token) if work[i] else ((), None)
+            values = tied(values, *arrays, all_of=True)
+            if then:
+                then(*values[2:])
+            values = values[:2]
             token = values[0]
             try:
                 values = ring.send(values)
             except StopIteration as end:
                 return end.value
+
+    def total_of(terms):
+        return sum(v.astype(F32) for v in terms)
 
     def sum_chips(v):
         step = 2
@@ -915,9 +961,9 @@
         slabs.append(jnp.where(group == 0, pair[:, :, 0], pair[:, :, 1]))
     slab = jnp.concatenate(slabs, axis=2).transpose(1, 0, 2)
     first = (to_right(n1), to_left(n1))
-    slab = after(slab, *first)
     near_head = lax.all_to_all(slab, "ctx", split_axis=0, concat_axis=0, axis_index_groups=same_core, tiled=True)
     far_head = group_swap(near_head)
+    near_head, *first = tied((near_head,) + first)
     n1_got = {0: n1, -1: first[0], 1: first[1]}
     for o in range(2, half):
         one, two = lax.optimization_barrier((n1_got[1 - o], n1_got[o - 1]) + ((near_head,) if o == 2 else ()))[:2]
@@ -949,7 +995,6 @@
             + [jax.ShapeDtypeStruct((2 * chips, rows), F32)],
             [ids] + shards + w_in,
             12 * len(blocks) * rows * width * hd,
-            light=i == 0,
         )
 
     project(0, [n1_got[o] for o in early])
@@ -999,10 +1044,10 @@
     attn_low = jnp.concatenate([low_own, low_other], axis=2).reshape(count, 2 * hd)
     out_part = dot(attn_low, w_out).astype(B16).reshape(chips, rows, width)
     weights = [jnp.concatenate(pair, axis=0) for pair in (wg_pair, wu_pair, wd_pair)]
-    h1 = inputs + ring_sum(
-        lambda o: out_part[offsets.index(o)],
-        1,
-        [(), (weights[0],), (weights[1],), (weights[2],)],
+    h1 = inputs + total_of(
+        ring_sum(
+            lambda o: out_part[offsets.index(o)], 1, [None] + [lambda token, w=w: ((w,), None) for w in weights]
+        )
     )
 
     n2 = norm_rows(h1, norm_ffn).astype(B16)
@@ -1012,17 +1057,16 @@
     )
     sent = split_three(probs * chosen)
     sent.append(jnp.zeros((rows, LANES - 3 * experts), B16))
-    names = jnp.stack([rank, rank ^ 1, jnp.int32(experts)]).astype(jnp.int32)
-    moe_part, dn2_part, dgate_part = {}, {}, []
+    names = jnp.stack(ranks).astype(jnp.int32)
+    moe_part, dn2_part = {}, {}
     kept = None
 
     def run_experts(which, spot):
-        moe, dn2, dgate, kept_now = expert_rows(
-            names, [n2_got[o] for o in which], [top_got[o] for o in which], *weights, kept, spot, chips
+        moe, dn2, kept_now = expert_rows(
+            names, [n2_got[o] for o in which], [top_got[o] for o in which], *weights, kept, spot, chips, experts
         )
         for i, o in enumerate(which):
             moe_part[o], dn2_part[o] = moe[i], dn2[i]
-        dgate_part.append(dgate)
         return kept_now
 
     n2_got = {0: jnp.concatenate([n2] + sent, axis=1)}
@@ -1049,38 +1093,35 @@
         across = i == 0
         at = expert * hidden
         return expert_grad_term(
-            after(left_side, token), right_side, plus, at if across else 0, 0 if across else at, hidden, across
+            left_side if token is None else after(left_side, token), right_side, plus, at if across else 0, 0 if across else at, hidden, across
         )
 
-    arrived, expert_grads, own_terms = [], [], []
+    arrived, expert_grads = [], []
 
     def own_term(i):
         def run(token):
-            own_terms.append(expert_term(i, 0, token, arrived[i]))
-            expert_grads.append(
-                lax.psum_scatter(own_terms[i], "dp", scatter_dimension=0 if i == 0 else 1, tiled=True)
-            )
-            return own_terms[-1:]
+            return (expert_term(i, 0, token, arrived[i]),), then
+
+        def then(mine):
+            expert_grads.append(lax.psum_scatter(mine, "dp", scatter_dimension=0 if i == 0 else 1, tiled=True))
 
         return run
 
     def other_term(i):
         def run(token):
-            other = expert_term(i, 1, token, None)
-            arrived.append(core_swap(other))
-            return (other,)
+            return tuple(expert_term(i, 1, token, None)), then
+
+        def then(*other):
+            arrived.append([core_swap(v) for v in other])
 
         return run
 
-    n2_sum = ring_sum(lambda o: dn2_part[o], 1, [(), other_term(0), own_term(0), other_term(1)])
-
-    dgates = jnp.concatenate(dgate_part, axis=0)[:, :, :2].transpose(0, 2, 1)
-    spread_out = (places[None, :] == jnp.arange(chips)[:, None]).astype(F32)
-    dgates = jnp.dot(spread_out, dgates.reshape(chips, 2 * rows), precision=HIGH)
-    dgates = dgates.reshape(chips, 2, rows)
-    dgates = jnp.where(core == 0, dgates, dgates[:, ::-1])
-    dgates = lax.all_to_all(dgates, "ctx", split_axis=0, concat_axis=0, axis_index_groups=same_core, tiled=True)
-    prob_grad = dgates.reshape(experts, rows).T * chosen
+    n2_sum = total_of(
+        ring_sum(lambda o: dn2_part[o], 1, [other_term(0), other_term(1), own_term(0), other_term(2)])
+    )
+    dgates = n2_sum[:, width : width + 3 * experts].reshape(rows, 3, experts)
+    n2_sum = n2_sum[:, :width]
+    prob_grad = (dgates[:, 0] + dgates[:, 1] + dgates[:, 2]) * chosen
     logit_grad = probs * (prob_grad - jnp.sum(probs * prob_grad, axis=-1, keepdims=True))
     router_term = lax.dot_general(logit_grad, n2.astype(F32), TN, precision=HIGH)
     n2_grad = n2_sum + jnp.dot(logit_grad, router.astype(F32).T, precision=HIGH)
@@ -1105,30 +1146,32 @@
 
     h1_got = {0: h1_low, -1: to_right(h1_low), 1: to_left(h1_low)}
 
-    def add_step(v, step, token):
-        v = after(v, token)
-        return v + lax.ppermute(v, "ctx", [(i, i ^ step) for i in range(devices)])
+    def from_across(v, step, token):
+        return lax.ppermute(after(v, token), "ctx", [(i, i ^ step) for i in range(devices)])
 
     early_sum = jnp.concatenate([router_term, ffn_gain_grad[None]], axis=0)
     early_sum = early_sum + core_swap(early_sum)
-    one, two = tied((h1_got[-1], h1_got[1]), early_sum)
-    work = ()
-    for o in range(2, half):
-        one, two = tied((h1_got[1 - o], h1_got[o - 1]), early_sum, *work)
-        h1_got[-o], h1_got[o] = to_right(one), to_left(two)
-        early_sum = add_step(early_sum, 2 ** (o - 1), one)
-        work = (own_term(1) if o == 2 else other_term(2))(one)
-    away = head_grad(0, [h1_got[o] for o in early])
-    one, two = tied((h1_got[1 - half], h1_got[half - 1]), early_sum, away, *work)
+    one, two = h1_got[-1], h1_got[1]
+    for o in range(1, half):
+        mine, then = own_term(o)(h1_low if o == 1 else one) if o < 3 else ((), lambda: None)
+        h1_got[-o], h1_got[o], *mine = tied((h1_got[-o], h1_got[o]), *mine, all_of=True)
+        then(*mine)
+        one, two = h1_got[-o], h1_got[o]
+        if o < half - 1:
+            h1_got[-o - 1], h1_got[o + 1] = to_right(one), to_left(two)
     cut = rows // 2
     h1_halves = (to_right(one[:cut]), to_left(two[cut:]))
-    early_sum = add_step(early_sum, 2 ** (half - 1), one)
-    head_grad(1, [h1_got[o] for o in late if o != half] + list(h1_halves))
-    moe_ring = ring_steps(lambda o: after(moe_part[o], grad_parts[1]) if o == half else moe_part[o], 1)
+    away = head_grad(0, [after(h1_got[0], one)] + [h1_got[o] for o in early[1:]])
+    h1_halves = tied(h1_halves, away)
+    away = head_grad(1, [h1_got[o] for o in late if o != half] + list(h1_halves))
+    moe_ring = ring_steps(lambda o: after(moe_part[o], *h1_halves) if o == half else moe_part[o], 1)
     moe_got = next(moe_ring)
+    attn = after(attn, *moe_got)
+    moe_got = moe_ring.send(moe_got)
+    early_recv = from_across(early_sum, 2, away)
     grads_own, grads_away = on_core(
         functools.partial(attention_backward, block=block, scale=scale),
-        [jax.ShapeDtypeStruct((chips, rows, 3 * hd), F32)] * 2,
+        [jax.ShapeDtypeStruct((chips, rows, 3 * hd), t) for t in (F32, B16)],
         [ids, head_qkv] + grad_parts + [attn, lse, seg_row],
         20 * half_wide * hd,
         [
@@ -1137,20 +1180,7 @@
             pltpu.VMEM((everything, block), F32),
         ],
     )
-    h1_shards = [h1_got[o] for o in offsets if o != half] + list(h1_halves)
-    o_own, o_away = on_core(
-        functools.partial(outer_kernel, count=2),
-        [jax.ShapeDtypeStruct((hd, width), F32), jax.ShapeDtypeStruct((hd, width), B16)],
-        [low_own, after(low_other, grads_own)] + h1_shards,
-        4 * count * width * hd,
-        [pltpu.VMEM((count, width), B16)],
-        True,
-    )
-    o_head = o_own + core_swap(o_away).astype(F32)
-    o_recv = group_swap(o_head.astype(B16))
-
-    moe_got = moe_ring.send(tied(moe_got, grads_own))
-    grads = list(tied((grads_own, core_swap(grads_away)), o_own))
+    grads = [grads_own, core_swap(grads_away)]
     inner, gain_grads = on_core(
         functools.partial(inner_kernel, width=width),
         [jax.ShapeDtypeStruct((2 * chips, rows), F32), jax.ShapeDtypeStruct((8, hd), F32)],
@@ -1158,13 +1188,26 @@
         0,
     )
     n1_shards = [n1_got[o] for o in offsets if o != half] + list(n1_halves)
-    own_term(2)(inner)
-    moe_got = tied(moe_got, gain_grads)
-    inner, o_recv, *moe_got = tied((sum_chips(inner), o_recv) + tuple(moe_got))
-    o_head = (o_head + o_recv.astype(F32)).astype(B16)
+    h1_shards = [h1_got[o] for o in offsets if o != half] + list(h1_halves)
+    o_own, *o_away = on_core(
+        functools.partial(outer_kernel, count=2),
+        [jax.ShapeDtypeStruct((hd, width), F32)] + [jax.ShapeDtypeStruct((hd, width // 4), B16)] * 4,
+        [low_own, after(low_other, gain_grads)] + h1_shards,
+        4 * count * width * hd,
+        [pltpu.VMEM((count, width), B16)],
+    )
+    o_head = o_own + jnp.concatenate([core_swap(v) for v in o_away], axis=1).astype(F32)
+    o_recv = group_swap(o_head.astype(B16))
+
+    early_recv, *moe_got = tied((early_recv,) + tuple(moe_got), grads_own)
     moe_got = moe_ring.send(tuple(moe_got))
-    inner, *moe_got = tied((inner,) + tuple(moe_got), own_terms[2])
-    moe_got = moe_ring.send(tuple(moe_got))
+    early_sum = early_sum + early_recv
+    early_recv = from_across(early_sum, 4, grads_own)
+    inner, *moe_got = tied((inner,) + tuple(moe_got), o_own)
+    inner = sum_chips(inner)
+    moe_got = moe_ring.send(tied(moe_got, inner))
+    early_sum = early_sum + after(early_recv, inner)
+    early_recv = from_across(early_sum, 8, inner)
     low_grad_own, low_grad_other, n1_part, attn_gain = on_core(
         functools.partial(finish_kernel, width=width),
         [
@@ -1178,6 +1221,81 @@
     )
     attn_gain = by_parity(jnp.sum(attn_gain, axis=0), 0, back=True) / norm_attn
 
+    n1_part, *moe_got = tied((n1_part,) + tuple(moe_got))
+    try:
+        moe_ring.send(tuple(moe_got))
+    except StopIteration as end:
+        moe_sum = total_of(end.value)
+
+    def heads_grads(token):
+        return on_core(
+            functools.partial(outer_kernel, count=2),
+            [jax.ShapeDtypeStruct((3 * hd, width), F32)] + [jax.ShapeDtypeStruct((3 * hd, width // 4), B16)] * 4,
+            [low_grad_own, after(low_grad_other, token)] + n1_shards,
+            12 * count * width * hd,
+            [pltpu.VMEM((count, width), B16)],
+        )
+
+    def placed(parts):
+        out = jnp.zeros((width,), F32)
+        for r, v in zip(ranks, parts):
+            out = lax.dynamic_update_slice(out, v, (r * hd,))
+        return out
+
+    gain_grads = after(gain_grads, n1_part)
+    late_sum = jnp.stack([attn_gain, placed(gain_grads[0::2][:2]), placed(gain_grads[1::2][:2])])
+    late_sum = [late_sum + core_swap(late_sum)]
+    w_got, grads_out = [], []
+
+    def kept_by(which):
+        size = width // 4
+        return jnp.concatenate(
+            [lax.dynamic_slice_in_dim(w_got[0], i * (width // 2) + which * size, size, 1) for i in range(2)], axis=1
+        )
+
+    early = []
+
+    def swap_heads(early_recv, w_own, *w_away):
+        early.append(group_swap(early_sum + early_recv))
+        early.append(early_sum + early_recv)
+        w_away = [core_swap(v) for v in w_away]
+        w_got.append(w_own + jnp.concatenate(w_away[2:] + w_away[:2], axis=1).astype(F32))
+        w_got.append(group_swap(kept_by(1 - group).astype(B16)))
+
+    def in_slabs(w_mine):
+        w_mine = w_mine.T.astype(B16).reshape(2, chips // 2, rows, 3 * hd)
+        return by_core(w_mine[0], w_mine[1], 1).reshape(devices, -1, 3 * hd)
+
+    def join(w_mine):
+        w_got.append(lax.all_to_all(w_mine, "ctx", split_axis=0, concat_axis=0, tiled=True))
+
+    def small_step(step, others=lambda token: (), then=None):
+        def run(token):
+            return (from_across(late_sum[-1], step, token),) + tuple(others(token)), finish
+
+        def finish(v, *rest):
+            late_sum.append(late_sum[-1] + v)
+            if then:
+                then(*rest)
+
+        return run
+
+    n1_grad = ring_sum(
+        lambda o: n1_part[offsets.index(o)],
+        1,
+        [
+            None,
+            small_step(2, lambda token: [early_recv] + list(heads_grads(token)), swap_heads),
+            small_step(4, lambda token: [in_slabs(kept_by(group) + after(w_got[1], token).astype(F32))], join),
+            small_step(
+                8,
+                lambda token: w_got[2:] + [v.astype(F32)[None] for v in tied(expert_grads, token)],
+                lambda w, *v: grads_out.extend((w,) + v),
+            ),
+        ],
+    )
+    w_got, down_grad_out, gate_grad_out, up_grad_out = grads_out
+    o_head = (o_head + after(o_recv, n1_grad[0]).astype(F32)).astype(B16)
     wo_grad = None
     for i in range(2):
         moves = [
@@ -1186,69 +1304,21 @@
         size = width // (2 * devices)
         piece = lax.ppermute(o_head[i * size : (i + 1) * size], ("dp", "ctx"), moves)
         wo_grad = piece if wo_grad is None else jnp.where(core == 0, wo_grad, piece)
-    n1_part, wo_grad, *moe_got = tied((n1_part, wo_grad) + tuple(moe_got))
-    try:
-        moe_ring.send(tuple(moe_got))
-    except StopIteration as end:
-        moe_sum = end.value
     wo_grad = wo_grad.astype(F32)
-
-    w_own, w_away = on_core(
-        functools.partial(outer_kernel, count=2),
-        [jax.ShapeDtypeStruct((3 * hd, width), F32), jax.ShapeDtypeStruct((3 * hd, width), B16)],
-        [low_grad_own, after(low_grad_other, n1_part)] + n1_shards,
-        12 * count * width * hd,
-        [pltpu.VMEM((count, width), B16)],
-        True,
-    )
-    w_away = core_swap(w_away).astype(F32)
-    w_head = w_own + jnp.concatenate([w_away[:, width // 2 :], w_away[:, : width // 2]], axis=1)
-
-    def kept_by(which):
-        size = width // 4
-        return jnp.concatenate(
-            [lax.dynamic_slice_in_dim(w_head, i * (width // 2) + which * size, size, 1) for i in range(2)], axis=1
-        )
-
-    w_sent = kept_by(1 - group).astype(B16)
-    w_mine = kept_by(group) + group_swap(w_sent).astype(F32)
-    w_mine = w_mine.T.astype(B16).reshape(2, chips // 2, rows, 3 * hd)
-    w_mine = by_core(w_mine[0], w_mine[1], 1).reshape(devices, -1, 3 * hd)
-    w_got = lax.all_to_all(w_mine, "ctx", split_axis=0, concat_axis=0, tiled=True)
-
-    def placed(parts):
-        out = jnp.zeros((width,), F32)
-        for r, v in zip(ranks, parts):
-            out = lax.dynamic_update_slice(out, v, (r * hd,))
-        return out
-
-    late_sum = jnp.stack([attn_gain, placed(gain_grads[0::2][:2]), placed(gain_grads[1::2][:2])])
-    late_sum = [late_sum + core_swap(late_sum)]
-
-    def beside(step, *others):
-        def run(token):
-            late_sum.append(add_step(late_sum[-1], step, token))
-            return (late_sum[-1],) + others
-
-        return run
-
-    n1_grad = ring_sum(
-        lambda o: n1_part[offsets.index(o)], 1, [(w_own,)] + [beside(2**i, *([w_sent], [], [w_mine])[i - 1]) for i in range(1, half)]
-    )
-    late_sum = after(late_sum[-1], n1_grad)
+    late_sum = after(late_sum[-1], n1_grad[0])
     late_sum = late_sum + group_swap(late_sum)
-    early_sum = early_sum + after(group_swap(early_sum), n1_grad)
-    expert_grads = lax.optimization_barrier(tuple(expert_grads) + (n1_grad,))[:3]
-    down_grad_out, gate_grad_out, up_grad_out = [v.astype(F32)[None] for v in expert_grads]
+    early_sum = early[1] + after(early[0], n1_grad[0])
     w_got = w_got.transpose(1, 0, 2).astype(F32)
     slab_rows = w_got.shape[0]
     wq_grad, wk_grad, wv_grad = [
         w_got[:, :, i * hd : (i + 1) * hd].reshape(slab_rows, width) for i in range(3)
     ]
-    n1_grad = by_parity(n1_grad, 1, back=True)
-    unused_norm, attn_back = jax.vjp(lambda v: norm_rows(v, norm_attn), inputs)
-    (input_part,) = attn_back(n1_grad)
-    tokens_grad = (h1_grad + input_part).astype(B16)
+    tokens_grad = on_core(
+        rows_grad_kernel,
+        jax.ShapeDtypeStruct((rows, width), B16),
+        [ids, *n1_grad, h1_grad, tokens, norm_attn.reshape(1, width)],
+        0,
+    )
 
     block_out = (h1 + moe_sum).astype(B16)
     router_sum, gain_sums = early_sum[:experts].T, [early_sum[experts]] + [late_sum[i] for i in range(3)]

time: 700 us -> 636 us (0.909)
  waiting for transfers between devices: 175 us -> 137 us
  blocking collectives: 31.7 us -> 0 us
  starting transfers between devices: 134 us -> 152 us
  other arithmetic: 61 us -> 51 us
  local copies, waits for them, and re-layouts: 53.9 us -> 45.3 us
  Pallas kernels: 214 us -> 222 us
    all_to_all x2 -> x0, blocking collectives: 31.7 us -> none  [the longest x1 23.5 us: local_fast(): lax.all_to_all(slab, 'ctx', split_axis=0, concat_axis=0, axis_index_group...]
    all_to_all x1 -> x2, waiting for transfers between devices: 5.67 us -> 29.8 us  [the longest x1 15.5 us: local_fast(): lax.all_to_all(slab, 'ctx', split_axis=0, concat_axis=0, axis_index_group...]
    ppermute x19 -> x34, starting transfers between devices: 43.6 us -> 67 us  [core_swap(): return lax.ppermute(v, 'ctx', [(i, i ^ 1) for i in range(devices)])]
    ppermute x32, waiting for transfers between devices: 82.1 us -> 60.1 us  [to_right(): return lax.ppermute(v, 'ctx', right)]
    ppermute x6, waiting for transfers between devices: 19.8 us -> 0.02 us  [from_across(): lax.ppermute(after(v, token), 'ctx', [(i, i ^ step) for i in range(device...]
    ppermute x32, waiting for transfers between devices: 35.1 us -> 16.6 us  [to_left(): return lax.ppermute(v, 'ctx', left)]
    ppermute x32, starting transfers between devices: 20 us -> 28.8 us  [to_right(): return lax.ppermute(v, 'ctx', right)]
    ppermute x32, starting transfers between devices: 33.3 us -> 25 us  [to_left(): return lax.ppermute(v, 'ctx', left)]
  transfers between devices with their start and end apart: 106 -> 122, of which waited for: 52 -> 41; matrix products, arithmetic and copies ran while one was open for 13% -> 12% of each run, Pallas kernels for 24% -> 30%
where the time goes in v3:
time: 636 us; the launch traced here: 627 us
  Pallas kernels  222 us (35%)
  starting transfers between devices  152 us (24%)
  waiting for transfers between devices  137 us (22%)
  other arithmetic  51 us (8%)
  local copies, waits for them, and re-layouts  45.3 us (7%)
  between operations  15.5 us (2%)
    pallas_call x3, Pallas kernels, expert_rows(): pl.pallas_call(functools.partial(expert_kernel, shards=shards, experts=ex...  88.1 us
    pallas_call x12, Pallas kernels, on_core(): pl.pallas_call(kernel, in_specs=[pl.BlockSpec(memory_space=m) for m in me...  73.4 us
    ppermute x34, starting transfers between devices, core_swap(): return lax.ppermute(v, 'ctx', [(i, i ^ 1) for i in range(devices)])  67 us
    pallas_call x6, Pallas kernels, expert_grad_term(): pl.pallas_call(functools.partial(expert_grad_kernel, pieces=pieces, whole...  60.4 us
    ppermute x32, waiting for transfers between devices, to_right(): return lax.ppermute(v, 'ctx', right)  60.1 us
    ppermute x32, starting transfers between devices, to_right(): return lax.ppermute(v, 'ctx', right)  28.8 us
    ppermute x32, starting transfers between devices, to_left(): return lax.ppermute(v, 'ctx', left)  25 us
    ppermute x5, waiting for transfers between devices, group_swap(): return lax.ppermute(v, 'dp', [(0, 1), (1, 0)])  16.9 us
  transfers between devices with their start and end apart: 122, of which 41 were waited for; matrix products, arithmetic and copies ran while one was open for 12% of the time, Pallas kernels for 30%

profile of v3, /device:TPU:9, one launch (start us, length us, event | category | flops | bytes accessed | tf_op | source)
XLA Modules:
  0.0 627.3 jit_solution(4672045590548470024)
XLA Ops:
  22.5 15.5 %all-to-all-done = bf16[8,128,384]{2,1,0:T(8,128)(2,1)S(1)} async-done(((bf16[8,128,384]{2,1,0:T(8,128)(2,1)}), bf16[8,128,384]{2,1,0:T(8,128)(2,1)S(1)}, u32[]{:S(2)}, u32[]{:S(2)}) %all-to-all-start) | async-done | bytes 786464 | tf_op jit(solution)/shard_map/all_to_all | solution.py:964
  41.8 9.6 %collective-permute-done.refs_2_.refs_15_.refs_4_ = bf16[128,2048]{1,0:T(8,128)(2,1)} collective-permute-done((bf16[128,2048]{1,0:T(8,128)(2,1)S(1)}, bf16[128,2048]{1,0:T(8,128)(2,1)}, u32[]{:S(2)}, u32[]{:S(2)}) %collective-permute-start) | collective-permute-done | bytes 524320 | tf_op jit(solution)/shard_map/ppermute | solution.py:849
  59.4 6.8 %collective-permute-done.2.refs_3_.refs_16_.refs_5_ = bf16[128,2048]{1,0:T(8,128)(2,1)} collective-permute-done((bf16[128,2048]{1,0:T(8,128)(2,1)}, bf16[128,2048]{1,0:T(8,128)(2,1)}, u32[]{:S(2)}, u32[]{:S(2)}) %collective-permute-start.2) | collective-permute-done | bytes 524320 | tf_op jit(solution)/shard_map/ppermute | solution.py:852
  111.5 9.0 %collective-permute-start.16 = (bf16[8,128,384]{2,1,0:T(8,128)(2,1)}, bf16[8,128,384]{2,1,0:T(8,128)(2,1)S(1)}, u32[]{:S(2)}, u32[]{:S(2)}) collective-permute-start(bf16[8,128,384]{2,1,0:T(8,128)(2,1)} %get-tuple-element.253), channel_id=1, source_target_pairs={{0,1},{1,0},{2,3},{3,2},{4,5},{5,4},{6,7},{7,6},{8,9},{9,8},{10,11... | collective-permute-start | bytes 2359304 | tf_op jit(solution)/shard_map/ppermute | solution.py:855
  125.1 9.3 %shard_map.266 = (f32[2048,128]{1,0:T(8,128)}, f32[1,2048]{1,0:T(1,128)}, bf16[2048,384]{1,0:T(8,128)(2,1)}, bf16[8,128,128]{2,1,0:T(8,128)(2,1)}, bf16[8,128,128]{2,1,0:T(8,128)(2,1)}) custom-call(s32[9]{0:T(128)} %concatenate.88.ids_ref, bf16[8,128,384]{2,1,0:T(8,128)(2,1)} %get-tuple-element.252.mine_ref, bf16[8,128,384]{2,1,0:T(8,128)(2,1)} %copy-done.62, ...), custom_call_target="tpu_custom_call" | custom-call | flops 2147483648 | bytes 4735012 | tf_op jit(solution)/shard_map/pallas_call | solution.py:534
  185.4 6.9 %collective-permute-done.33.refs_2_ = bf16[128,2176]{1,0:T(8,128)(2,1)S(1)} collective-permute-done((bf16[128,2176]{1,0:T(8,128)(2,1)S(1)}, bf16[128,2176]{1,0:T(8,128)(2,1)S(1)}, u32[]{:S(2)}, u32[]{:S(2)}) %collective-permute-start.33) | collective-permute-done | bytes 557088 | tf_op jit(solution)/shard_map/ppermute | solution.py:849
  196.4 32.4 %shard_map.267 = (bf16[3,128,2048]{2,1,0:T(8,128)(2,1)}, bf16[3,128,2176]{2,1,0:T(8,128)(2,1)}, bf16[8,128,2048]{2,1,0:T(8,128)(2,1)}, bf16[8,128,2048]{2,1,0:T(...) custom-call(s32[2]{0:T(128)} %pad_add_fusion.ids_ref, ...), custom_call_target="tpu_custom_call" | custom-call | flops 19327352832 | bytes 25165824 | tf_op jit(solution)/shard_map/pallas_call | solution.py:707
  232.2 23.4 %shard_map.268 = (bf16[2,128,2048]{2,1,0:T(8,128)(2,1)}, bf16[2,128,2176]{2,1,0:T(8,128)(2,1)}, bf16[8,128,2048]{2,1,0:T(8,128)(2,1)}, bf16[8,128,2048]{2,1,0:T(...) custom-call(s32[2]{0:T(128)} %pad_add_fusion.ids_ref, ...), custom_call_target="tpu_custom_call", output_to_operand_aliasing={{2}: (8, {}), {3}: (9, {}), {4}: (10, {}), {5}: (11, {}), {... | custom-call | flops 12884901888 | bytes 25165824 | tf_op jit(solution)/shard_map/pallas_call | solution.py:707
  263.5 32.3 %shard_map.269 = (bf16[3,128,2048]{2,1,0:T(8,128)(2,1)}, bf16[3,128,2176]{2,1,0:T(8,128)(2,1)}, bf16[8,128,2048]{2,1,0:T(8,128)(2,1)}, bf16[8,128,2048]{2,1,0:T(...) custom-call(s32[2]{0:T(128)} %pad_add_fusion.ids_ref, ...), custom_call_target="tpu_custom_call", output_to_operand_aliasing={{2}: (10, {}), {3}: (11, {}), {4}: (12, {}), {5}: (13, {}),... | custom-call | flops 19327352832 | bytes 25165824 | tf_op jit(solution)/shard_map/pallas_call | solution.py:707
  299.1 10.0 %shard_map.270 = (bf16[256,2048]{1,0:T(8,128)(2,1)}, bf16[256,2048]{1,0:T(8,128)(2,1)}, bf16[256,2048]{1,0:T(8,128)(2,1)}, bf16[256,2048]{1,0:T(8,128)(2,1)}) custom-call(bf16[1024,2048]{1,0:T(8,128)(2,1)} %bitcast.161, bf16[1024,2048]{1,0:T(8,128)(2,1)} %bitcast.167), custom_call_target="tpu_custom_call" | custom-call | flops 4294967296 | bytes 10485760 | tf_op jit(solution)/shard_map/pallas_call | solution.py:795
  311.6 15.7 %collective-permute-start.51 = (bf16[256,2048]{1,0:T(8,128)(2,1)}, bf16[256,2048]{1,0:T(8,128)(2,1)S(1)}, u32[]{:S(2)}, u32[]{:S(2)}) collective-permute-start(bf16[256,2048]{1,0:T(8,128)(2,1)} %get-tuple-element.322), channel_id=1, source_target_pairs={{0,1},{1,0},{2,3},{3,2},{4,5},{5,4},{6,7},{7,6},{8,9},{9,8},{10,11... | collective-permute-start | bytes 3145736 | tf_op jit(solution)/shard_map/ppermute | solution.py:855
  327.9 7.0 %collective-permute-start.54 = (bf16[256,2048]{1,0:T(8,128)(2,1)}, bf16[256,2048]{1,0:T(8,128)(2,1)S(1)}, u32[]{:S(2)}, u32[]{:S(2)}) collective-permute-start(bf16[256,2048]{1,0:T(8,128)(2,1)} %get-tuple-element.325), channel_id=1, source_target_pairs={{0,1},{1,0},{2,3},{3,2},{4,5},{5,4},{6,7},{7,6},{8,9},{9,8},{10,11... | collective-permute-start | bytes 3145736 | tf_op jit(solution)/shard_map/ppermute | solution.py:855
  334.9 9.6 %shard_map.271 = (bf16[512,1024]{1,0:T(8,128)(2,1)}, bf16[512,1024]{1,0:T(8,128)(2,1)}, bf16[512,1024]{1,0:T(8,128)(2,1)}, bf16[512,1024]{1,0:T(8,128)(2,1)}) custom-call(bf16[1024,2048]{1,0:T(8,128)(2,1)} %bitcast.157, bf16[1024,2048]{1,0:T(8,128)(2,1)} %bitcast.163), custom_call_target="tpu_custom_call" | custom-call | flops 4294967296 | bytes 10485760 | tf_op jit(solution)/shard_map/pallas_call | solution.py:795
  350.5 10.4 %shard_map.272 = bf16[1024,2048]{1,0:T(8,128)(2,1)} custom-call(bf16[1024,2048]{1,0:T(8,128)(2,1)} %bitcast.162, bf16[1024,2048]{1,0:T(8,128)(2,1)} %bitcast.168, bf16[256,2048]{1,0:T(8,128)(2,1)} %copy-done.28, bf16[256,2048]{1,0:T(8,128)(2,1)} %copy-done.29, bf16[256,2048]{1,0:T(8,128)(2,1)} %copy-done.30, bf16[256,2048]{1,0:T(8,128)(2,1)} %copy-done.31), custom_call_target="tpu_custom_call" | custom-call | flops 4294967296 | bytes 10485760 | tf_op jit(solution)/shard_map/pallas_call | solution.py:795
  366.9 9.8 %shard_map.273 = (bf16[512,1024]{1,0:T(8,128)(2,1)}, bf16[512,1024]{1,0:T(8,128)(2,1)}, bf16[512,1024]{1,0:T(8,128)(2,1)}, bf16[512,1024]{1,0:T(8,128)(2,1)}) custom-call(bf16[1024,2048]{1,0:T(8,128)(2,1)} %bitcast.158, bf16[1024,2048]{1,0:T(8,128)(2,1)} %bitcast.165), custom_call_target="tpu_custom_call" | custom-call | flops 4294967296 | bytes 10485760 | tf_op jit(solution)/shard_map/pallas_call | solution.py:795
  385.5 10.4 %shard_map.274 = bf16[2048,1024]{1,0:T(8,128)(2,1)} custom-call(bf16[1024,2048]{1,0:T(8,128)(2,1)} %bitcast.159, bf16[1024,2048]{1,0:T(8,128)(2,1)} %bitcast.164, bf16[512,1024]{1,0:T(8,128)(2,1)} %collective-permute-done.59.refs_0_, bf16[512,1024]{1,0:T(8,128)(2,1)} %collective-permute-done.60.refs_1_, bf16[512,1024]{1,0:T(8,128)(2,1)} %collective-permute-done.61.refs_2_, ...), custom_call_target="tpu_custom_call" | custom-call | flops 4294967296 | bytes 10485760 | tf_op jit(solution)/shard_map/pallas_call | solution.py:795
  406.7 10.2 %shard_map.275 = bf16[2048,1024]{1,0:T(8,128)(2,1)} custom-call(bf16[1024,2048]{1,0:T(8,128)(2,1)} %bitcast.160, bf16[1024,2048]{1,0:T(8,128)(2,1)} %bitcast.166, bf16[512,1024]{1,0:T(8,128)(2,1)} %copy-done.32, bf16[512,1024]{1,0:T(8,128)(2,1)} %copy-done.33, bf16[512,1024]{1,0:T(8,128)(2,1)} %copy-done.34, bf16[512,1024]{1,0:T(8,128)(2,1)} %copy-done.35), custom_call_target="tpu_custom_call" | custom-call | flops 4294967296 | bytes 10485760 | tf_op jit(solution)/shard_map/pallas_call | solution.py:795
  420.0 10.3 %collective-permute-done.69.refs_1_.refs_8_ = bf16[128,2048]{1,0:T(8,128)(2,1)S(1)} collective-permute-done((bf16[128,2048]{1,0:T(8,128)(2,1)S(1)}, bf16[128,2048]{1,0:T(8,128)(2,1)S(1)}, u32[]{:S(2)}, u32[]{:S(2)}) %collective-permute-start.69) | collective-permute-done | bytes 524320 | tf_op jit(solution)/shard_map/ppermute | solution.py:849
  452.7 9.9 %shard_map.278 = (f32[8,128,384]{2,1,0:T(8,128)}, bf16[8,128,384]{2,1,0:T(8,128)(2,1)}) custom-call(s32[9]{0:T(128)} %concatenate.88.ids_ref, bf16[2048,384]{1,0:T(8,128)(2,1)} %get-tuple-element.275.qkv_ref, bf16[5,128,128]{2,1,0:T(8,128)(2,1)} %get-tuple-element.355.refs_0_, bf16[3,128,128]{2,1,0:T(8,128)(2,1)} %get-tuple-element.360.refs_1_, ...), custom_call_target="tpu_custom_call" | custom-call | flops 5368709120 | bytes 5521444 | tf_op jit(solution)/shard_map/pallas_call | solution.py:534
  496.1 12.0 %shard_map.281 = (bf16[8,128,384]{2,1,0:T(8,128)(2,1)}, bf16[8,128,384]{2,1,0:T(8,128)(2,1)}, bf16[8,128,2048]{2,1,0:T(8,128)(2,1)}, f32[8,2048]{1,0:T(8,128)}) custom-call(s32[9]{0:T(128)} %concatenate.88.ids_ref, f32[8,128,384]{2,1,0:T(8,128)} %get-tuple-element.369.grad_own, bf16[8,128,384]{2,1,0:T(8,128)(2,1)} %copy-done.17, ...), custom_call_target="tpu_custom_call" | custom-call | flops 3221225472 | bytes 19750948 | tf_op jit(solution)/shard_map/pallas_call | solution.py:534
  513.3 7.5 %collective-permute-start.93 = (f32[3,2048]{1,0:T(4,128)S(1)}, f32[3,2048]{1,0:T(4,128)S(1)}, u32[]{:S(2)}, u32[]{:S(2)}) collective-permute-start(f32[3,2048]{1,0:T(4,128)S(1)} %pad_maximum_fusion.17), channel_id=1, source_target_pairs={{0,1},{1,0},{2,3},{3,2},{4,5},{5,4},{6,7},{7,6},{8,9},{9,8},{10,11... | collective-permute-start | bytes 73736 | tf_op jit(solution)/shard_map/ppermute | solution.py:855
  523.2 7.1 %shard_map.282 = (f32[384,2048]{1,0:T(8,128)}, bf16[384,512]{1,0:T(8,128)(2,1)}, bf16[384,512]{1,0:T(8,128)(2,1)}, bf16[384,512]{1,0:T(8,128)(2,1)}, bf16[384,512]{1,0:T(8,128)(2,1)}) custom-call(bf16[8,128,384]{2,1,0:T(8,128)(2,1)} %get-tuple-element.408.refs_0_, bf16[8,128,384]{2,1,0:T(8,128)(2,1)} %get-tuple-element.410.refs_1_, ...), custom_call_target="tpu_custom_call" | custom-call | flops 3221225472 | bytes 10485760 | tf_op jit(solution)/shard_map/pallas_call | solution.py:534
  547.7 16.9 %collective-permute-done.104 = bf16[384,1024]{1,0:T(8,128)(2,1)S(1)} collective-permute-done((bf16[384,1024]{1,0:T(8,128)(2,1)S(1)}, bf16[384,1024]{1,0:T(8,128)(2,1)S(1)}, u32[]{:S(2)}, u32[]{:S(2)}) %collective-permute-start.104) | collective-permute-done | bytes 786464 | tf_op jit(solution)/shard_map/ppermute | solution.py:858
  588.0 14.4 %all-to-all-done.1 = bf16[16,64,384]{2,1,0:T(8,128)(2,1)S(1)} async-done(((bf16[16,64,384]{2,1,0:T(8,128)(2,1)}), bf16[16,64,384]{2,1,0:T(8,128)(2,1)S(1)}, u32[]{:S(2)}, u32[]{:S(2)}) %all-to-all-start.1) | async-done | bytes 786464 | tf_op jit(solution)/shard_map/all_to_all | solution.py:1270
  (556 shorter events, 305.6 us)
Async XLA Ops:
  15.3 22.7 %all-to-all-start = ((bf16[8,128,384]{2,1,0:T(8,128)(2,1)}), bf16[8,128,384]{2,1,0:T(8,128)(2,1)S(1)}, u32[]{:S(2)}, u32[]{:S(2)}) async-start(bf16[8,128,384]{2,1,0:T(8,128)(2,1)} %maximum_bitcast_fusion), calls=%async_computation | async-start | bytes 1572864 | tf_op jit(solution)/shard_map/all_to_all | solution.py:964
  20.9 557.5 %reduce-scatter.4.cloned.1.call-start = ((), (), s32[]{:S(2)}) async-start(), calls=%async_computation.5 | async-start | bytes 6291456 | tf_op jit(solution)/shard_map/reduce_scatter | solution.py:1106
  67.7 84.4 %collective-permute-start.26 = (bf16[1,2048,1024]{2,1,0:T(8,128)(2,1)}, bf16[1,2048,1024]{2,1,0:T(8,128)(2,1)}, u32[]{:S(2)}, u32[]{:S(2)}) collective-permute-start(bf16[1,2048,1024]{2,1,0:T(8,128)(2,1)} %param.28), channel_id=1, source_target_pairs={{0,1},{1,0},{2,3},{3,2},{4,5},{5,4},{6,7},{7,6},{8,9},{9,8},{10,11... | collective-permute-start | bytes 12582920 | tf_op jit(solution)/shard_map/ppermute | solution.py:855
  121.7 43.6 %collective-permute-start.29 = (bf16[1,2048,1024]{2,1,0:T(8,128)(2,1)}, bf16[1,2048,1024]{2,1,0:T(8,128)(2,1)}, u32[]{:S(2)}, u32[]{:S(2)}) collective-permute-start(bf16[1,2048,1024]{2,1,0:T(8,128)(2,1)} %param.29), channel_id=1, source_target_pairs={{0,1},{1,0},{2,3},{3,2},{4,5},{5,4},{6,7},{7,6},{8,9},{9,8},{10,11... | collective-permute-start | bytes 12582920 | tf_op jit(solution)/shard_map/ppermute | solution.py:855
  135.8 40.0 %collective-permute-start.32 = (bf16[1,1024,2048]{2,1,0:T(8,128)(2,1)}, bf16[1,1024,2048]{2,1,0:T(8,128)(2,1)}, u32[]{:S(2)}, u32[]{:S(2)}) collective-permute-start(bf16[1,1024,2048]{2,1,0:T(8,128)(2,1)} %param.30), channel_id=1, source_target_pairs={{0,1},{1,0},{2,3},{3,2},{4,5},{5,4},{6,7},{7,6},{8,9},{9,8},{10,11... | collective-permute-start | bytes 12582920 | tf_op jit(solution)/shard_map/ppermute | solution.py:855
  193.2 35.7 %collective-permute-start.35 = (bf16[128,2176]{1,0:T(8,128)(2,1)S(1)}, bf16[128,2176]{1,0:T(8,128)(2,1)S(1)}, u32[]{:S(2)}, u32[]{:S(2)}) collective-permute-start(bf16[128,2176]{1,0:T(8,128)(2,1)S(1)} %collective-permute-done.33.refs_2_), channel_id=1, source_target_pairs={{0,4},{1,5},{4,8},{5,9},{8,12},{9,13},{12,14},{13,15},{14,10},{15,... | collective-permute-start | bytes 1671176 | tf_op jit(solution)/shard_map/ppermute | solution.py:849
  194.9 34.0 %collective-permute-start.36 = (bf16[128,2176]{1,0:T(8,128)(2,1)S(1)}, bf16[128,2176]{1,0:T(8,128)(2,1)S(1)}, u32[]{:S(2)}, u32[]{:S(2)}) collective-permute-start(bf16[128,2176]{1,0:T(8,128)(2,1)S(1)} %collective-permute-done.34.refs_1_), channel_id=1, source_target_pairs={{4,0},{5,1},{8,4},{9,5},{12,8},{13,9},{14,12},{15,13},{10,14},{11,... | collective-permute-start | bytes 1671176 | tf_op jit(solution)/shard_map/ppermute | solution.py:852
  194.9 33.9 %collective-permute-start.37 = (bf16[128,2048]{1,0:T(8,128)(2,1)}, bf16[128,2048]{1,0:T(8,128)(2,1)S(1)}, u32[]{:S(2)}, u32[]{:S(2)}) collective-permute-start(bf16[128,2048]{1,0:T(8,128)(2,1)} %copy-done.45), channel_id=1, source_target_pairs={{0,4},{1,5},{4,8},{5,9},{8,12},{9,13},{12,14},{13,15},{14,10},{15,... | collective-permute-start | bytes 1572872 | tf_op jit(solution)/shard_map/ppermute | solution.py:849
  196.4 32.4 %collective-permute-start.38 = (bf16[128,2048]{1,0:T(8,128)(2,1)}, bf16[128,2048]{1,0:T(8,128)(2,1)S(1)}, u32[]{:S(2)}, u32[]{:S(2)}) collective-permute-start(bf16[128,2048]{1,0:T(8,128)(2,1)} %copy-done.44), channel_id=1, source_target_pairs={{4,0},{5,1},{8,4},{9,5},{12,8},{13,9},{14,12},{15,13},{10,14},{11,... | collective-permute-start | bytes 1572872 | tf_op jit(solution)/shard_map/ppermute | solution.py:852
  228.9 28.3 %collective-permute-start.43 = (bf16[64,2048]{1,0:T(8,128)(2,1)S(1)}, bf16[64,2048]{1,0:T(8,128)(2,1)S(1)}, u32[]{:S(2)}, u32[]{:S(2)}) collective-permute-start(bf16[64,2048]{1,0:T(8,128)(2,1)S(1)} %slice.340), channel_id=1, source_target_pairs={{0,4},{1,5},{4,8},{5,9},{8,12},{9,13},{12,14},{13,15},{14,10},{15,... | collective-permute-start | bytes 786440 | tf_op jit(solution)/shard_map/ppermute | solution.py:849
  230.4 26.8 %collective-permute-start.44 = (bf16[64,2048]{1,0:T(8,128)(2,1)S(1)}, bf16[64,2048]{1,0:T(8,128)(2,1)S(1)}, u32[]{:S(2)}, u32[]{:S(2)}) collective-permute-start(bf16[64,2048]{1,0:T(8,128)(2,1)S(1)} %slice.341), channel_id=1, source_target_pairs={{4,0},{5,1},{8,4},{9,5},{12,8},{13,9},{14,12},{15,13},{10,14},{11,... | collective-permute-start | bytes 786440 | tf_op jit(solution)/shard_map/ppermute | solution.py:852
  230.5 25.1 %collective-permute-start.39 = (bf16[128,2176]{1,0:T(8,128)(2,1)S(1)}, bf16[128,2176]{1,0:T(8,128)(2,1)S(1)}, u32[]{:S(2)}, u32[]{:S(2)}) collective-permute-start(bf16[128,2176]{1,0:T(8,128)(2,1)S(1)} %collective-permute-done.36.refs_0_), channel_id=1, source_target_pairs={{4,0},{5,1},{8,4},{9,5},{12,8},{13,9},{14,12},{15,13},{10,14},{11,... | collective-permute-start | bytes 1671176 | tf_op jit(solution)/shard_map/ppermute | solution.py:852
  231.1 24.5 %collective-permute-start.40 = (bf16[128,2176]{1,0:T(8,128)(2,1)S(1)}, bf16[128,2176]{1,0:T(8,128)(2,1)S(1)}, u32[]{:S(2)}, u32[]{:S(2)}) collective-permute-start(bf16[128,2176]{1,0:T(8,128)(2,1)S(1)} %collective-permute-done.35.refs_1_), channel_id=1, source_target_pairs={{0,4},{1,5},{4,8},{5,9},{8,12},{9,13},{12,14},{13,15},{14,10},{15,... | collective-permute-start | bytes 1671176 | tf_op jit(solution)/shard_map/ppermute | solution.py:849
  311.1 33.4 %collective-permute-start.48 = (bf16[128,2176]{1,0:T(8,128)(2,1)}, bf16[128,2176]{1,0:T(8,128)(2,1)}, u32[]{:S(2)}, u32[]{:S(2)}) collective-permute-start(bf16[128,2176]{1,0:T(8,128)(2,1)} %pad_maximum_fusion.3), channel_id=1, source_target_pairs={{4,0},{5,1},{8,4},{9,5},{12,8},{13,9},{14,12},{15,13},{10,14},{11,... | collective-permute-start | bytes 1671176 | tf_op jit(solution)/shard_map/ppermute | solution.py:852
  311.6 35.2 %collective-permute-start.51 = (bf16[256,2048]{1,0:T(8,128)(2,1)}, bf16[256,2048]{1,0:T(8,128)(2,1)S(1)}, u32[]{:S(2)}, u32[]{:S(2)}) collective-permute-start(bf16[256,2048]{1,0:T(8,128)(2,1)} %get-tuple-element.322), channel_id=1, source_target_pairs={{0,1},{1,0},{2,3},{3,2},{4,5},{5,4},{6,7},{7,6},{8,9},{9,8},{10,11... | collective-permute-start | bytes 3145736 | tf_op jit(solution)/shard_map/ppermute | solution.py:855
  361.3 217.1 %reduce-scatter.6.cloned.1.call-start = ((), (), s32[]{:S(2)}) async-start(), calls=%async_computation.6 | async-start | bytes 6291456 | tf_op jit(solution)/shard_map/reduce_scatter | solution.py:1106
  397.6 180.9 %reduce-scatter.8.cloned.1.call-start = ((), (), s32[]{:S(2)}) async-start(), calls=%async_computation.7 | async-start | bytes 6291456 | tf_op jit(solution)/shard_map/reduce_scatter | solution.py:1106
  488.8 115.8 %collective-permute-start.114 = (bf16[128,2048]{1,0:T(8,128)(2,1)}, bf16[128,2048]{1,0:T(8,128)(2,1)S(1)}, u32[]{:S(2)}, u32[]{:S(2)}) collective-permute-start(bf16[128,2048]{1,0:T(8,128)(2,1)} %fusion.8), channel_id=1, source_target_pairs={{0,16},{16,0},{1,17},{17,1},{2,18},{18,2},{3,19},{19,3},{4,20},{20... | collective-permute-start | bytes 1572872 | tf_op jit(solution)/shard_map/ppermute | solution.py:858
  495.5 34.7 %collective-permute-start.96 = (f32[17,2048]{1,0:T(8,128)S(1)}, f32[17,2048]{1,0:T(8,128)}, u32[]{:S(2)}, u32[]{:S(2)}) collective-permute-start(f32[17,2048]{1,0:T(8,128)S(1)} %add.447), channel_id=1, source_target_pairs={{0,8},{1,9},{2,10},{3,11},{4,12},{5,13},{6,14},{7,15},{8,0},{9,1},... | collective-permute-start | bytes 417800 | tf_op jit(solution)/shard_map/ppermute | solution.py:1150
  540.7 23.8 %collective-permute-start.104 = (bf16[384,1024]{1,0:T(8,128)(2,1)S(1)}, bf16[384,1024]{1,0:T(8,128)(2,1)S(1)}, u32[]{:S(2)}, u32[]{:S(2)}) collective-permute-start(bf16[384,1024]{1,0:T(8,128)(2,1)S(1)} %pad_maximum_fusion), channel_id=1, source_target_pairs={{0,16},{16,0},{1,17},{17,1},{2,18},{18,2},{3,19},{19,3},{4,20},{20... | collective-permute-start | bytes 2359304 | tf_op jit(solution)/shard_map/ppermute | solution.py:858
  540.8 25.7 %collective-permute-start.99 = (f32[3,2048]{1,0:T(4,128)S(1)}, f32[3,2048]{1,0:T(4,128)S(1)}, u32[]{:S(2)}, u32[]{:S(2)}) collective-permute-start(f32[3,2048]{1,0:T(4,128)S(1)} %fusion.50), channel_id=1, source_target_pairs={{0,4},{1,5},{2,6},{3,7},{4,0},{5,1},{6,2},{7,3},{8,12},{9,13},{10,... | collective-permute-start | bytes 73736 | tf_op jit(solution)/shard_map/ppermute | solution.py:1150
  544.5 21.9 %collective-permute-start.97 = (bf16[128,2048]{1,0:T(8,128)(2,1)}, bf16[128,2048]{1,0:T(8,128)(2,1)}, u32[]{:S(2)}, u32[]{:S(2)}) collective-permute-start(bf16[128,2048]{1,0:T(8,128)(2,1)} %get-tuple-element.418), channel_id=1, source_target_pairs={{0,4},{1,5},{4,8},{5,9},{8,12},{9,13},{12,14},{13,15},{14,10},{15,... | collective-permute-start | bytes 1572872 | tf_op jit(solution)/shard_map/ppermute | solution.py:849
  564.5 37.9 %collective-permute-start.109 = (f32[17,2048]{1,0:T(8,128)S(1)}, f32[17,2048]{1,0:T(8,128)}, u32[]{:S(2)}, u32[]{:S(2)}) collective-permute-start(f32[17,2048]{1,0:T(8,128)S(1)} %add.464), channel_id=1, source_target_pairs={{0,16},{16,0},{1,17},{17,1},{2,18},{18,2},{3,19},{19,3},{4,20},{20... | collective-permute-start | bytes 417800 | tf_op jit(solution)/shard_map/ppermute | solution.py:858
  572.5 29.9 %all-to-all-start.1 = ((bf16[16,64,384]{2,1,0:T(8,128)(2,1)}), bf16[16,64,384]{2,1,0:T(8,128)(2,1)S(1)}, u32[]{:S(2)}, u32[]{:S(2)}) async-start(bf16[16,64,384]{2,1,0:T(8,128)(2,1)} %bitcast.65), calls=%async_computation.1 | async-start | bytes 1572864 | tf_op jit(solution)/shard_map/all_to_all | solution.py:1270
  (168 other events, 1786.0 us)
Sparse Core Ops, SparseCore 0:
  361.4 53.0 reduce-scatter.3
  416.9 54.2 reduce-scatter.5
  485.0 68.4 reduce-scatter.7

commit v4 on v3

--- a/solution.py
+++ b/solution.py
@@ -525,6 +525,16 @@
     grad = dot(joined(x_refs), w_ref[...], NT).astype(B16)
     own_ref[...] = grad[:, :hd].reshape(own_ref.shape)
     other_ref[...] = grad[:, hd:].reshape(other_ref.shape)
+
+
+def slab_kernel(ids_ref, *refs):
+    w_refs, out_ref = refs[:-1], refs[-1]
+    chips, rows, wide = out_ref.shape
+    hd = wide // len(w_refs)
+    for c in range(chips):
+        spot = pl.ds(pl.multiple_of((2 * c + ids_ref[0]) * hd, hd), hd)
+        for i, w_ref in enumerate(w_refs):
+            out_ref[c, :, i * hd : (i + 1) * hd] = w_ref[:, spot]
 
 
 def on_core(kernel, shapes, operands, flops, scratch=()):
@@ -955,11 +965,12 @@
     inputs = tokens.astype(F32)
     n1 = by_parity(norm_rows(inputs, norm_attn).astype(B16), 1)
 
-    slabs = []
-    for w in (w_query, w_key, w_value):
-        pair = w.reshape(rows, chips, 2, hd)
-        slabs.append(jnp.where(group == 0, pair[:, :, 0], pair[:, :, 1]))
-    slab = jnp.concatenate(slabs, axis=2).transpose(1, 0, 2)
+    slab = on_core(
+        slab_kernel,
+        jax.ShapeDtypeStruct((chips, rows, 3 * hd), B16),
+        [group[None].astype(jnp.int32), w_query, w_key, w_value],
+        0,
+    )
     first = (to_right(n1), to_left(n1))
     near_head = lax.all_to_all(slab, "ctx", split_axis=0, concat_axis=0, axis_index_groups=same_core, tiled=True)
     far_head = group_swap(near_head)
@@ -1117,7 +1128,7 @@
         return run
 
     n2_sum = total_of(
-        ring_sum(lambda o: dn2_part[o], 1, [other_term(0), other_term(1), own_term(0), other_term(2)])
+        ring_sum(lambda o: dn2_part[o], 1, [other_term(0), own_term(0), other_term(1), other_term(2)])
     )
     dgates = n2_sum[:, width : width + 3 * experts].reshape(rows, 3, experts)
     n2_sum = n2_sum[:, :width]
@@ -1255,7 +1266,11 @@
 
     early = []
 
+    expert_done = []
+
     def swap_heads(early_recv, w_own, *w_away):
+        expert_done.extend(w_away[4:])
+        w_away = w_away[:4]
         early.append(group_swap(early_sum + early_recv))
         early.append(early_sum + early_recv)
         w_away = [core_swap(v) for v in w_away]
@@ -1284,17 +1299,17 @@
         lambda o: n1_part[offsets.index(o)],
         1,
         [
-            None,
-            small_step(2, lambda token: [early_recv] + list(heads_grads(token)), swap_heads),
-            small_step(4, lambda token: [in_slabs(kept_by(group) + after(w_got[1], token).astype(F32))], join),
+            lambda token: ([early_recv] + list(heads_grads(n1_part)) + expert_grads, swap_heads),
+            small_step(2, lambda token: [in_slabs(kept_by(group) + after(w_got[1], token).astype(F32))], join),
+            small_step(4),
             small_step(
                 8,
-                lambda token: w_got[2:] + [v.astype(F32)[None] for v in tied(expert_grads, token)],
-                lambda w, *v: grads_out.extend((w,) + v),
+                lambda token: [after(v, token).astype(F32)[None] for v in expert_done] + w_got[2:],
+                lambda *v: grads_out.extend(v),
             ),
         ],
     )
-    w_got, down_grad_out, gate_grad_out, up_grad_out = grads_out
+    down_grad_out, gate_grad_out, up_grad_out, w_got = grads_out
     o_head = (o_head + after(o_recv, n1_grad[0]).astype(F32)).astype(B16)
     wo_grad = None
     for i in range(2):

time: 636 us -> 634 us (level)
  starting transfers between devices: 152 us -> 143 us
    all_to_all x1, waiting for transfers between devices: 14.4 us -> 0.01 us  [join(): lax.all_to_all(w_mine, 'ctx', split_axis=0, concat_axis=0, tiled=True)]
    ppermute x34, starting transfers between devices: 67 us -> 54 us  [core_swap(): return lax.ppermute(v, 'ctx', [(i, i ^ 1) for i in range(devices)])]
    ppermute x32, waiting for transfers between devices: 60.1 us -> 72.5 us  [to_right(): return lax.ppermute(v, 'ctx', right)]
    unnamed x149 -> x165, local copies, waits for them, and re-layouts: 15.2 us -> 18.4 us
    pallas_call x12 -> x13, Pallas kernels: 73.4 us -> 76.2 us  [on_core(): pl.pallas_call(kernel, in_specs=[pl.BlockSpec(memory_space=m) for m in me...]
  transfers between devices with their start and end apart: 122 -> 122, of which waited for: 41 -> 42; matrix products, arithmetic and copies ran while one was open for 12% -> 13% of each run, Pallas kernels for 30% -> 31%
where the time goes in v4:
time: 634 us; the launch traced here: 624 us
  Pallas kernels  225 us (35%)
  starting transfers between devices  143 us (23%)
  waiting for transfers between devices  140 us (22%)
  other arithmetic  52.8 us (8%)
  local copies, waits for them, and re-layouts  43.3 us (7%)
  between operations  15.7 us (2%)
    pallas_call x3, Pallas kernels, expert_rows(): pl.pallas_call(functools.partial(expert_kernel, shards=shards, experts=ex...  88 us
    pallas_call x13, Pallas kernels, on_core(): pl.pallas_call(kernel, in_specs=[pl.BlockSpec(memory_space=m) for m in me...  76.2 us
    ppermute x32, waiting for transfers between devices, to_right(): return lax.ppermute(v, 'ctx', right)  72.5 us
    pallas_call x6, Pallas kernels, expert_grad_term(): pl.pallas_call(functools.partial(expert_grad_kernel, pieces=pieces, whole...  61.1 us
    ppermute x34, starting transfers between devices, core_swap(): return lax.ppermute(v, 'ctx', [(i, i ^ 1) for i in range(devices)])  54 us
    ppermute x32, starting transfers between devices, to_left(): return lax.ppermute(v, 'ctx', left)  27.1 us
    ppermute x32, starting transfers between devices, to_right(): return lax.ppermute(v, 'ctx', right)  24.1 us
    unnamed x165, local copies, waits for them, and re-layouts  18.4 us
  transfers between devices with their start and end apart: 122, of which 42 were waited for; matrix products, arithmetic and copies ran while one was open for 13% of the time, Pallas kernels for 31%

profile of v4, /device:TPU:9, one launch (start us, length us, event | category | flops | bytes accessed | tf_op | source)
XLA Modules:
  0.0 623.7 jit_solution(8552307174716767064)
XLA Ops:
  16.9 15.5 %all-to-all-done = bf16[8,128,384]{2,1,0:T(8,128)(2,1)S(1)} async-done(((bf16[8,128,384]{2,1,0:T(8,128)(2,1)}), bf16[8,128,384]{2,1,0:T(8,128)(2,1)S(1)}, u32[]{:S(2)}, u32[]{:S(2)}) %all-to-all-start) | async-done | bytes 786464 | tf_op jit(solution)/shard_map/all_to_all | solution.py:975
  36.2 9.6 %collective-permute-done.refs_2_.refs_15_.refs_4_ = bf16[128,2048]{1,0:T(8,128)(2,1)S(1)} collective-permute-done((bf16[128,2048]{1,0:T(8,128)(2,1)S(1)}, bf16[128,2048]{1,0:T(8,128)(2,1)S(1)}, u32[]{:S(2)}, u32[]{:S(2)}) %collective-permute-start) | collective-permute-done | bytes 524320 | tf_op jit(solution)/shard_map/ppermute | solution.py:859
  54.1 6.6 %collective-permute-done.2.refs_3_.refs_16_.refs_5_ = bf16[128,2048]{1,0:T(8,128)(2,1)} collective-permute-done((bf16[128,2048]{1,0:T(8,128)(2,1)}, bf16[128,2048]{1,0:T(8,128)(2,1)}, u32[]{:S(2)}, u32[]{:S(2)}) %collective-permute-start.2) | collective-permute-done | bytes 524320 | tf_op jit(solution)/shard_map/ppermute | solution.py:862
  66.1 6.5 %shard_map.264 = (f32[5,128,384]{2,1,0:T(8,128)}, f32[5,128,384]{2,1,0:T(8,128)}, f32[16,128]{1,0:T(8,128)}) custom-call(s32[9]{0:T(128)} %concatenate.85.ids_ref, bf16[128,2048]{1,0:T(8,128)(2,1)} %bitcast.171, bf16[128,2048]{1,0:T(8,128)(2,1)} %collective-permute-done.1.refs_1_.refs_14_.refs_3_, bf16[128,2048]{1,0:T(8,128)(2,1)} %copy-done.46, ...), custom_call_target="tpu_custom_call" | custom-call | flops 2013265920 | bytes 7741476 | tf_op jit(solution)/shard_map/pallas_call | solution.py:544
  105.9 8.5 %collective-permute-start.16 = (bf16[8,128,384]{2,1,0:T(8,128)(2,1)}, bf16[8,128,384]{2,1,0:T(8,128)(2,1)S(1)}, u32[]{:S(2)}, u32[]{:S(2)}) collective-permute-start(bf16[8,128,384]{2,1,0:T(8,128)(2,1)} %get-tuple-element.256), channel_id=1, source_target_pairs={{0,1},{1,0},{2,3},{3,2},{4,5},{5,4},{6,7},{7,6},{8,9},{9,8},{10,11... | collective-permute-start | bytes 2359304 | tf_op jit(solution)/shard_map/ppermute | solution.py:865
  119.5 9.3 %shard_map.267 = (f32[2048,128]{1,0:T(8,128)}, f32[1,2048]{1,0:T(1,128)}, bf16[2048,384]{1,0:T(8,128)(2,1)}, bf16[8,128,128]{2,1,0:T(8,128)(2,1)}, bf16[8,128,128]{2,1,0:T(8,128)(2,1)}) custom-call(s32[9]{0:T(128)} %concatenate.85.ids_ref, bf16[8,128,384]{2,1,0:T(8,128)(2,1)} %get-tuple-element.255.mine_ref, bf16[8,128,384]{2,1,0:T(8,128)(2,1)} %copy-done.70, ...), custom_call_target="tpu_custom_call" | custom-call | flops 2147483648 | bytes 4735012 | tf_op jit(solution)/shard_map/pallas_call | solution.py:544
  179.8 6.8 %collective-permute-done.33.refs_2_ = bf16[128,2176]{1,0:T(8,128)(2,1)S(1)} collective-permute-done((bf16[128,2176]{1,0:T(8,128)(2,1)S(1)}, bf16[128,2176]{1,0:T(8,128)(2,1)S(1)}, u32[]{:S(2)}, u32[]{:S(2)}) %collective-permute-start.33) | collective-permute-done | bytes 557088 | tf_op jit(solution)/shard_map/ppermute | solution.py:859
  190.7 32.4 %shard_map.268 = (bf16[3,128,2048]{2,1,0:T(8,128)(2,1)}, bf16[3,128,2176]{2,1,0:T(8,128)(2,1)}, bf16[8,128,2048]{2,1,0:T(8,128)(2,1)}, bf16[8,128,2048]{2,1,0:T(...) custom-call(s32[2]{0:T(128)} %pad_add_fusion.ids_ref, ...), custom_call_target="tpu_custom_call" | custom-call | flops 19327352832 | bytes 25165824 | tf_op jit(solution)/shard_map/pallas_call | solution.py:717
  226.4 23.3 %shard_map.269 = (bf16[2,128,2048]{2,1,0:T(8,128)(2,1)}, bf16[2,128,2176]{2,1,0:T(8,128)(2,1)}, bf16[8,128,2048]{2,1,0:T(8,128)(2,1)}, bf16[8,128,2048]{2,1,0:T(...) custom-call(s32[2]{0:T(128)} %pad_add_fusion.ids_ref, ...), custom_call_target="tpu_custom_call", output_to_operand_aliasing={{2}: (8, {}), {3}: (9, {}), {4}: (10, {}), {5}: (11, {}), {... | custom-call | flops 12884901888 | bytes 25165824 | tf_op jit(solution)/shard_map/pallas_call | solution.py:717
  257.2 32.3 %shard_map.270 = (bf16[3,128,2048]{2,1,0:T(8,128)(2,1)}, bf16[3,128,2176]{2,1,0:T(8,128)(2,1)}, bf16[8,128,2048]{2,1,0:T(8,128)(2,1)}, bf16[8,128,2048]{2,1,0:T(...) custom-call(s32[2]{0:T(128)} %pad_add_fusion.ids_ref, ...), custom_call_target="tpu_custom_call", output_to_operand_aliasing={{2}: (10, {}), {3}: (11, {}), {4}: (12, {}), {5}: (13, {}),... | custom-call | flops 19327352832 | bytes 25165824 | tf_op jit(solution)/shard_map/pallas_call | solution.py:717
  293.0 10.0 %shard_map.271 = (bf16[256,2048]{1,0:T(8,128)(2,1)}, bf16[256,2048]{1,0:T(8,128)(2,1)}, bf16[256,2048]{1,0:T(8,128)(2,1)}, bf16[256,2048]{1,0:T(8,128)(2,1)}) custom-call(bf16[1024,2048]{1,0:T(8,128)(2,1)} %bitcast.154, bf16[1024,2048]{1,0:T(8,128)(2,1)} %bitcast.160), custom_call_target="tpu_custom_call" | custom-call | flops 4294967296 | bytes 10485760 | tf_op jit(solution)/shard_map/pallas_call | solution.py:805
  303.7 15.6 %collective-permute-start.49 = (bf16[256,2048]{1,0:T(8,128)(2,1)}, bf16[256,2048]{1,0:T(8,128)(2,1)S(1)}, u32[]{:S(2)}, u32[]{:S(2)}) collective-permute-start(bf16[256,2048]{1,0:T(8,128)(2,1)} %get-tuple-element.313), channel_id=1, source_target_pairs={{0,1},{1,0},{2,3},{3,2},{4,5},{5,4},{6,7},{7,6},{8,9},{9,8},{10,11... | collective-permute-start | bytes 3145736 | tf_op jit(solution)/shard_map/ppermute | solution.py:865
  327.3 10.4 %shard_map.272 = bf16[1024,2048]{1,0:T(8,128)(2,1)} custom-call(bf16[1024,2048]{1,0:T(8,128)(2,1)} %bitcast.155, bf16[1024,2048]{1,0:T(8,128)(2,1)} %bitcast.161, bf16[256,2048]{1,0:T(8,128)(2,1)} %copy-done.28, bf16[256,2048]{1,0:T(8,128)(2,1)} %copy-done.29, bf16[256,2048]{1,0:T(8,128)(2,1)} %copy-done.30, bf16[256,2048]{1,0:T(8,128)(2,1)} %copy-done.31), custom_call_target="tpu_custom_call" | custom-call | flops 4294967296 | bytes 10485760 | tf_op jit(solution)/shard_map/pallas_call | solution.py:805
  341.8 10.2 %shard_map.273 = (bf16[512,1024]{1,0:T(8,128)(2,1)}, bf16[512,1024]{1,0:T(8,128)(2,1)}, bf16[512,1024]{1,0:T(8,128)(2,1)}, bf16[512,1024]{1,0:T(8,128)(2,1)}) custom-call(bf16[1024,2048]{1,0:T(8,128)(2,1)} %bitcast.150, bf16[1024,2048]{1,0:T(8,128)(2,1)} %bitcast.156), custom_call_target="tpu_custom_call" | custom-call | flops 4294967296 | bytes 10485760 | tf_op jit(solution)/shard_map/pallas_call | solution.py:805
  358.1 9.5 %shard_map.274 = (bf16[512,1024]{1,0:T(8,128)(2,1)}, bf16[512,1024]{1,0:T(8,128)(2,1)}, bf16[512,1024]{1,0:T(8,128)(2,1)}, bf16[512,1024]{1,0:T(8,128)(2,1)}) custom-call(bf16[1024,2048]{1,0:T(8,128)(2,1)} %bitcast.151, bf16[1024,2048]{1,0:T(8,128)(2,1)} %bitcast.158), custom_call_target="tpu_custom_call" | custom-call | flops 4294967296 | bytes 10485760 | tf_op jit(solution)/shard_map/pallas_call | solution.py:805
  375.1 10.1 %shard_map.275 = bf16[2048,1024]{1,0:T(8,128)(2,1)} custom-call(bf16[1024,2048]{1,0:T(8,128)(2,1)} %bitcast.152, bf16[1024,2048]{1,0:T(8,128)(2,1)} %bitcast.157, bf16[512,1024]{1,0:T(8,128)(2,1)} %collective-permute-done.59.refs_0_, bf16[512,1024]{1,0:T(8,128)(2,1)} %collective-permute-done.60.refs_1_, bf16[512,1024]{1,0:T(8,128)(2,1)} %collective-permute-done.61.refs_2_, ...), custom_call_target="tpu_custom_call" | custom-call | flops 4294967296 | bytes 10485760 | tf_op jit(solution)/shard_map/pallas_call | solution.py:805
  397.2 10.8 %shard_map.276 = bf16[2048,1024]{1,0:T(8,128)(2,1)} custom-call(bf16[1024,2048]{1,0:T(8,128)(2,1)} %bitcast.153, bf16[1024,2048]{1,0:T(8,128)(2,1)} %bitcast.159, bf16[512,1024]{1,0:T(8,128)(2,1)} %copy-done.32, bf16[512,1024]{1,0:T(8,128)(2,1)} %copy-done.33, bf16[512,1024]{1,0:T(8,128)(2,1)} %copy-done.34, bf16[512,1024]{1,0:T(8,128)(2,1)} %copy-done.35), custom_call_target="tpu_custom_call" | custom-call | flops 4294967296 | bytes 10485760 | tf_op jit(solution)/shard_map/pallas_call | solution.py:805
  411.1 10.3 %collective-permute-done.69.refs_1_.refs_8_ = bf16[128,2048]{1,0:T(8,128)(2,1)S(1)} collective-permute-done((bf16[128,2048]{1,0:T(8,128)(2,1)S(1)}, bf16[128,2048]{1,0:T(8,128)(2,1)S(1)}, u32[]{:S(2)}, u32[]{:S(2)}) %collective-permute-start.69) | collective-permute-done | bytes 524320 | tf_op jit(solution)/shard_map/ppermute | solution.py:859
  443.6 9.8 %shard_map.279 = (f32[8,128,384]{2,1,0:T(8,128)}, bf16[8,128,384]{2,1,0:T(8,128)(2,1)}) custom-call(s32[9]{0:T(128)} %concatenate.85.ids_ref, bf16[2048,384]{1,0:T(8,128)(2,1)} %get-tuple-element.278.qkv_ref, bf16[5,128,128]{2,1,0:T(8,128)(2,1)} %get-tuple-element.358.refs_0_, bf16[3,128,128]{2,1,0:T(8,128)(2,1)} %get-tuple-element.363.refs_1_, ...), custom_call_target="tpu_custom_call" | custom-call | flops 5368709120 | bytes 5521444 | tf_op jit(solution)/shard_map/pallas_call | solution.py:544
  490.7 12.0 %shard_map.282 = (bf16[8,128,384]{2,1,0:T(8,128)(2,1)}, bf16[8,128,384]{2,1,0:T(8,128)(2,1)}, bf16[8,128,2048]{2,1,0:T(8,128)(2,1)}, f32[8,2048]{1,0:T(8,128)}) custom-call(s32[9]{0:T(128)} %concatenate.85.ids_ref, f32[8,128,384]{2,1,0:T(8,128)} %get-tuple-element.372.grad_own, bf16[8,128,384]{2,1,0:T(8,128)(2,1)} %copy-done.16, ...), custom_call_target="tpu_custom_call" | custom-call | flops 3221225472 | bytes 19750948 | tf_op jit(solution)/shard_map/pallas_call | solution.py:544
  514.7 7.1 %shard_map.283 = (f32[384,2048]{1,0:T(8,128)}, bf16[384,512]{1,0:T(8,128)(2,1)}, bf16[384,512]{1,0:T(8,128)(2,1)}, bf16[384,512]{1,0:T(8,128)(2,1)}, bf16[384,512]{1,0:T(8,128)(2,1)}) custom-call(bf16[8,128,384]{2,1,0:T(8,128)(2,1)} %get-tuple-element.404.refs_0_, bf16[8,128,384]{2,1,0:T(8,128)(2,1)} %get-tuple-element.406.refs_1_, ...), custom_call_target="tpu_custom_call" | custom-call | flops 3221225472 | bytes 10485760 | tf_op jit(solution)/shard_map/pallas_call | solution.py:544
  533.9 13.4 %collective-permute-done.101 = bf16[384,1024]{1,0:T(8,128)(2,1)S(1)} collective-permute-done((bf16[384,1024]{1,0:T(8,128)(2,1)S(1)}, bf16[384,1024]{1,0:T(8,128)(2,1)S(1)}, u32[]{:S(2)}, u32[]{:S(2)}) %collective-permute-start.101) | collective-permute-done | bytes 786464 | tf_op jit(solution)/shard_map/ppermute | solution.py:868
  557.6 7.3 %all-to-all-start.1 = ((bf16[16,64,384]{2,1,0:T(8,128)(2,1)}), bf16[16,64,384]{2,1,0:T(8,128)(2,1)S(1)}, u32[]{:S(2)}, u32[]{:S(2)}) async-start(bf16[16,64,384]{2,1,0:T(8,128)(2,1)} %bitcast.60), calls=%async_computation.4 | async-start | bytes 1572864 | tf_op jit(solution)/shard_map/all_to_all | solution.py:1285
  583.6 11.2 %collective-permute-done.105.there_ref = bf16[128,2048]{1,0:T(8,128)(2,1)S(1)} collective-permute-done((bf16[128,2048]{1,0:T(8,128)(2,1)S(1)}, bf16[128,2048]{1,0:T(8,128)(2,1)S(1)}, u32[]{:S(2)}, u32[]{:S(2)}) %collective-permute-start.105) | collective-permute-done | bytes 524320 | tf_op jit(solution)/shard_map/ppermute | solution.py:859
  (564 shorter events, 309.5 us)
Async XLA Ops:
  9.7 22.7 %all-to-all-start = ((bf16[8,128,384]{2,1,0:T(8,128)(2,1)}), bf16[8,128,384]{2,1,0:T(8,128)(2,1)S(1)}, u32[]{:S(2)}, u32[]{:S(2)}) async-start(bf16[8,128,384]{2,1,0:T(8,128)(2,1)} %shard_map.263), calls=%async_computation | async-start | bytes 1572864 | tf_op jit(solution)/shard_map/all_to_all | solution.py:975
  15.4 506.4 %reduce-scatter.4.cloned.1.call-start = ((), (), s32[]{:S(2)}) async-start(), calls=%async_computation.5 | async-start | bytes 6291456 | tf_op jit(solution)/shard_map/reduce_scatter | solution.py:1117
  62.2 84.3 %collective-permute-start.26 = (bf16[1,2048,1024]{2,1,0:T(8,128)(2,1)}, bf16[1,2048,1024]{2,1,0:T(8,128)(2,1)}, u32[]{:S(2)}, u32[]{:S(2)}) collective-permute-start(bf16[1,2048,1024]{2,1,0:T(8,128)(2,1)} %param.28), channel_id=1, source_target_pairs={{0,1},{1,0},{2,3},{3,2},{4,5},{5,4},{6,7},{7,6},{8,9},{9,8},{10,11... | collective-permute-start | bytes 12582920 | tf_op jit(solution)/shard_map/ppermute | solution.py:865
  115.6 44.0 %collective-permute-start.29 = (bf16[1,2048,1024]{2,1,0:T(8,128)(2,1)}, bf16[1,2048,1024]{2,1,0:T(8,128)(2,1)}, u32[]{:S(2)}, u32[]{:S(2)}) collective-permute-start(bf16[1,2048,1024]{2,1,0:T(8,128)(2,1)} %param.29), channel_id=1, source_target_pairs={{0,1},{1,0},{2,3},{3,2},{4,5},{5,4},{6,7},{7,6},{8,9},{9,8},{10,11... | collective-permute-start | bytes 12582920 | tf_op jit(solution)/shard_map/ppermute | solution.py:865
  129.8 40.1 %collective-permute-start.32 = (bf16[1,1024,2048]{2,1,0:T(8,128)(2,1)}, bf16[1,1024,2048]{2,1,0:T(8,128)(2,1)}, u32[]{:S(2)}, u32[]{:S(2)}) collective-permute-start(bf16[1,1024,2048]{2,1,0:T(8,128)(2,1)} %param.30), channel_id=1, source_target_pairs={{0,1},{1,0},{2,3},{3,2},{4,5},{5,4},{6,7},{7,6},{8,9},{9,8},{10,11... | collective-permute-start | bytes 12582920 | tf_op jit(solution)/shard_map/ppermute | solution.py:865
  187.7 35.4 %collective-permute-start.35 = (bf16[128,2176]{1,0:T(8,128)(2,1)S(1)}, bf16[128,2176]{1,0:T(8,128)(2,1)S(1)}, u32[]{:S(2)}, u32[]{:S(2)}) collective-permute-start(bf16[128,2176]{1,0:T(8,128)(2,1)S(1)} %collective-permute-done.33.refs_2_), channel_id=1, source_target_pairs={{0,4},{1,5},{4,8},{5,9},{8,12},{9,13},{12,14},{13,15},{14,10},{15,... | collective-permute-start | bytes 1671176 | tf_op jit(solution)/shard_map/ppermute | solution.py:859
  188.5 34.6 %collective-permute-start.36 = (bf16[128,2176]{1,0:T(8,128)(2,1)S(1)}, bf16[128,2176]{1,0:T(8,128)(2,1)S(1)}, u32[]{:S(2)}, u32[]{:S(2)}) collective-permute-start(bf16[128,2176]{1,0:T(8,128)(2,1)S(1)} %collective-permute-done.34.refs_1_), channel_id=1, source_target_pairs={{4,0},{5,1},{8,4},{9,5},{12,8},{13,9},{14,12},{15,13},{10,14},{11,... | collective-permute-start | bytes 1671176 | tf_op jit(solution)/shard_map/ppermute | solution.py:862
  189.2 33.9 %collective-permute-start.37 = (bf16[128,2048]{1,0:T(8,128)(2,1)}, bf16[128,2048]{1,0:T(8,128)(2,1)S(1)}, u32[]{:S(2)}, u32[]{:S(2)}) collective-permute-start(bf16[128,2048]{1,0:T(8,128)(2,1)} %copy-done.45), channel_id=1, source_target_pairs={{0,4},{1,5},{4,8},{5,9},{8,12},{9,13},{12,14},{13,15},{14,10},{15,... | collective-permute-start | bytes 1572872 | tf_op jit(solution)/shard_map/ppermute | solution.py:859
  190.1 33.0 %collective-permute-start.38 = (bf16[128,2048]{1,0:T(8,128)(2,1)}, bf16[128,2048]{1,0:T(8,128)(2,1)S(1)}, u32[]{:S(2)}, u32[]{:S(2)}) collective-permute-start(bf16[128,2048]{1,0:T(8,128)(2,1)} %copy-done.44), channel_id=1, source_target_pairs={{4,0},{5,1},{8,4},{9,5},{12,8},{13,9},{14,12},{15,13},{10,14},{11,... | collective-permute-start | bytes 1572872 | tf_op jit(solution)/shard_map/ppermute | solution.py:862
  223.2 28.3 %collective-permute-start.43 = (bf16[64,2048]{1,0:T(8,128)(2,1)S(1)}, bf16[64,2048]{1,0:T(8,128)(2,1)S(1)}, u32[]{:S(2)}, u32[]{:S(2)}) collective-permute-start(bf16[64,2048]{1,0:T(8,128)(2,1)S(1)} %slice.316), channel_id=1, source_target_pairs={{0,4},{1,5},{4,8},{5,9},{8,12},{9,13},{12,14},{13,15},{14,10},{15,... | collective-permute-start | bytes 786440 | tf_op jit(solution)/shard_map/ppermute | solution.py:859
  224.2 27.3 %collective-permute-start.44 = (bf16[64,2048]{1,0:T(8,128)(2,1)S(1)}, bf16[64,2048]{1,0:T(8,128)(2,1)S(1)}, u32[]{:S(2)}, u32[]{:S(2)}) collective-permute-start(bf16[64,2048]{1,0:T(8,128)(2,1)S(1)} %slice.317), channel_id=1, source_target_pairs={{4,0},{5,1},{8,4},{9,5},{12,8},{13,9},{14,12},{15,13},{10,14},{11,... | collective-permute-start | bytes 786440 | tf_op jit(solution)/shard_map/ppermute | solution.py:862
  224.7 25.0 %collective-permute-start.39 = (bf16[128,2176]{1,0:T(8,128)(2,1)S(1)}, bf16[128,2176]{1,0:T(8,128)(2,1)S(1)}, u32[]{:S(2)}, u32[]{:S(2)}) collective-permute-start(bf16[128,2176]{1,0:T(8,128)(2,1)S(1)} %collective-permute-done.36.refs_0_), channel_id=1, source_target_pairs={{4,0},{5,1},{8,4},{9,5},{12,8},{13,9},{14,12},{15,13},{10,14},{11,... | collective-permute-start | bytes 1671176 | tf_op jit(solution)/shard_map/ppermute | solution.py:862
  225.4 24.4 %collective-permute-start.40 = (bf16[128,2176]{1,0:T(8,128)(2,1)S(1)}, bf16[128,2176]{1,0:T(8,128)(2,1)S(1)}, u32[]{:S(2)}, u32[]{:S(2)}) collective-permute-start(bf16[128,2176]{1,0:T(8,128)(2,1)S(1)} %collective-permute-done.35.refs_1_), channel_id=1, source_target_pairs={{0,4},{1,5},{4,8},{5,9},{8,12},{9,13},{12,14},{13,15},{14,10},{15,... | collective-permute-start | bytes 1671176 | tf_op jit(solution)/shard_map/ppermute | solution.py:859
  337.7 184.2 %reduce-scatter.6.cloned.1.call-start = ((), (), s32[]{:S(2)}) async-start(), calls=%async_computation.6 | async-start | bytes 6291456 | tf_op jit(solution)/shard_map/reduce_scatter | solution.py:1117
  355.9 18.8 %collective-permute-start.59 = (bf16[512,1024]{1,0:T(8,128)(2,1)}, bf16[512,1024]{1,0:T(8,128)(2,1)}, u32[]{:S(2)}, u32[]{:S(2)}) collective-permute-start(bf16[512,1024]{1,0:T(8,128)(2,1)} %get-tuple-element.343), channel_id=1, source_target_pairs={{0,1},{1,0},{2,3},{3,2},{4,5},{5,4},{6,7},{7,6},{8,9},{9,8},{10,11... | collective-permute-start | bytes 3145736 | tf_op jit(solution)/shard_map/ppermute | solution.py:865
  387.7 134.2 %reduce-scatter.8.cloned.1.call-start = ((), (), s32[]{:S(2)}) async-start(), calls=%async_computation.7 | async-start | bytes 6291456 | tf_op jit(solution)/shard_map/reduce_scatter | solution.py:1117
  483.9 114.2 %collective-permute-start.114 = (bf16[128,2048]{1,0:T(8,128)(2,1)}, bf16[128,2048]{1,0:T(8,128)(2,1)S(1)}, u32[]{:S(2)}, u32[]{:S(2)}) collective-permute-start(bf16[128,2048]{1,0:T(8,128)(2,1)} %fusion.8), channel_id=1, source_target_pairs={{0,16},{16,0},{1,17},{17,1},{2,18},{18,2},{3,19},{19,3},{4,20},{20... | collective-permute-start | bytes 1572872 | tf_op jit(solution)/shard_map/ppermute | solution.py:868
  488.3 33.5 %collective-permute-start.92 = (f32[17,2048]{1,0:T(8,128)S(1)}, f32[17,2048]{1,0:T(8,128)S(1)}, u32[]{:S(2)}, u32[]{:S(2)}) collective-permute-start(f32[17,2048]{1,0:T(8,128)S(1)} %add.444), channel_id=1, source_target_pairs={{0,8},{1,9},{2,10},{3,11},{4,12},{5,13},{6,14},{7,15},{8,0},{9,1},... | collective-permute-start | bytes 417800 | tf_op jit(solution)/shard_map/ppermute | solution.py:1161
  524.7 24.5 %collective-permute-start.96 = (f32[3,2048]{1,0:T(4,128)}, f32[3,2048]{1,0:T(4,128)}, u32[]{:S(2)}, u32[]{:S(2)}) collective-permute-start(f32[3,2048]{1,0:T(4,128)} %fusion.18), channel_id=1, source_target_pairs={{0,2},{1,3},{2,0},{3,1},{4,6},{5,7},{6,4},{7,5},{8,10},{9,11},{10,... | collective-permute-start | bytes 73736 | tf_op jit(solution)/shard_map/ppermute | solution.py:1161
  528.2 19.2 %collective-permute-start.101 = (bf16[384,1024]{1,0:T(8,128)(2,1)S(1)}, bf16[384,1024]{1,0:T(8,128)(2,1)S(1)}, u32[]{:S(2)}, u32[]{:S(2)}) collective-permute-start(bf16[384,1024]{1,0:T(8,128)(2,1)S(1)} %pad_maximum_fusion), channel_id=1, source_target_pairs={{0,16},{16,0},{1,17},{17,1},{2,18},{18,2},{3,19},{19,3},{4,20},{20... | collective-permute-start | bytes 2359304 | tf_op jit(solution)/shard_map/ppermute | solution.py:868
  556.3 40.5 %collective-permute-start.109 = (f32[17,2048]{1,0:T(8,128)S(1)}, f32[17,2048]{1,0:T(8,128)S(1)}, u32[]{:S(2)}, u32[]{:S(2)}) collective-permute-start(f32[17,2048]{1,0:T(8,128)S(1)} %add.464), channel_id=1, source_target_pairs={{0,16},{16,0},{1,17},{17,1},{2,18},{18,2},{3,19},{19,3},{4,20},{20... | collective-permute-start | bytes 417800 | tf_op jit(solution)/shard_map/ppermute | solution.py:868
  557.6 39.1 %all-to-all-start.1 = ((bf16[16,64,384]{2,1,0:T(8,128)(2,1)}), bf16[16,64,384]{2,1,0:T(8,128)(2,1)S(1)}, u32[]{:S(2)}, u32[]{:S(2)}) async-start(bf16[16,64,384]{2,1,0:T(8,128)(2,1)} %bitcast.60), calls=%async_computation.4 | async-start | bytes 1572864 | tf_op jit(solution)/shard_map/all_to_all | solution.py:1285
  573.6 21.2 %collective-permute-start.105 = (bf16[128,2048]{1,0:T(8,128)(2,1)S(1)}, bf16[128,2048]{1,0:T(8,128)(2,1)S(1)}, u32[]{:S(2)}, u32[]{:S(2)}) collective-permute-start(bf16[128,2048]{1,0:T(8,128)(2,1)S(1)} %get-tuple-element.436), channel_id=1, source_target_pairs={{0,4},{1,5},{4,8},{5,9},{8,12},{9,13},{12,14},{13,15},{14,10},{15,... | collective-permute-start | bytes 1572872 | tf_op jit(solution)/shard_map/ppermute | solution.py:859
  573.9 22.9 %collective-permute-start.106 = (bf16[128,2048]{1,0:T(8,128)(2,1)S(1)}, bf16[128,2048]{1,0:T(8,128)(2,1)}, u32[]{:S(2)}, u32[]{:S(2)}) collective-permute-start(bf16[128,2048]{1,0:T(8,128)(2,1)S(1)} %get-tuple-element.437), channel_id=1, source_target_pairs={{4,0},{5,1},{8,4},{9,5},{12,8},{13,9},{14,12},{15,13},{10,14},{11,... | collective-permute-start | bytes 1572872 | tf_op jit(solution)/shard_map/ppermute | solution.py:862
  (176 other events, 1862.4 us)
Sparse Core Ops, SparseCore 0:
  337.8 52.2 reduce-scatter.3
  392.5 54.3 reduce-scatter.5
  449.8 65.5 reduce-scatter.7

commit v5 on v4

--- a/solution.py
+++ b/solution.py
@@ -413,7 +413,7 @@
     own_ref[...] = own.reshape(own_ref.shape)
     other_ref[...] = other.reshape(other_ref.shape)
     square_ref[...] = jnp.zeros_like(square_ref)
-    chips = square_ref.shape[0] // 2
+    chips = square_ref.shape[0] // 3
     for i in range(blocks):
         at = slice(i * rows, (i + 1) * rows)
         for j in range(2):
@@ -451,6 +451,7 @@
     hd = wide // 3
     cut = raw[0].shape[0]
     out = [jnp.zeros((rows, hd), F32)] * 4
+    inner_ref[...] = jnp.zeros_like(inner_ref)
     for i in range(chips):
         for j in range(2):
             cols = slice(j * hd, (j + 1) * hd)
@@ -1003,7 +1004,7 @@
         raw[i], raw[i + 2], squares[i] = on_core(
             functools.partial(project_kernel, first=i * len(early)),
             [jax.ShapeDtypeStruct((len(blocks), rows, 3 * hd), F32)] * 2
-            + [jax.ShapeDtypeStruct((2 * chips, rows), F32)],
+            + [jax.ShapeDtypeStruct((3 * chips, rows), F32)],
             [ids] + shards + w_in,
             12 * len(blocks) * rows * width * hd,
         )
@@ -1017,7 +1018,8 @@
     top = after(out_grad, *n1_halves)
     top_first = (to_right(top), to_left(top))
     flags = lax.dynamic_update_index_in_dim(jnp.zeros((chips, rows), F32), doc_starts.astype(F32), chip, 0)
-    total = sum_chips(after(jnp.concatenate([squares, flags], axis=0), *top_first))
+    flags = jnp.concatenate([jnp.zeros((2 * chips, rows), F32), flags], axis=0)
+    total = sum_chips(after(squares + flags, *top_first))
     one, two = lax.optimization_barrier(top_first + (total,))[:2]
     top_got = {0: out_grad, -1: top_first[0], 1: top_first[1], -2: to_right(one), 2: to_left(two)}
     heads = on_core(
@@ -1194,7 +1196,7 @@
     grads = [grads_own, core_swap(grads_away)]
     inner, gain_grads = on_core(
         functools.partial(inner_kernel, width=width),
-        [jax.ShapeDtypeStruct((2 * chips, rows), F32), jax.ShapeDtypeStruct((8, hd), F32)],
+        [jax.ShapeDtypeStruct((3 * chips, rows), F32), jax.ShapeDtypeStruct((8, hd), F32)],
         [ids] + grads + raw + [total, cosine, sine, gains],
         0,
     )

time: 634 us -> 634 us (level)
  transfers between devices with their start and end apart: 122 -> 122, of which waited for: 42 -> 43; matrix products, arithmetic and copies ran while one was open for 13% -> 13% of each run, Pallas kernels for 31% -> 31%
where the time goes in v5:
time: 634 us; the launch traced here: 624 us
  Pallas kernels  225 us (35%)
  starting transfers between devices  143 us (23%)
  waiting for transfers between devices  140 us (22%)
  other arithmetic  52.7 us (8%)
  local copies, waits for them, and re-layouts  43.3 us (7%)
  between operations  15.7 us (2%)
    pallas_call x3, Pallas kernels, expert_rows(): pl.pallas_call(functools.partial(expert_kernel, shards=shards, experts=ex...  88 us
    pallas_call x13, Pallas kernels, on_core(): pl.pallas_call(kernel, in_specs=[pl.BlockSpec(memory_space=m) for m in me...  76.1 us
    ppermute x32, waiting for transfers between devices, to_right(): return lax.ppermute(v, 'ctx', right)  72.4 us
    pallas_call x6, Pallas kernels, expert_grad_term(): pl.pallas_call(functools.partial(expert_grad_kernel, pieces=pieces, whole...  61.2 us
    ppermute x34, starting transfers between devices, core_swap(): return lax.ppermute(v, 'ctx', [(i, i ^ 1) for i in range(devices)])  53.9 us
    ppermute x32, starting transfers between devices, to_left(): return lax.ppermute(v, 'ctx', left)  26.9 us
    ppermute x32, starting transfers between devices, to_right(): return lax.ppermute(v, 'ctx', right)  24.3 us
    unnamed x165, local copies, waits for them, and re-layouts  18.4 us
  transfers between devices with their start and end apart: 122, of which 43 were waited for; matrix products, arithmetic and copies ran while one was open for 13% of the time, Pallas kernels for 31%

profile of v5, /device:TPU:9, one launch (start us, length us, event | category | flops | bytes accessed | tf_op | source)
XLA Modules:
  0.0 623.8 jit_solution(3409581852570303217)
XLA Ops:
  16.9 15.4 %all-to-all-done = bf16[8,128,384]{2,1,0:T(8,128)(2,1)S(1)} async-done(((bf16[8,128,384]{2,1,0:T(8,128)(2,1)}), bf16[8,128,384]{2,1,0:T(8,128)(2,1)S(1)}, u32[]{:S(2)}, u32[]{:S(2)}) %all-to-all-start) | async-done | bytes 786464 | tf_op jit(solution)/shard_map/all_to_all | solution.py:976
  36.2 9.6 %collective-permute-done.refs_2_.refs_15_.refs_4_ = bf16[128,2048]{1,0:T(8,128)(2,1)S(1)} collective-permute-done((bf16[128,2048]{1,0:T(8,128)(2,1)S(1)}, bf16[128,2048]{1,0:T(8,128)(2,1)S(1)}, u32[]{:S(2)}, u32[]{:S(2)}) %collective-permute-start) | collective-permute-done | bytes 524320 | tf_op jit(solution)/shard_map/ppermute | solution.py:860
  54.1 6.6 %collective-permute-done.2.refs_3_.refs_16_.refs_5_ = bf16[128,2048]{1,0:T(8,128)(2,1)} collective-permute-done((bf16[128,2048]{1,0:T(8,128)(2,1)}, bf16[128,2048]{1,0:T(8,128)(2,1)}, u32[]{:S(2)}, u32[]{:S(2)}) %collective-permute-start.2) | collective-permute-done | bytes 524320 | tf_op jit(solution)/shard_map/ppermute | solution.py:863
  66.1 6.5 %shard_map.264 = (f32[5,128,384]{2,1,0:T(8,128)}, f32[5,128,384]{2,1,0:T(8,128)}, f32[24,128]{1,0:T(8,128)}) custom-call(s32[9]{0:T(128)} %concatenate.85.ids_ref, bf16[128,2048]{1,0:T(8,128)(2,1)} %bitcast.171, bf16[128,2048]{1,0:T(8,128)(2,1)} %collective-permute-done.1.refs_1_.refs_14_.refs_3_, bf16[128,2048]{1,0:T(8,128)(2,1)} %copy-done.46, ...), custom_call_target="tpu_custom_call" | custom-call | flops 2013265920 | bytes 7745572 | tf_op jit(solution)/shard_map/pallas_call | solution.py:545
  105.9 8.5 %collective-permute-start.16 = (bf16[8,128,384]{2,1,0:T(8,128)(2,1)}, bf16[8,128,384]{2,1,0:T(8,128)(2,1)S(1)}, u32[]{:S(2)}, u32[]{:S(2)}) collective-permute-start(bf16[8,128,384]{2,1,0:T(8,128)(2,1)} %get-tuple-element.256), channel_id=1, source_target_pairs={{0,1},{1,0},{2,3},{3,2},{4,5},{5,4},{6,7},{7,6},{8,9},{9,8},{10,11... | collective-permute-start | bytes 2359304 | tf_op jit(solution)/shard_map/ppermute | solution.py:866
  119.5 9.3 %shard_map.267 = (f32[2048,128]{1,0:T(8,128)}, f32[1,2048]{1,0:T(1,128)}, bf16[2048,384]{1,0:T(8,128)(2,1)}, bf16[8,128,128]{2,1,0:T(8,128)(2,1)}, bf16[8,128,128]{2,1,0:T(8,128)(2,1)}) custom-call(s32[9]{0:T(128)} %concatenate.85.ids_ref, bf16[8,128,384]{2,1,0:T(8,128)(2,1)} %get-tuple-element.255.mine_ref, bf16[8,128,384]{2,1,0:T(8,128)(2,1)} %copy-done.70, ...), custom_call_target="tpu_custom_call" | custom-call | flops 2147483648 | bytes 4735012 | tf_op jit(solution)/shard_map/pallas_call | solution.py:545
  179.8 6.8 %collective-permute-done.33.refs_2_ = bf16[128,2176]{1,0:T(8,128)(2,1)S(1)} collective-permute-done((bf16[128,2176]{1,0:T(8,128)(2,1)S(1)}, bf16[128,2176]{1,0:T(8,128)(2,1)S(1)}, u32[]{:S(2)}, u32[]{:S(2)}) %collective-permute-start.33) | collective-permute-done | bytes 557088 | tf_op jit(solution)/shard_map/ppermute | solution.py:860
  190.7 32.4 %shard_map.268 = (bf16[3,128,2048]{2,1,0:T(8,128)(2,1)}, bf16[3,128,2176]{2,1,0:T(8,128)(2,1)}, bf16[8,128,2048]{2,1,0:T(8,128)(2,1)}, bf16[8,128,2048]{2,1,0:T(...) custom-call(s32[2]{0:T(128)} %pad_add_fusion.1.ids_ref, ...), custom_call_target="tpu_custom_call" | custom-call | flops 19327352832 | bytes 25165824 | tf_op jit(solution)/shard_map/pallas_call | solution.py:718
  226.4 23.3 %shard_map.269 = (bf16[2,128,2048]{2,1,0:T(8,128)(2,1)}, bf16[2,128,2176]{2,1,0:T(8,128)(2,1)}, bf16[8,128,2048]{2,1,0:T(8,128)(2,1)}, bf16[8,128,2048]{2,1,0:T(...) custom-call(s32[2]{0:T(128)} %pad_add_fusion.1.ids_ref, ...), custom_call_target="tpu_custom_call", output_to_operand_aliasing={{2}: (8, {}), {3}: (9, {}), {4}: (10, {}), {5}: (11, {}), {... | custom-call | flops 12884901888 | bytes 25165824 | tf_op jit(solution)/shard_map/pallas_call | solution.py:718
  257.2 32.3 %shard_map.270 = (bf16[3,128,2048]{2,1,0:T(8,128)(2,1)}, bf16[3,128,2176]{2,1,0:T(8,128)(2,1)}, bf16[8,128,2048]{2,1,0:T(8,128)(2,1)}, bf16[8,128,2048]{2,1,0:T(...) custom-call(s32[2]{0:T(128)} %pad_add_fusion.1.ids_ref, ...), custom_call_target="tpu_custom_call", output_to_operand_aliasing={{2}: (10, {}), {3}: (11, {}), {4}: (12, {}), {5}: (13, {}),... | custom-call | flops 19327352832 | bytes 25165824 | tf_op jit(solution)/shard_map/pallas_call | solution.py:718
  293.0 10.0 %shard_map.271 = (bf16[256,2048]{1,0:T(8,128)(2,1)}, bf16[256,2048]{1,0:T(8,128)(2,1)}, bf16[256,2048]{1,0:T(8,128)(2,1)}, bf16[256,2048]{1,0:T(8,128)(2,1)}) custom-call(bf16[1024,2048]{1,0:T(8,128)(2,1)} %bitcast.154, bf16[1024,2048]{1,0:T(8,128)(2,1)} %bitcast.160), custom_call_target="tpu_custom_call" | custom-call | flops 4294967296 | bytes 10485760 | tf_op jit(solution)/shard_map/pallas_call | solution.py:806
  303.7 15.5 %collective-permute-start.49 = (bf16[256,2048]{1,0:T(8,128)(2,1)}, bf16[256,2048]{1,0:T(8,128)(2,1)S(1)}, u32[]{:S(2)}, u32[]{:S(2)}) collective-permute-start(bf16[256,2048]{1,0:T(8,128)(2,1)} %get-tuple-element.313), channel_id=1, source_target_pairs={{0,1},{1,0},{2,3},{3,2},{4,5},{5,4},{6,7},{7,6},{8,9},{9,8},{10,11... | collective-permute-start | bytes 3145736 | tf_op jit(solution)/shard_map/ppermute | solution.py:866
  327.2 10.4 %shard_map.272 = bf16[1024,2048]{1,0:T(8,128)(2,1)} custom-call(bf16[1024,2048]{1,0:T(8,128)(2,1)} %bitcast.155, bf16[1024,2048]{1,0:T(8,128)(2,1)} %bitcast.161, bf16[256,2048]{1,0:T(8,128)(2,1)} %copy-done.28, bf16[256,2048]{1,0:T(8,128)(2,1)} %copy-done.29, bf16[256,2048]{1,0:T(8,128)(2,1)} %copy-done.30, bf16[256,2048]{1,0:T(8,128)(2,1)} %copy-done.31), custom_call_target="tpu_custom_call" | custom-call | flops 4294967296 | bytes 10485760 | tf_op jit(solution)/shard_map/pallas_call | solution.py:806
  341.7 10.2 %shard_map.273 = (bf16[512,1024]{1,0:T(8,128)(2,1)}, bf16[512,1024]{1,0:T(8,128)(2,1)}, bf16[512,1024]{1,0:T(8,128)(2,1)}, bf16[512,1024]{1,0:T(8,128)(2,1)}) custom-call(bf16[1024,2048]{1,0:T(8,128)(2,1)} %bitcast.150, bf16[1024,2048]{1,0:T(8,128)(2,1)} %bitcast.156), custom_call_target="tpu_custom_call" | custom-call | flops 4294967296 | bytes 10485760 | tf_op jit(solution)/shard_map/pallas_call | solution.py:806
  358.1 9.6 %shard_map.274 = (bf16[512,1024]{1,0:T(8,128)(2,1)}, bf16[512,1024]{1,0:T(8,128)(2,1)}, bf16[512,1024]{1,0:T(8,128)(2,1)}, bf16[512,1024]{1,0:T(8,128)(2,1)}) custom-call(bf16[1024,2048]{1,0:T(8,128)(2,1)} %bitcast.151, bf16[1024,2048]{1,0:T(8,128)(2,1)} %bitcast.158), custom_call_target="tpu_custom_call" | custom-call | flops 4294967296 | bytes 10485760 | tf_op jit(solution)/shard_map/pallas_call | solution.py:806
  375.0 10.1 %shard_map.275 = bf16[2048,1024]{1,0:T(8,128)(2,1)} custom-call(bf16[1024,2048]{1,0:T(8,128)(2,1)} %bitcast.152, bf16[1024,2048]{1,0:T(8,128)(2,1)} %bitcast.157, bf16[512,1024]{1,0:T(8,128)(2,1)} %collective-permute-done.59.refs_0_, bf16[512,1024]{1,0:T(8,128)(2,1)} %collective-permute-done.60.refs_1_, bf16[512,1024]{1,0:T(8,128)(2,1)} %collective-permute-done.61.refs_2_, ...), custom_call_target="tpu_custom_call" | custom-call | flops 4294967296 | bytes 10485760 | tf_op jit(solution)/shard_map/pallas_call | solution.py:806
  397.2 10.8 %shard_map.276 = bf16[2048,1024]{1,0:T(8,128)(2,1)} custom-call(bf16[1024,2048]{1,0:T(8,128)(2,1)} %bitcast.153, bf16[1024,2048]{1,0:T(8,128)(2,1)} %bitcast.159, bf16[512,1024]{1,0:T(8,128)(2,1)} %copy-done.32, bf16[512,1024]{1,0:T(8,128)(2,1)} %copy-done.33, bf16[512,1024]{1,0:T(8,128)(2,1)} %copy-done.34, bf16[512,1024]{1,0:T(8,128)(2,1)} %copy-done.35), custom_call_target="tpu_custom_call" | custom-call | flops 4294967296 | bytes 10485760 | tf_op jit(solution)/shard_map/pallas_call | solution.py:806
  411.1 10.3 %collective-permute-done.69.refs_1_.refs_8_ = bf16[128,2048]{1,0:T(8,128)(2,1)S(1)} collective-permute-done((bf16[128,2048]{1,0:T(8,128)(2,1)S(1)}, bf16[128,2048]{1,0:T(8,128)(2,1)S(1)}, u32[]{:S(2)}, u32[]{:S(2)}) %collective-permute-start.69) | collective-permute-done | bytes 524320 | tf_op jit(solution)/shard_map/ppermute | solution.py:860
  443.5 9.8 %shard_map.279 = (f32[8,128,384]{2,1,0:T(8,128)}, bf16[8,128,384]{2,1,0:T(8,128)(2,1)}) custom-call(s32[9]{0:T(128)} %concatenate.85.ids_ref, bf16[2048,384]{1,0:T(8,128)(2,1)} %get-tuple-element.278.qkv_ref, bf16[5,128,128]{2,1,0:T(8,128)(2,1)} %get-tuple-element.358.refs_0_, bf16[3,128,128]{2,1,0:T(8,128)(2,1)} %get-tuple-element.363.refs_1_, ...), custom_call_target="tpu_custom_call" | custom-call | flops 5368709120 | bytes 5521444 | tf_op jit(solution)/shard_map/pallas_call | solution.py:545
  490.8 12.0 %shard_map.282 = (bf16[8,128,384]{2,1,0:T(8,128)(2,1)}, bf16[8,128,384]{2,1,0:T(8,128)(2,1)}, bf16[8,128,2048]{2,1,0:T(8,128)(2,1)}, f32[8,2048]{1,0:T(8,128)}) custom-call(s32[9]{0:T(128)} %concatenate.85.ids_ref, f32[8,128,384]{2,1,0:T(8,128)} %get-tuple-element.372.grad_own, bf16[8,128,384]{2,1,0:T(8,128)(2,1)} %copy-done.16, ...), custom_call_target="tpu_custom_call" | custom-call | flops 3221225472 | bytes 19755044 | tf_op jit(solution)/shard_map/pallas_call | solution.py:545
  514.8 7.1 %shard_map.283 = (f32[384,2048]{1,0:T(8,128)}, bf16[384,512]{1,0:T(8,128)(2,1)}, bf16[384,512]{1,0:T(8,128)(2,1)}, bf16[384,512]{1,0:T(8,128)(2,1)}, bf16[384,512]{1,0:T(8,128)(2,1)}) custom-call(bf16[8,128,384]{2,1,0:T(8,128)(2,1)} %get-tuple-element.404.refs_0_, bf16[8,128,384]{2,1,0:T(8,128)(2,1)} %get-tuple-element.406.refs_1_, ...), custom_call_target="tpu_custom_call" | custom-call | flops 3221225472 | bytes 10485760 | tf_op jit(solution)/shard_map/pallas_call | solution.py:545
  534.1 13.4 %collective-permute-done.101 = bf16[384,1024]{1,0:T(8,128)(2,1)S(1)} collective-permute-done((bf16[384,1024]{1,0:T(8,128)(2,1)S(1)}, bf16[384,1024]{1,0:T(8,128)(2,1)S(1)}, u32[]{:S(2)}, u32[]{:S(2)}) %collective-permute-start.101) | collective-permute-done | bytes 786464 | tf_op jit(solution)/shard_map/ppermute | solution.py:869
  557.8 7.3 %all-to-all-start.1 = ((bf16[16,64,384]{2,1,0:T(8,128)(2,1)}), bf16[16,64,384]{2,1,0:T(8,128)(2,1)S(1)}, u32[]{:S(2)}, u32[]{:S(2)}) async-start(bf16[16,64,384]{2,1,0:T(8,128)(2,1)} %bitcast.60), calls=%async_computation.4 | async-start | bytes 1572864 | tf_op jit(solution)/shard_map/all_to_all | solution.py:1287
  583.7 11.2 %collective-permute-done.105.there_ref = bf16[128,2048]{1,0:T(8,128)(2,1)S(1)} collective-permute-done((bf16[128,2048]{1,0:T(8,128)(2,1)S(1)}, bf16[128,2048]{1,0:T(8,128)(2,1)S(1)}, u32[]{:S(2)}, u32[]{:S(2)}) %collective-permute-start.105) | collective-permute-done | bytes 524320 | tf_op jit(solution)/shard_map/ppermute | solution.py:860
  (563 shorter events, 309.6 us)
Async XLA Ops:
  9.7 22.7 %all-to-all-start = ((bf16[8,128,384]{2,1,0:T(8,128)(2,1)}), bf16[8,128,384]{2,1,0:T(8,128)(2,1)S(1)}, u32[]{:S(2)}, u32[]{:S(2)}) async-start(bf16[8,128,384]{2,1,0:T(8,128)(2,1)} %shard_map.263), calls=%async_computation | async-start | bytes 1572864 | tf_op jit(solution)/shard_map/all_to_all | solution.py:976
  15.4 506.5 %reduce-scatter.4.cloned.1.call-start = ((), (), s32[]{:S(2)}) async-start(), calls=%async_computation.5 | async-start | bytes 6291456 | tf_op jit(solution)/shard_map/reduce_scatter | solution.py:1119
  62.2 84.3 %collective-permute-start.26 = (bf16[1,2048,1024]{2,1,0:T(8,128)(2,1)}, bf16[1,2048,1024]{2,1,0:T(8,128)(2,1)}, u32[]{:S(2)}, u32[]{:S(2)}) collective-permute-start(bf16[1,2048,1024]{2,1,0:T(8,128)(2,1)} %param.28), channel_id=1, source_target_pairs={{0,1},{1,0},{2,3},{3,2},{4,5},{5,4},{6,7},{7,6},{8,9},{9,8},{10,11... | collective-permute-start | bytes 12582920 | tf_op jit(solution)/shard_map/ppermute | solution.py:866
  115.6 44.0 %collective-permute-start.29 = (bf16[1,2048,1024]{2,1,0:T(8,128)(2,1)}, bf16[1,2048,1024]{2,1,0:T(8,128)(2,1)}, u32[]{:S(2)}, u32[]{:S(2)}) collective-permute-start(bf16[1,2048,1024]{2,1,0:T(8,128)(2,1)} %param.29), channel_id=1, source_target_pairs={{0,1},{1,0},{2,3},{3,2},{4,5},{5,4},{6,7},{7,6},{8,9},{9,8},{10,11... | collective-permute-start | bytes 12582920 | tf_op jit(solution)/shard_map/ppermute | solution.py:866
  129.8 40.1 %collective-permute-start.32 = (bf16[1,1024,2048]{2,1,0:T(8,128)(2,1)}, bf16[1,1024,2048]{2,1,0:T(8,128)(2,1)}, u32[]{:S(2)}, u32[]{:S(2)}) collective-permute-start(bf16[1,1024,2048]{2,1,0:T(8,128)(2,1)} %param.30), channel_id=1, source_target_pairs={{0,1},{1,0},{2,3},{3,2},{4,5},{5,4},{6,7},{7,6},{8,9},{9,8},{10,11... | collective-permute-start | bytes 12582920 | tf_op jit(solution)/shard_map/ppermute | solution.py:866
  187.7 35.4 %collective-permute-start.35 = (bf16[128,2176]{1,0:T(8,128)(2,1)S(1)}, bf16[128,2176]{1,0:T(8,128)(2,1)S(1)}, u32[]{:S(2)}, u32[]{:S(2)}) collective-permute-start(bf16[128,2176]{1,0:T(8,128)(2,1)S(1)} %collective-permute-done.33.refs_2_), channel_id=1, source_target_pairs={{0,4},{1,5},{4,8},{5,9},{8,12},{9,13},{12,14},{13,15},{14,10},{15,... | collective-permute-start | bytes 1671176 | tf_op jit(solution)/shard_map/ppermute | solution.py:860
  188.5 34.6 %collective-permute-start.36 = (bf16[128,2176]{1,0:T(8,128)(2,1)S(1)}, bf16[128,2176]{1,0:T(8,128)(2,1)S(1)}, u32[]{:S(2)}, u32[]{:S(2)}) collective-permute-start(bf16[128,2176]{1,0:T(8,128)(2,1)S(1)} %collective-permute-done.34.refs_1_), channel_id=1, source_target_pairs={{4,0},{5,1},{8,4},{9,5},{12,8},{13,9},{14,12},{15,13},{10,14},{11,... | collective-permute-start | bytes 1671176 | tf_op jit(solution)/shard_map/ppermute | solution.py:863
  189.2 33.9 %collective-permute-start.37 = (bf16[128,2048]{1,0:T(8,128)(2,1)}, bf16[128,2048]{1,0:T(8,128)(2,1)S(1)}, u32[]{:S(2)}, u32[]{:S(2)}) collective-permute-start(bf16[128,2048]{1,0:T(8,128)(2,1)} %copy-done.45), channel_id=1, source_target_pairs={{0,4},{1,5},{4,8},{5,9},{8,12},{9,13},{12,14},{13,15},{14,10},{15,... | collective-permute-start | bytes 1572872 | tf_op jit(solution)/shard_map/ppermute | solution.py:860
  190.1 33.0 %collective-permute-start.38 = (bf16[128,2048]{1,0:T(8,128)(2,1)}, bf16[128,2048]{1,0:T(8,128)(2,1)S(1)}, u32[]{:S(2)}, u32[]{:S(2)}) collective-permute-start(bf16[128,2048]{1,0:T(8,128)(2,1)} %copy-done.44), channel_id=1, source_target_pairs={{4,0},{5,1},{8,4},{9,5},{12,8},{13,9},{14,12},{15,13},{10,14},{11,... | collective-permute-start | bytes 1572872 | tf_op jit(solution)/shard_map/ppermute | solution.py:863
  223.2 28.3 %collective-permute-start.43 = (bf16[64,2048]{1,0:T(8,128)(2,1)S(1)}, bf16[64,2048]{1,0:T(8,128)(2,1)S(1)}, u32[]{:S(2)}, u32[]{:S(2)}) collective-permute-start(bf16[64,2048]{1,0:T(8,128)(2,1)S(1)} %slice.316), channel_id=1, source_target_pairs={{0,4},{1,5},{4,8},{5,9},{8,12},{9,13},{12,14},{13,15},{14,10},{15,... | collective-permute-start | bytes 786440 | tf_op jit(solution)/shard_map/ppermute | solution.py:860
  224.1 27.3 %collective-permute-start.44 = (bf16[64,2048]{1,0:T(8,128)(2,1)S(1)}, bf16[64,2048]{1,0:T(8,128)(2,1)S(1)}, u32[]{:S(2)}, u32[]{:S(2)}) collective-permute-start(bf16[64,2048]{1,0:T(8,128)(2,1)S(1)} %slice.317), channel_id=1, source_target_pairs={{4,0},{5,1},{8,4},{9,5},{12,8},{13,9},{14,12},{15,13},{10,14},{11,... | collective-permute-start | bytes 786440 | tf_op jit(solution)/shard_map/ppermute | solution.py:863
  224.7 25.0 %collective-permute-start.39 = (bf16[128,2176]{1,0:T(8,128)(2,1)S(1)}, bf16[128,2176]{1,0:T(8,128)(2,1)S(1)}, u32[]{:S(2)}, u32[]{:S(2)}) collective-permute-start(bf16[128,2176]{1,0:T(8,128)(2,1)S(1)} %collective-permute-done.36.refs_0_), channel_id=1, source_target_pairs={{4,0},{5,1},{8,4},{9,5},{12,8},{13,9},{14,12},{15,13},{10,14},{11,... | collective-permute-start | bytes 1671176 | tf_op jit(solution)/shard_map/ppermute | solution.py:863
  225.4 24.4 %collective-permute-start.40 = (bf16[128,2176]{1,0:T(8,128)(2,1)S(1)}, bf16[128,2176]{1,0:T(8,128)(2,1)S(1)}, u32[]{:S(2)}, u32[]{:S(2)}) collective-permute-start(bf16[128,2176]{1,0:T(8,128)(2,1)S(1)} %collective-permute-done.35.refs_1_), channel_id=1, source_target_pairs={{0,4},{1,5},{4,8},{5,9},{8,12},{9,13},{12,14},{13,15},{14,10},{15,... | collective-permute-start | bytes 1671176 | tf_op jit(solution)/shard_map/ppermute | solution.py:860
  337.6 184.3 %reduce-scatter.6.cloned.1.call-start = ((), (), s32[]{:S(2)}) async-start(), calls=%async_computation.6 | async-start | bytes 6291456 | tf_op jit(solution)/shard_map/reduce_scatter | solution.py:1119
  355.8 18.9 %collective-permute-start.59 = (bf16[512,1024]{1,0:T(8,128)(2,1)}, bf16[512,1024]{1,0:T(8,128)(2,1)}, u32[]{:S(2)}, u32[]{:S(2)}) collective-permute-start(bf16[512,1024]{1,0:T(8,128)(2,1)} %get-tuple-element.343), channel_id=1, source_target_pairs={{0,1},{1,0},{2,3},{3,2},{4,5},{5,4},{6,7},{7,6},{8,9},{9,8},{10,11... | collective-permute-start | bytes 3145736 | tf_op jit(solution)/shard_map/ppermute | solution.py:866
  387.7 134.3 %reduce-scatter.8.cloned.1.call-start = ((), (), s32[]{:S(2)}) async-start(), calls=%async_computation.7 | async-start | bytes 6291456 | tf_op jit(solution)/shard_map/reduce_scatter | solution.py:1119
  484.0 114.2 %collective-permute-start.114 = (bf16[128,2048]{1,0:T(8,128)(2,1)}, bf16[128,2048]{1,0:T(8,128)(2,1)S(1)}, u32[]{:S(2)}, u32[]{:S(2)}) collective-permute-start(bf16[128,2048]{1,0:T(8,128)(2,1)} %fusion.8), channel_id=1, source_target_pairs={{0,16},{16,0},{1,17},{17,1},{2,18},{18,2},{3,19},{19,3},{4,20},{20... | collective-permute-start | bytes 1572872 | tf_op jit(solution)/shard_map/ppermute | solution.py:869
  488.4 33.5 %collective-permute-start.92 = (f32[17,2048]{1,0:T(8,128)S(1)}, f32[17,2048]{1,0:T(8,128)S(1)}, u32[]{:S(2)}, u32[]{:S(2)}) collective-permute-start(f32[17,2048]{1,0:T(8,128)S(1)} %add.450), channel_id=1, source_target_pairs={{0,8},{1,9},{2,10},{3,11},{4,12},{5,13},{6,14},{7,15},{8,0},{9,1},... | collective-permute-start | bytes 417800 | tf_op jit(solution)/shard_map/ppermute | solution.py:1163
  524.8 24.5 %collective-permute-start.96 = (f32[3,2048]{1,0:T(4,128)}, f32[3,2048]{1,0:T(4,128)}, u32[]{:S(2)}, u32[]{:S(2)}) collective-permute-start(f32[3,2048]{1,0:T(4,128)} %fusion.18), channel_id=1, source_target_pairs={{0,2},{1,3},{2,0},{3,1},{4,6},{5,7},{6,4},{7,5},{8,10},{9,11},{10,... | collective-permute-start | bytes 73736 | tf_op jit(solution)/shard_map/ppermute | solution.py:1163
  528.3 19.2 %collective-permute-start.101 = (bf16[384,1024]{1,0:T(8,128)(2,1)S(1)}, bf16[384,1024]{1,0:T(8,128)(2,1)S(1)}, u32[]{:S(2)}, u32[]{:S(2)}) collective-permute-start(bf16[384,1024]{1,0:T(8,128)(2,1)S(1)} %pad_maximum_fusion), channel_id=1, source_target_pairs={{0,16},{16,0},{1,17},{17,1},{2,18},{18,2},{3,19},{19,3},{4,20},{20... | collective-permute-start | bytes 2359304 | tf_op jit(solution)/shard_map/ppermute | solution.py:869
  556.4 40.5 %collective-permute-start.109 = (f32[17,2048]{1,0:T(8,128)S(1)}, f32[17,2048]{1,0:T(8,128)S(1)}, u32[]{:S(2)}, u32[]{:S(2)}) collective-permute-start(f32[17,2048]{1,0:T(8,128)S(1)} %add.470), channel_id=1, source_target_pairs={{0,16},{16,0},{1,17},{17,1},{2,18},{18,2},{3,19},{19,3},{4,20},{20... | collective-permute-start | bytes 417800 | tf_op jit(solution)/shard_map/ppermute | solution.py:869
  557.8 39.1 %all-to-all-start.1 = ((bf16[16,64,384]{2,1,0:T(8,128)(2,1)}), bf16[16,64,384]{2,1,0:T(8,128)(2,1)S(1)}, u32[]{:S(2)}, u32[]{:S(2)}) async-start(bf16[16,64,384]{2,1,0:T(8,128)(2,1)} %bitcast.60), calls=%async_computation.4 | async-start | bytes 1572864 | tf_op jit(solution)/shard_map/all_to_all | solution.py:1287
  573.8 21.2 %collective-permute-start.105 = (bf16[128,2048]{1,0:T(8,128)(2,1)S(1)}, bf16[128,2048]{1,0:T(8,128)(2,1)S(1)}, u32[]{:S(2)}, u32[]{:S(2)}) collective-permute-start(bf16[128,2048]{1,0:T(8,128)(2,1)S(1)} %get-tuple-element.436), channel_id=1, source_target_pairs={{0,4},{1,5},{4,8},{5,9},{8,12},{9,13},{12,14},{13,15},{14,10},{15,... | collective-permute-start | bytes 1572872 | tf_op jit(solution)/shard_map/ppermute | solution.py:860
  574.0 22.9 %collective-permute-start.106 = (bf16[128,2048]{1,0:T(8,128)(2,1)S(1)}, bf16[128,2048]{1,0:T(8,128)(2,1)}, u32[]{:S(2)}, u32[]{:S(2)}) collective-permute-start(bf16[128,2048]{1,0:T(8,128)(2,1)S(1)} %get-tuple-element.437), channel_id=1, source_target_pairs={{4,0},{5,1},{8,4},{9,5},{12,8},{13,9},{14,12},{15,13},{10,14},{11,... | collective-permute-start | bytes 1572872 | tf_op jit(solution)/shard_map/ppermute | solution.py:863
  (176 other events, 1902.6 us)
Sparse Core Ops, SparseCore 0:
  337.8 52.3 reduce-scatter.3
  392.5 54.3 reduce-scatter.5
  449.7 65.5 reduce-scatter.7

commit v6 on v5

--- a/solution.py
+++ b/solution.py
@@ -1313,14 +1313,13 @@
     )
     down_grad_out, gate_grad_out, up_grad_out, w_got = grads_out
     o_head = (o_head + after(o_recv, n1_grad[0]).astype(F32)).astype(B16)
-    wo_grad = None
-    for i in range(2):
-        moves = [
-            (g * devices + devices // 2 * g + j, g * devices + 2 * j + i) for g in range(2) for j in range(devices // 2)
-        ]
-        size = width // (2 * devices)
-        piece = lax.ppermute(o_head[i * size : (i + 1) * size], ("dp", "ctx"), moves)
-        wo_grad = piece if wo_grad is None else jnp.where(core == 0, wo_grad, piece)
+    moves = [
+        (g * devices + devices // 2 * g + j, g * devices + 2 * j + j % 2) for g in range(2) for j in range(devices // 2)
+    ]
+    whole = lax.ppermute(o_head, ("dp", "ctx"), moves)
+    size = width // (2 * devices)
+    pieces = (whole[:size], whole[size:])
+    wo_grad = jnp.where(core == chip % 2, pick(pieces, core), core_swap(pick(pieces, 1 - core)))
     wo_grad = wo_grad.astype(F32)
     late_sum = after(late_sum[-1], n1_grad[0])
     late_sum = late_sum + group_swap(late_sum)

time: 634 us -> 635 us (level)
    ppermute x34 -> x35, starting transfers between devices: 53.9 us -> 58.3 us  [core_swap(): return lax.ppermute(v, 'ctx', [(i, i ^ 1) for i in range(devices)])]
    unnamed x165 -> x161, local copies, waits for them, and re-layouts: 18.4 us -> 17.6 us
  transfers between devices with their start and end apart: 122 -> 122, of which waited for: 43 -> 45; matrix products, arithmetic and copies ran while one was open for 13% -> 14% of each run, Pallas kernels for 31% -> 30%
where the time goes in v6:
time: 635 us; the launch traced here: 625 us
  Pallas kernels  225 us (35%)
  starting transfers between devices  145 us (23%)
  waiting for transfers between devices  138 us (22%)
  other arithmetic  54.7 us (9%)
  local copies, waits for them, and re-layouts  42.4 us (7%)
  between operations  15.7 us (2%)
    pallas_call x3, Pallas kernels, expert_rows(): pl.pallas_call(functools.partial(expert_kernel, shards=shards, experts=ex...  88 us
    pallas_call x13, Pallas kernels, on_core(): pl.pallas_call(kernel, in_specs=[pl.BlockSpec(memory_space=m) for m in me...  76.2 us
    ppermute x32, waiting for transfers between devices, to_right(): return lax.ppermute(v, 'ctx', right)  72.7 us
    pallas_call x6, Pallas kernels, expert_grad_term(): pl.pallas_call(functools.partial(expert_grad_kernel, pieces=pieces, whole...  61.1 us
    ppermute x35, starting transfers between devices, core_swap(): return lax.ppermute(v, 'ctx', [(i, i ^ 1) for i in range(devices)])  58.3 us
    ppermute x32, starting transfers between devices, to_left(): return lax.ppermute(v, 'ctx', left)  26.8 us
    ppermute x32, starting transfers between devices, to_right(): return lax.ppermute(v, 'ctx', right)  24.3 us
    ppermute x32, waiting for transfers between devices, to_left(): return lax.ppermute(v, 'ctx', left)  17.6 us
  transfers between devices with their start and end apart: 122, of which 45 were waited for; matrix products, arithmetic and copies ran while one was open for 14% of the time, Pallas kernels for 30%

profile of v6, /device:TPU:9, one launch (start us, length us, event | category | flops | bytes accessed | tf_op | source)
XLA Modules:
  0.0 624.9 jit_solution(13967309419328871486)
XLA Ops:
  16.9 15.4 %all-to-all-done = bf16[8,128,384]{2,1,0:T(8,128)(2,1)S(1)} async-done(((bf16[8,128,384]{2,1,0:T(8,128)(2,1)}), bf16[8,128,384]{2,1,0:T(8,128)(2,1)S(1)}, u32[]{:S(2)}, u32[]{:S(2)}) %all-to-all-start) | async-done | bytes 786464 | tf_op jit(solution)/shard_map/all_to_all | solution.py:976
  36.2 9.6 %collective-permute-done.refs_2_.refs_15_.refs_4_ = bf16[128,2048]{1,0:T(8,128)(2,1)S(1)} collective-permute-done((bf16[128,2048]{1,0:T(8,128)(2,1)S(1)}, bf16[128,2048]{1,0:T(8,128)(2,1)S(1)}, u32[]{:S(2)}, u32[]{:S(2)}) %collective-permute-start) | collective-permute-done | bytes 524320 | tf_op jit(solution)/shard_map/ppermute | solution.py:860
  54.1 6.6 %collective-permute-done.2.refs_3_.refs_16_.refs_5_ = bf16[128,2048]{1,0:T(8,128)(2,1)} collective-permute-done((bf16[128,2048]{1,0:T(8,128)(2,1)}, bf16[128,2048]{1,0:T(8,128)(2,1)}, u32[]{:S(2)}, u32[]{:S(2)}) %collective-permute-start.2) | collective-permute-done | bytes 524320 | tf_op jit(solution)/shard_map/ppermute | solution.py:863
  66.1 6.5 %shard_map.264 = (f32[5,128,384]{2,1,0:T(8,128)}, f32[5,128,384]{2,1,0:T(8,128)}, f32[24,128]{1,0:T(8,128)}) custom-call(s32[9]{0:T(128)} %concatenate.85.ids_ref, bf16[128,2048]{1,0:T(8,128)(2,1)} %bitcast.171, bf16[128,2048]{1,0:T(8,128)(2,1)} %collective-permute-done.1.refs_1_.refs_14_.refs_3_, bf16[128,2048]{1,0:T(8,128)(2,1)} %copy-done.46, ...), custom_call_target="tpu_custom_call" | custom-call | flops 2013265920 | bytes 7745572 | tf_op jit(solution)/shard_map/pallas_call | solution.py:545
  105.9 8.6 %collective-permute-start.16 = (bf16[8,128,384]{2,1,0:T(8,128)(2,1)}, bf16[8,128,384]{2,1,0:T(8,128)(2,1)S(1)}, u32[]{:S(2)}, u32[]{:S(2)}) collective-permute-start(bf16[8,128,384]{2,1,0:T(8,128)(2,1)} %get-tuple-element.256), channel_id=1, source_target_pairs={{0,1},{1,0},{2,3},{3,2},{4,5},{5,4},{6,7},{7,6},{8,9},{9,8},{10,11... | collective-permute-start | bytes 2359304 | tf_op jit(solution)/shard_map/ppermute | solution.py:866
  119.5 9.3 %shard_map.267 = (f32[2048,128]{1,0:T(8,128)}, f32[1,2048]{1,0:T(1,128)}, bf16[2048,384]{1,0:T(8,128)(2,1)}, bf16[8,128,128]{2,1,0:T(8,128)(2,1)}, bf16[8,128,128]{2,1,0:T(8,128)(2,1)}) custom-call(s32[9]{0:T(128)} %concatenate.85.ids_ref, bf16[8,128,384]{2,1,0:T(8,128)(2,1)} %get-tuple-element.255.mine_ref, bf16[8,128,384]{2,1,0:T(8,128)(2,1)} %copy-done.68, ...), custom_call_target="tpu_custom_call" | custom-call | flops 2147483648 | bytes 4735012 | tf_op jit(solution)/shard_map/pallas_call | solution.py:545
  179.8 6.8 %collective-permute-done.33.refs_2_ = bf16[128,2176]{1,0:T(8,128)(2,1)S(1)} collective-permute-done((bf16[128,2176]{1,0:T(8,128)(2,1)S(1)}, bf16[128,2176]{1,0:T(8,128)(2,1)S(1)}, u32[]{:S(2)}, u32[]{:S(2)}) %collective-permute-start.33) | collective-permute-done | bytes 557088 | tf_op jit(solution)/shard_map/ppermute | solution.py:860
  190.6 32.4 %shard_map.268 = (bf16[3,128,2048]{2,1,0:T(8,128)(2,1)}, bf16[3,128,2176]{2,1,0:T(8,128)(2,1)}, bf16[8,128,2048]{2,1,0:T(8,128)(2,1)}, bf16[8,128,2048]{2,1,0:T(...) custom-call(s32[2]{0:T(128)} %pad_add_fusion.1.ids_ref, ...), custom_call_target="tpu_custom_call" | custom-call | flops 19327352832 | bytes 25165824 | tf_op jit(solution)/shard_map/pallas_call | solution.py:718
  226.3 23.4 %shard_map.269 = (bf16[2,128,2048]{2,1,0:T(8,128)(2,1)}, bf16[2,128,2176]{2,1,0:T(8,128)(2,1)}, bf16[8,128,2048]{2,1,0:T(8,128)(2,1)}, bf16[8,128,2048]{2,1,0:T(...) custom-call(s32[2]{0:T(128)} %pad_add_fusion.1.ids_ref, ...), custom_call_target="tpu_custom_call", output_to_operand_aliasing={{2}: (8, {}), {3}: (9, {}), {4}: (10, {}), {5}: (11, {}), {... | custom-call | flops 12884901888 | bytes 25165824 | tf_op jit(solution)/shard_map/pallas_call | solution.py:718
  257.3 32.3 %shard_map.270 = (bf16[3,128,2048]{2,1,0:T(8,128)(2,1)}, bf16[3,128,2176]{2,1,0:T(8,128)(2,1)}, bf16[8,128,2048]{2,1,0:T(8,128)(2,1)}, bf16[8,128,2048]{2,1,0:T(...) custom-call(s32[2]{0:T(128)} %pad_add_fusion.1.ids_ref, ...), custom_call_target="tpu_custom_call", output_to_operand_aliasing={{2}: (10, {}), {3}: (11, {}), {4}: (12, {}), {5}: (13, {}),... | custom-call | flops 19327352832 | bytes 25165824 | tf_op jit(solution)/shard_map/pallas_call | solution.py:718
  293.2 9.9 %shard_map.271 = (bf16[256,2048]{1,0:T(8,128)(2,1)}, bf16[256,2048]{1,0:T(8,128)(2,1)}, bf16[256,2048]{1,0:T(8,128)(2,1)}, bf16[256,2048]{1,0:T(8,128)(2,1)}) custom-call(bf16[1024,2048]{1,0:T(8,128)(2,1)} %bitcast.154, bf16[1024,2048]{1,0:T(8,128)(2,1)} %bitcast.160), custom_call_target="tpu_custom_call" | custom-call | flops 4294967296 | bytes 10485760 | tf_op jit(solution)/shard_map/pallas_call | solution.py:806
  303.8 15.6 %collective-permute-start.49 = (bf16[256,2048]{1,0:T(8,128)(2,1)}, bf16[256,2048]{1,0:T(8,128)(2,1)S(1)}, u32[]{:S(2)}, u32[]{:S(2)}) collective-permute-start(bf16[256,2048]{1,0:T(8,128)(2,1)} %get-tuple-element.313), channel_id=1, source_target_pairs={{0,1},{1,0},{2,3},{3,2},{4,5},{5,4},{6,7},{7,6},{8,9},{9,8},{10,11... | collective-permute-start | bytes 3145736 | tf_op jit(solution)/shard_map/ppermute | solution.py:866
  327.4 10.4 %shard_map.272 = bf16[1024,2048]{1,0:T(8,128)(2,1)} custom-call(bf16[1024,2048]{1,0:T(8,128)(2,1)} %bitcast.155, bf16[1024,2048]{1,0:T(8,128)(2,1)} %bitcast.161, bf16[256,2048]{1,0:T(8,128)(2,1)} %copy-done.28, bf16[256,2048]{1,0:T(8,128)(2,1)} %copy-done.29, bf16[256,2048]{1,0:T(8,128)(2,1)} %copy-done.30, bf16[256,2048]{1,0:T(8,128)(2,1)} %copy-done.31), custom_call_target="tpu_custom_call" | custom-call | flops 4294967296 | bytes 10485760 | tf_op jit(solution)/shard_map/pallas_call | solution.py:806
  341.9 10.2 %shard_map.273 = (bf16[512,1024]{1,0:T(8,128)(2,1)}, bf16[512,1024]{1,0:T(8,128)(2,1)}, bf16[512,1024]{1,0:T(8,128)(2,1)}, bf16[512,1024]{1,0:T(8,128)(2,1)}) custom-call(bf16[1024,2048]{1,0:T(8,128)(2,1)} %bitcast.150, bf16[1024,2048]{1,0:T(8,128)(2,1)} %bitcast.156), custom_call_target="tpu_custom_call" | custom-call | flops 4294967296 | bytes 10485760 | tf_op jit(solution)/shard_map/pallas_call | solution.py:806
  358.3 9.6 %shard_map.274 = (bf16[512,1024]{1,0:T(8,128)(2,1)}, bf16[512,1024]{1,0:T(8,128)(2,1)}, bf16[512,1024]{1,0:T(8,128)(2,1)}, bf16[512,1024]{1,0:T(8,128)(2,1)}) custom-call(bf16[1024,2048]{1,0:T(8,128)(2,1)} %bitcast.151, bf16[1024,2048]{1,0:T(8,128)(2,1)} %bitcast.158), custom_call_target="tpu_custom_call" | custom-call | flops 4294967296 | bytes 10485760 | tf_op jit(solution)/shard_map/pallas_call | solution.py:806
  375.2 10.2 %shard_map.275 = bf16[2048,1024]{1,0:T(8,128)(2,1)} custom-call(bf16[1024,2048]{1,0:T(8,128)(2,1)} %bitcast.152, bf16[1024,2048]{1,0:T(8,128)(2,1)} %bitcast.157, bf16[512,1024]{1,0:T(8,128)(2,1)} %collective-permute-done.59.refs_0_, bf16[512,1024]{1,0:T(8,128)(2,1)} %collective-permute-done.60.refs_1_, bf16[512,1024]{1,0:T(8,128)(2,1)} %collective-permute-done.61.refs_2_, ...), custom_call_target="tpu_custom_call" | custom-call | flops 4294967296 | bytes 10485760 | tf_op jit(solution)/shard_map/pallas_call | solution.py:806
  397.2 10.8 %shard_map.276 = bf16[2048,1024]{1,0:T(8,128)(2,1)} custom-call(bf16[1024,2048]{1,0:T(8,128)(2,1)} %bitcast.153, bf16[1024,2048]{1,0:T(8,128)(2,1)} %bitcast.159, bf16[512,1024]{1,0:T(8,128)(2,1)} %copy-done.32, bf16[512,1024]{1,0:T(8,128)(2,1)} %copy-done.33, bf16[512,1024]{1,0:T(8,128)(2,1)} %copy-done.34, bf16[512,1024]{1,0:T(8,128)(2,1)} %copy-done.35), custom_call_target="tpu_custom_call" | custom-call | flops 4294967296 | bytes 10485760 | tf_op jit(solution)/shard_map/pallas_call | solution.py:806
  411.1 10.3 %collective-permute-done.69.refs_1_.refs_8_ = bf16[128,2048]{1,0:T(8,128)(2,1)S(1)} collective-permute-done((bf16[128,2048]{1,0:T(8,128)(2,1)S(1)}, bf16[128,2048]{1,0:T(8,128)(2,1)S(1)}, u32[]{:S(2)}, u32[]{:S(2)}) %collective-permute-start.69) | collective-permute-done | bytes 524320 | tf_op jit(solution)/shard_map/ppermute | solution.py:860
  443.8 9.8 %shard_map.279 = (f32[8,128,384]{2,1,0:T(8,128)}, bf16[8,128,384]{2,1,0:T(8,128)(2,1)}) custom-call(s32[9]{0:T(128)} %concatenate.85.ids_ref, bf16[2048,384]{1,0:T(8,128)(2,1)} %get-tuple-element.278.qkv_ref, bf16[5,128,128]{2,1,0:T(8,128)(2,1)} %get-tuple-element.358.refs_0_, bf16[3,128,128]{2,1,0:T(8,128)(2,1)} %get-tuple-element.363.refs_1_, ...), custom_call_target="tpu_custom_call" | custom-call | flops 5368709120 | bytes 5521444 | tf_op jit(solution)/shard_map/pallas_call | solution.py:545
  490.8 12.0 %shard_map.282 = (bf16[8,128,384]{2,1,0:T(8,128)(2,1)}, bf16[8,128,384]{2,1,0:T(8,128)(2,1)}, bf16[8,128,2048]{2,1,0:T(8,128)(2,1)}, f32[8,2048]{1,0:T(8,128)}) custom-call(s32[9]{0:T(128)} %concatenate.85.ids_ref, f32[8,128,384]{2,1,0:T(8,128)} %get-tuple-element.372.grad_own, bf16[8,128,384]{2,1,0:T(8,128)(2,1)} %copy-done.16, ...), custom_call_target="tpu_custom_call" | custom-call | flops 3221225472 | bytes 19755044 | tf_op jit(solution)/shard_map/pallas_call | solution.py:545
  514.8 7.1 %shard_map.283 = (f32[384,2048]{1,0:T(8,128)}, bf16[384,512]{1,0:T(8,128)(2,1)}, bf16[384,512]{1,0:T(8,128)(2,1)}, bf16[384,512]{1,0:T(8,128)(2,1)}, bf16[384,512]{1,0:T(8,128)(2,1)}) custom-call(bf16[8,128,384]{2,1,0:T(8,128)(2,1)} %get-tuple-element.404.refs_0_, bf16[8,128,384]{2,1,0:T(8,128)(2,1)} %get-tuple-element.406.refs_1_, ...), custom_call_target="tpu_custom_call" | custom-call | flops 3221225472 | bytes 10485760 | tf_op jit(solution)/shard_map/pallas_call | solution.py:545
  534.0 13.4 %collective-permute-done.101 = bf16[384,1024]{1,0:T(8,128)(2,1)S(1)} collective-permute-done((bf16[384,1024]{1,0:T(8,128)(2,1)S(1)}, bf16[384,1024]{1,0:T(8,128)(2,1)S(1)}, u32[]{:S(2)}, u32[]{:S(2)}) %collective-permute-start.101) | collective-permute-done | bytes 786464 | tf_op jit(solution)/shard_map/ppermute | solution.py:869
  557.7 7.3 %all-to-all-start.1 = ((bf16[16,64,384]{2,1,0:T(8,128)(2,1)}), bf16[16,64,384]{2,1,0:T(8,128)(2,1)S(1)}, u32[]{:S(2)}, u32[]{:S(2)}) async-start(bf16[16,64,384]{2,1,0:T(8,128)(2,1)} %bitcast.60), calls=%async_computation.4 | async-start | bytes 1572864 | tf_op jit(solution)/shard_map/all_to_all | solution.py:1287
  583.6 11.2 %collective-permute-done.105.there_ref = bf16[128,2048]{1,0:T(8,128)(2,1)S(1)} collective-permute-done((bf16[128,2048]{1,0:T(8,128)(2,1)S(1)}, bf16[128,2048]{1,0:T(8,128)(2,1)S(1)}, u32[]{:S(2)}, u32[]{:S(2)}) %collective-permute-start.105) | collective-permute-done | bytes 524320 | tf_op jit(solution)/shard_map/ppermute | solution.py:860
  (559 shorter events, 310.6 us)
Async XLA Ops:
  9.7 22.7 %all-to-all-start = ((bf16[8,128,384]{2,1,0:T(8,128)(2,1)}), bf16[8,128,384]{2,1,0:T(8,128)(2,1)S(1)}, u32[]{:S(2)}, u32[]{:S(2)}) async-start(bf16[8,128,384]{2,1,0:T(8,128)(2,1)} %shard_map.263), calls=%async_computation | async-start | bytes 1572864 | tf_op jit(solution)/shard_map/all_to_all | solution.py:976
  15.4 506.5 %reduce-scatter.4.cloned.1.call-start = ((), (), s32[]{:S(2)}) async-start(), calls=%async_computation.5 | async-start | bytes 6291456 | tf_op jit(solution)/shard_map/reduce_scatter | solution.py:1119
  62.2 84.3 %collective-permute-start.26 = (bf16[1,2048,1024]{2,1,0:T(8,128)(2,1)}, bf16[1,2048,1024]{2,1,0:T(8,128)(2,1)}, u32[]{:S(2)}, u32[]{:S(2)}) collective-permute-start(bf16[1,2048,1024]{2,1,0:T(8,128)(2,1)} %param.28), channel_id=1, source_target_pairs={{0,1},{1,0},{2,3},{3,2},{4,5},{5,4},{6,7},{7,6},{8,9},{9,8},{10,11... | collective-permute-start | bytes 12582920 | tf_op jit(solution)/shard_map/ppermute | solution.py:866
  115.6 44.0 %collective-permute-start.29 = (bf16[1,2048,1024]{2,1,0:T(8,128)(2,1)}, bf16[1,2048,1024]{2,1,0:T(8,128)(2,1)}, u32[]{:S(2)}, u32[]{:S(2)}) collective-permute-start(bf16[1,2048,1024]{2,1,0:T(8,128)(2,1)} %param.29), channel_id=1, source_target_pairs={{0,1},{1,0},{2,3},{3,2},{4,5},{5,4},{6,7},{7,6},{8,9},{9,8},{10,11... | collective-permute-start | bytes 12582920 | tf_op jit(solution)/shard_map/ppermute | solution.py:866
  129.8 40.2 %collective-permute-start.32 = (bf16[1,1024,2048]{2,1,0:T(8,128)(2,1)}, bf16[1,1024,2048]{2,1,0:T(8,128)(2,1)}, u32[]{:S(2)}, u32[]{:S(2)}) collective-permute-start(bf16[1,1024,2048]{2,1,0:T(8,128)(2,1)} %param.30), channel_id=1, source_target_pairs={{0,1},{1,0},{2,3},{3,2},{4,5},{5,4},{6,7},{7,6},{8,9},{9,8},{10,11... | collective-permute-start | bytes 12582920 | tf_op jit(solution)/shard_map/ppermute | solution.py:866
  187.6 35.4 %collective-permute-start.35 = (bf16[128,2176]{1,0:T(8,128)(2,1)S(1)}, bf16[128,2176]{1,0:T(8,128)(2,1)S(1)}, u32[]{:S(2)}, u32[]{:S(2)}) collective-permute-start(bf16[128,2176]{1,0:T(8,128)(2,1)S(1)} %collective-permute-done.33.refs_2_), channel_id=1, source_target_pairs={{0,4},{1,5},{4,8},{5,9},{8,12},{9,13},{12,14},{13,15},{14,10},{15,... | collective-permute-start | bytes 1671176 | tf_op jit(solution)/shard_map/ppermute | solution.py:860
  188.5 34.5 %collective-permute-start.36 = (bf16[128,2176]{1,0:T(8,128)(2,1)S(1)}, bf16[128,2176]{1,0:T(8,128)(2,1)S(1)}, u32[]{:S(2)}, u32[]{:S(2)}) collective-permute-start(bf16[128,2176]{1,0:T(8,128)(2,1)S(1)} %collective-permute-done.34.refs_1_), channel_id=1, source_target_pairs={{4,0},{5,1},{8,4},{9,5},{12,8},{13,9},{14,12},{15,13},{10,14},{11,... | collective-permute-start | bytes 1671176 | tf_op jit(solution)/shard_map/ppermute | solution.py:863
  189.1 33.8 %collective-permute-start.37 = (bf16[128,2048]{1,0:T(8,128)(2,1)}, bf16[128,2048]{1,0:T(8,128)(2,1)S(1)}, u32[]{:S(2)}, u32[]{:S(2)}) collective-permute-start(bf16[128,2048]{1,0:T(8,128)(2,1)} %copy-done.45), channel_id=1, source_target_pairs={{0,4},{1,5},{4,8},{5,9},{8,12},{9,13},{12,14},{13,15},{14,10},{15,... | collective-permute-start | bytes 1572872 | tf_op jit(solution)/shard_map/ppermute | solution.py:860
  190.1 32.8 %collective-permute-start.38 = (bf16[128,2048]{1,0:T(8,128)(2,1)}, bf16[128,2048]{1,0:T(8,128)(2,1)S(1)}, u32[]{:S(2)}, u32[]{:S(2)}) collective-permute-start(bf16[128,2048]{1,0:T(8,128)(2,1)} %copy-done.44), channel_id=1, source_target_pairs={{4,0},{5,1},{8,4},{9,5},{12,8},{13,9},{14,12},{15,13},{10,14},{11,... | collective-permute-start | bytes 1572872 | tf_op jit(solution)/shard_map/ppermute | solution.py:863
  223.0 28.3 %collective-permute-start.43 = (bf16[64,2048]{1,0:T(8,128)(2,1)S(1)}, bf16[64,2048]{1,0:T(8,128)(2,1)S(1)}, u32[]{:S(2)}, u32[]{:S(2)}) collective-permute-start(bf16[64,2048]{1,0:T(8,128)(2,1)S(1)} %slice.316), channel_id=1, source_target_pairs={{0,4},{1,5},{4,8},{5,9},{8,12},{9,13},{12,14},{13,15},{14,10},{15,... | collective-permute-start | bytes 786440 | tf_op jit(solution)/shard_map/ppermute | solution.py:860
  224.2 27.2 %collective-permute-start.44 = (bf16[64,2048]{1,0:T(8,128)(2,1)S(1)}, bf16[64,2048]{1,0:T(8,128)(2,1)S(1)}, u32[]{:S(2)}, u32[]{:S(2)}) collective-permute-start(bf16[64,2048]{1,0:T(8,128)(2,1)S(1)} %slice.317), channel_id=1, source_target_pairs={{4,0},{5,1},{8,4},{9,5},{12,8},{13,9},{14,12},{15,13},{10,14},{11,... | collective-permute-start | bytes 786440 | tf_op jit(solution)/shard_map/ppermute | solution.py:863
  224.6 25.1 %collective-permute-start.39 = (bf16[128,2176]{1,0:T(8,128)(2,1)S(1)}, bf16[128,2176]{1,0:T(8,128)(2,1)S(1)}, u32[]{:S(2)}, u32[]{:S(2)}) collective-permute-start(bf16[128,2176]{1,0:T(8,128)(2,1)S(1)} %collective-permute-done.36.refs_0_), channel_id=1, source_target_pairs={{4,0},{5,1},{8,4},{9,5},{12,8},{13,9},{14,12},{15,13},{10,14},{11,... | collective-permute-start | bytes 1671176 | tf_op jit(solution)/shard_map/ppermute | solution.py:863
  225.4 24.3 %collective-permute-start.40 = (bf16[128,2176]{1,0:T(8,128)(2,1)S(1)}, bf16[128,2176]{1,0:T(8,128)(2,1)S(1)}, u32[]{:S(2)}, u32[]{:S(2)}) collective-permute-start(bf16[128,2176]{1,0:T(8,128)(2,1)S(1)} %collective-permute-done.35.refs_1_), channel_id=1, source_target_pairs={{0,4},{1,5},{4,8},{5,9},{8,12},{9,13},{12,14},{13,15},{14,10},{15,... | collective-permute-start | bytes 1671176 | tf_op jit(solution)/shard_map/ppermute | solution.py:860
  303.8 18.9 %collective-permute-start.49 = (bf16[256,2048]{1,0:T(8,128)(2,1)}, bf16[256,2048]{1,0:T(8,128)(2,1)S(1)}, u32[]{:S(2)}, u32[]{:S(2)}) collective-permute-start(bf16[256,2048]{1,0:T(8,128)(2,1)} %get-tuple-element.313), channel_id=1, source_target_pairs={{0,1},{1,0},{2,3},{3,2},{4,5},{5,4},{6,7},{7,6},{8,9},{9,8},{10,11... | collective-permute-start | bytes 3145736 | tf_op jit(solution)/shard_map/ppermute | solution.py:866
  337.9 184.1 %reduce-scatter.6.cloned.1.call-start = ((), (), s32[]{:S(2)}) async-start(), calls=%async_computation.6 | async-start | bytes 6291456 | tf_op jit(solution)/shard_map/reduce_scatter | solution.py:1119
  387.7 134.2 %reduce-scatter.8.cloned.1.call-start = ((), (), s32[]{:S(2)}) async-start(), calls=%async_computation.7 | async-start | bytes 6291456 | tf_op jit(solution)/shard_map/reduce_scatter | solution.py:1119
  484.0 112.8 %collective-permute-start.114 = (bf16[128,2048]{1,0:T(8,128)(2,1)}, bf16[128,2048]{1,0:T(8,128)(2,1)S(1)}, u32[]{:S(2)}, u32[]{:S(2)}) collective-permute-start(bf16[128,2048]{1,0:T(8,128)(2,1)} %fusion.8), channel_id=1, source_target_pairs={{0,16},{16,0},{1,17},{17,1},{2,18},{18,2},{3,19},{19,3},{4,20},{20... | collective-permute-start | bytes 1572872 | tf_op jit(solution)/shard_map/ppermute | solution.py:869
  488.5 33.4 %collective-permute-start.92 = (f32[17,2048]{1,0:T(8,128)S(1)}, f32[17,2048]{1,0:T(8,128)S(1)}, u32[]{:S(2)}, u32[]{:S(2)}) collective-permute-start(f32[17,2048]{1,0:T(8,128)S(1)} %add.451), channel_id=1, source_target_pairs={{0,8},{1,9},{2,10},{3,11},{4,12},{5,13},{6,14},{7,15},{8,0},{9,1},... | collective-permute-start | bytes 417800 | tf_op jit(solution)/shard_map/ppermute | solution.py:1163
  524.7 24.5 %collective-permute-start.96 = (f32[3,2048]{1,0:T(4,128)}, f32[3,2048]{1,0:T(4,128)}, u32[]{:S(2)}, u32[]{:S(2)}) collective-permute-start(f32[3,2048]{1,0:T(4,128)} %fusion.18), channel_id=1, source_target_pairs={{0,2},{1,3},{2,0},{3,1},{4,6},{5,7},{6,4},{7,5},{8,10},{9,11},{10,... | collective-permute-start | bytes 73736 | tf_op jit(solution)/shard_map/ppermute | solution.py:1163
  528.2 19.2 %collective-permute-start.101 = (bf16[384,1024]{1,0:T(8,128)(2,1)S(1)}, bf16[384,1024]{1,0:T(8,128)(2,1)S(1)}, u32[]{:S(2)}, u32[]{:S(2)}) collective-permute-start(bf16[384,1024]{1,0:T(8,128)(2,1)S(1)} %pad_maximum_fusion), channel_id=1, source_target_pairs={{0,16},{16,0},{1,17},{17,1},{2,18},{18,2},{3,19},{19,3},{4,20},{20... | collective-permute-start | bytes 2359304 | tf_op jit(solution)/shard_map/ppermute | solution.py:869
  556.3 44.8 %collective-permute-start.109 = (f32[17,2048]{1,0:T(8,128)S(1)}, f32[17,2048]{1,0:T(8,128)}, u32[]{:S(2)}, u32[]{:S(2)}) collective-permute-start(f32[17,2048]{1,0:T(8,128)S(1)} %add.471), channel_id=1, source_target_pairs={{0,16},{16,0},{1,17},{17,1},{2,18},{18,2},{3,19},{19,3},{4,20},{20... | collective-permute-start | bytes 417800 | tf_op jit(solution)/shard_map/ppermute | solution.py:869
  557.7 39.1 %all-to-all-start.1 = ((bf16[16,64,384]{2,1,0:T(8,128)(2,1)}), bf16[16,64,384]{2,1,0:T(8,128)(2,1)S(1)}, u32[]{:S(2)}, u32[]{:S(2)}) async-start(bf16[16,64,384]{2,1,0:T(8,128)(2,1)} %bitcast.60), calls=%async_computation.4 | async-start | bytes 1572864 | tf_op jit(solution)/shard_map/all_to_all | solution.py:1287
  573.7 21.2 %collective-permute-start.105 = (bf16[128,2048]{1,0:T(8,128)(2,1)S(1)}, bf16[128,2048]{1,0:T(8,128)(2,1)S(1)}, u32[]{:S(2)}, u32[]{:S(2)}) collective-permute-start(bf16[128,2048]{1,0:T(8,128)(2,1)S(1)} %get-tuple-element.436), channel_id=1, source_target_pairs={{0,4},{1,5},{4,8},{5,9},{8,12},{9,13},{12,14},{13,15},{14,10},{15,... | collective-permute-start | bytes 1572872 | tf_op jit(solution)/shard_map/ppermute | solution.py:860
  573.9 22.9 %collective-permute-start.106 = (bf16[128,2048]{1,0:T(8,128)(2,1)S(1)}, bf16[128,2048]{1,0:T(8,128)(2,1)}, u32[]{:S(2)}, u32[]{:S(2)}) collective-permute-start(bf16[128,2048]{1,0:T(8,128)(2,1)S(1)} %get-tuple-element.437), channel_id=1, source_target_pairs={{4,0},{5,1},{8,4},{9,5},{12,8},{13,9},{14,12},{15,13},{10,14},{11,... | collective-permute-start | bytes 1572872 | tf_op jit(solution)/shard_map/ppermute | solution.py:863
  (174 other events, 1855.9 us)
Sparse Core Ops, SparseCore 0:
  338.0 52.1 reduce-scatter.3
  392.6 54.3 reduce-scatter.5
  449.8 65.5 reduce-scatter.7
